TPU v7x, 128 devices: a whole 4x4x4 slice. The times are simulated.
128 devices in a mesh: gx: 8 (over y, x_lo), gy: 16 (over z, x_hi, core).
Axes of the slice: x: 4 (x_hi: 2, x_lo: 2; x = x_hi * 2 + x_lo), y: 4, z: 4, core: 2. Of those that a mesh axis runs over, the one named last changes fastest.
Arguments:
- dist_start: float32 [19, 2, 1024, 2048], P(None, None, 'gx', 'gy'), may hold values from -6 to 6
- cotangent: float32 [19, 2, 1024, 2048], P(None, None, 'gx', 'gy'), may hold values from -6 to 6
- solid_mask: int32 [2, 1024, 2048], P(None, 'gx', 'gy'), may hold values 0 or 1
- weight_in: bfloat16 [19, 128], replicated, may hold values from -1.25 to 1.25
- bias_in: float32 [128], replicated, may hold values from -3 to 3
- weight_out: bfloat16 [128, 19], replicated, may hold values from -0.5 to 0.5
- bias_out: float32 [19], replicated, may hold values from -3 to 3
Outputs:
- grad_start: float32 [19, 2, 1024, 2048], P(None, None, 'gx', 'gy')
- grad_weight_in: float32 [19, 128], replicated
- grad_bias_in: float32 [128], replicated
- grad_weight_out: float32 [128, 19], replicated
- grad_bias_out: float32 [19], replicated
Inputs may be any that keep to these rules, and one draw needn't show every extreme that they name: `solid_mask`: 1 marks a solid cell.
All inputs are finite; a program needn't handle non-finite values. No bound on the sum of `solid_mask` on one device may be relied on, other than what follows from the above.
Results may differ from a plain program's by a relative error of at most 0.0067.
Values may be sent and summed in bfloat16 or wider, within the bound.
No kernel may reach another device: no remote copies, remote signals or barrier semaphores. Data moves between devices by JAX's collectives and lax.ppermute only.
A program may use at most 256 MiB of HBM per device.

v0:
```python
import math

import jax
import jax.numpy as jnp
from jax import lax
from jax.experimental import pallas as pl
from jax.experimental.pallas import tpu as pltpu
from jax.sharding import PartitionSpec as P

VEL = (
    (0, 0, 0), (1, 0, 0), (-1, 0, 0), (0, 1, 0), (0, -1, 0), (0, 0, 1), (0, 0, -1),
    (1, 1, 0), (-1, -1, 0), (1, -1, 0), (-1, 1, 0), (1, 0, 1), (-1, 0, -1), (1, 0, -1),
    (-1, 0, 1), (0, 1, 1), (0, -1, -1), (0, 1, -1), (0, -1, 1),
)
OPP = (0, 2, 1, 4, 3, 6, 5, 8, 7, 10, 9, 12, 11, 14, 13, 16, 15, 18, 17)
Q = 19
SIDE = tuple(q for q in range(Q) if VEL[q][1])
PLACE = {q: i for i, q in enumerate(SIDE)}
f32 = jnp.float32
bf16 = jnp.bfloat16
NT = (((1,), (1,)), ((), ()))
IDX = 80
COLS = (126, 127, 0, 0, 127, 127, 0, 1)


def iota(shape, dim):
    return lax.broadcasted_iota(jnp.int32, shape, dim)


def vmem(n):
    return [pl.BlockSpec(memory_space=pltpu.VMEM)] * n


def weights_kernel(wint, wout, wtin, wtout, bias, a_in, a_out, b_out, b_in):
    rep = jnp.where(iota((Q, 160), 1) // 8 == iota((Q, 160), 0), 1.0, 0.0).astype(bf16)
    rept = jnp.where(iota((160, Q), 0) // 8 == iota((160, Q), 1), 1.0, 0.0).astype(bf16)
    wide_in = jnp.dot(wint[...], rep, preferred_element_type=f32)
    wide_out = jnp.dot(wout[...], rep, preferred_element_type=f32)
    tall_out = jnp.dot(rept, wtout[...], preferred_element_type=f32)
    tall_in = jnp.dot(rept, wtin[...], preferred_element_type=f32)
    b = bias[...]
    high = b.astype(bf16).astype(f32)
    mid = (b - high).astype(bf16).astype(f32)
    low = b - high - mid
    col = iota((128, 160), 1)
    row = iota((160, 128), 0)
    biased = jnp.where(col == 152, high, jnp.where(col == 153, mid, jnp.where(col == 154, low, 0.0)))
    for k in range(8):
        own = (col % 8 == k) & (col < 152)
        own_row = (row % 8 == k) & (row < 152)
        part = slice(k * 128, k * 128 + 128)
        a_in[part, :] = jnp.where(own, wide_in, biased).astype(bf16)
        a_out[part, :] = jnp.where(own, wide_out, 0.0).astype(bf16)
        b_out[:, part] = jnp.where(own_row, tall_out, 0.0).astype(bf16)
        b_in[:, part] = jnp.where(own_row, tall_in, 0.0).astype(bf16)


def make_weights(weight_in, weight_out, bias_in):
    return pl.pallas_call(
        weights_kernel,
        out_shape=[jax.ShapeDtypeStruct((1024, 160), bf16)] * 2
        + [jax.ShapeDtypeStruct((160, 1024), bf16)] * 2,
        in_specs=vmem(5),
        out_specs=vmem(4),
        cost_estimate=pl.CostEstimate(flops=10**8, bytes_accessed=2 * 10**6, transcendentals=0),
    )(weight_in.T, weight_out, weight_in, weight_out.T, bias_in[:, None])


def pack_kernel(dist, cot, mask, up, down, cols, line):
    for out, rows in ((up, (126, 127)), (down, (0, 1))):
        for i, r in enumerate(rows):
            line[pl.ds(0, 38), :] = dist[pl.ds(r, 38, stride=128), :]
            line[pl.ds(38, 2), :] = mask[pl.ds(r, 2, stride=128), :].astype(f32)
            line[pl.ds(40, 38), :] = cot[pl.ds(r, 38, stride=128), :]
            line[pl.ds(78, 2), :] = jnp.zeros((2, 128), f32)
            out[pl.ds(i * 80, 80), :] = line[...].astype(bf16)
    lane, row = iota((8, 128), 1), iota((8, 128), 0)
    pick = jnp.zeros((8, 128), f32)
    for j, y in enumerate(COLS):
        pick = jnp.where((row == j) & (lane == y), 1.0, pick)
    pick = pick.astype(bf16)

    def slab(ref, i, place):
        values = ref[pl.ds(pl.multiple_of(i * 128, 128), 128), :].astype(f32).astype(bf16)
        got = lax.dot_general(pick, values, NT, preferred_element_type=f32)
        cols[pl.ds(place, 8, stride=IDX), :] = got

    def both(i, carry):
        slab(dist, i, i)
        slab(cot, i, i + 40)
        return carry

    lax.fori_loop(0, 38, both, 0)
    for z in range(2):
        slab(mask, z, 38 + z)
        cols[pl.ds(78 + z, 8, stride=IDX), :] = jnp.zeros((8, 128), f32)


def pack(dist, cot, mask):
    return pl.pallas_call(
        pack_kernel,
        out_shape=[jax.ShapeDtypeStruct((160, 128), bf16)] * 2 + [jax.ShapeDtypeStruct((640, 128), f32)],
        in_specs=vmem(3),
        out_specs=vmem(3),
        scratch_shapes=[pltpu.VMEM((80, 128), f32)],
    )(dist.reshape(38 * 128, 128), cot.reshape(38 * 128, 128), mask.reshape(256, 128))


def corner_kernel(from_up, from_down, cols, send_up, send_down, edge, lines):
    sides = ((from_down, 0, 0), (from_down, 1, 1), (from_up, 0, 126), (from_up, 1, 127))
    lane = iota((80, 128), 1)
    got = [ref[pl.ds(i * 80, 80), :].astype(f32) for ref, i, _ in sides]
    for (_, _, place), values in zip(sides, got):
        lines[pl.ds(place % 8, 80, stride=8), :] = values
    for r in range(2, 6):
        lines[pl.ds(r, 80, stride=8), :] = jnp.zeros((80, 128), f32)
    for j, y in enumerate(COLS):
        out = jnp.zeros((80, 128), f32)
        for (_, _, place), values in zip(sides, got):
            out = jnp.where(lane == place, values[:, y : y + 1], out)
        edge[pl.ds(j * 80, 80), :] = out
    for out, first in ((send_up, 0), (send_down, 6)):
        out[:, :128] = cols[pl.ds(first * 80, 160), :].astype(bf16)
        out[:, 128:] = edge[pl.ds(first * 80, 160), :].astype(bf16)


def corners(from_up, from_down, cols):
    return pl.pallas_call(
        corner_kernel,
        out_shape=[jax.ShapeDtypeStruct((160, 256), bf16)] * 2
        + [jax.ShapeDtypeStruct((640, 128), f32)] * 2,
        in_specs=vmem(3),
        out_specs=vmem(4),
    )(from_up, from_down, cols)


def main_kernel(
    dist, cot, mask, cols, edge, from_left, from_right, lines,
    a_in, a_out, b_out, b_in, bias_out,
    out, parts,
    post, gmid, gpad, hid, hpost, hcot, hmid, strip, spost, smid, flip, uo, acc, accb,
):
    lane = iota((8, 128), 1)
    row8 = iota((8, 128), 0)

    def pair(a, b):
        return jnp.concatenate([a, b], axis=1)

    strip[0] = cols[...]
    strip[1] = edge[...]
    strip[0, pl.ds(0, 160), :] = from_left[:, :128].astype(f32)
    strip[1, pl.ds(0, 160), :] = from_left[:, 128:].astype(f32)
    strip[0, pl.ds(480, 160), :] = from_right[:, :128].astype(f32)
    strip[1, pl.ds(480, 160), :] = from_right[:, 128:].astype(f32)

    def strip_of(i):
        return pair(strip[0, pl.ds(i, 8, stride=IDX), :], strip[1, pl.ds(i, 8, stride=IDX), :])

    def line_of(i):
        return lines[pl.ds(i * 8, 8), :]

    for q in range(Q):
        for z in range(2):
            i = 2 * q + z
            gpad[q, z, pl.ds(8, 128), :] = cot[q, z]
            halo = line_of(40 + i)
            gpad[q, z, pl.ds(0, 8), :] = halo
            gpad[q, z, pl.ds(136, 8), :] = halo
            gpad[q, z, pl.ds(144, 8), :] = cot[q, z, pl.ds(0, 8), :]

    uo[:, pl.ds(152, 8), :] = jnp.ones((2, 8, 128), f32)
    uo[:, pl.ds(312, 8), :] = jnp.ones((2, 8, 128), f32)
    acc[...] = jnp.zeros_like(acc)
    accb[...] = jnp.zeros_like(accb)
    flip[...] = jnp.zeros_like(flip)

    def stacked(values):
        both = jnp.concatenate(values, axis=0)
        return both

    def collide(d, solid, keep):
        ones = jnp.ones((8, 256), f32)
        field = stacked(d + [ones]).astype(bf16)
        t = jnp.tanh(jnp.dot(a_in[...], field, preferred_element_type=f32))
        if keep is not None:
            hid[keep] = t
        o = jnp.dot(b_out[...], t.astype(bf16), preferred_element_type=f32)
        res = []
        for q in range(Q):
            bias = bias_out[pl.ds(q * 8, 8), :]
            val = d[q] + o[q * 8 : q * 8 + 8] + pair(bias, bias)
            val = jnp.where(solid, d[OPP[q]], val)
            res.append(val.astype(bf16).astype(f32))
        return res

    def backward(u, g, solid, t, partial):
        og = [jnp.where(solid, 0.0, v) for v in g]
        ones = jnp.ones((8, 256), f32)
        if t is None:
            field = stacked(u + [ones]).astype(bf16)
            t = jnp.tanh(jnp.dot(a_in[...], field, preferred_element_type=f32))
        grad = stacked(og + [ones]).astype(bf16)
        hg = jnp.dot(a_out[...], grad, preferred_element_type=f32)
        hb = (hg * (1.0 - t * t)).astype(bf16)
        ig = jnp.dot(b_in[...], hb, preferred_element_type=f32)
        if partial:
            act = t.astype(bf16)
            for q in range(Q):
                for z in range(2):
                    uo[z, pl.ds(q * 8, 8), :] = u[q][:, z * 128 : z * 128 + 128]
                    uo[z, pl.ds(160 + q * 8, 8), :] = og[q][:, z * 128 : z * 128 + 128]
                accb[pl.ds(q * 8, 8), :] += og[q][:, :128] + og[q][:, 128:]
            total = acc[...]
            for k in range(8):
                left = pair(uo[0, pl.ds(k, 40, stride=8), :], uo[1, pl.ds(k, 40, stride=8), :])
                part = slice(k * 128, k * 128 + 128)
                right = jnp.concatenate([hb[part], act[part]], axis=0)
                total = total + lax.dot_general(left.astype(bf16), right, NT, preferred_element_type=f32)
            acc[...] = total
        return [
            og[q] + ig[q * 8 : q * 8 + 8] + jnp.where(solid, g[OPP[q]], 0.0) for q in range(Q)
        ]

    def streamed(ref, halo, row, orient):
        res = []
        for q in range(Q):
            cx, cy, cz = (orient * c for c in VEL[q])
            halves = []
            for z in range(2):
                zs = (z - cz) % 2
                v = ref[q, zs, pl.ds(row - cx, 8), :]
                if cy:
                    k = PLACE[q] * 2 + zs
                    h = halo[pl.ds(row - cx, 8), :][:, k : k + 1]
                    v = pltpu.roll(v, 1 if cy == 1 else 127, 1)
                    v = jnp.where(lane == (0 if cy == 1 else 127), h, v)
                halves.append(v)
            res.append(pair(*halves))
        return res

    def streamed_strip(get, orient, z):
        res = []
        for q in range(Q):
            cx, cy, cz = (orient * c for c in VEL[q])
            v = get(q, (z - cz) % 2)
            if cy:
                v = pltpu.roll(v, cy % 8, 0)
            if cx:
                v = pltpu.roll(v, cx % 256, 1)
            res.append(v)
        return res

    def to_halo(get, halo, orient):
        for q in SIDE:
            j = 1 if orient * VEL[q][1] == 1 else 6
            for z in range(2):
                flip[pl.ds(PLACE[q] * 2 + z, 1), :] = get(q, z, j)
        low = flip[:, :128].T
        high = flip[:, 128:].T
        halo[pl.ds(8, 128), :] = low
        outer = jnp.where(row8 < 4, high[0:8], high[120:128])
        halo[pl.ds(136, 8), :] = outer
        halo[pl.ds(0, 8), :] = outer
        halo[pl.ds(144, 8), :] = low[0:8]

    def put(ref, row, values):
        for q in range(Q):
            for z in range(2):
                ref[q, z, pl.ds(row, 8), :] = values[q][:, z * 128 : z * 128 + 128]

    def wrap(ref):
        for q in range(Q):
            for z in range(2):
                ref[q, z, pl.ds(0, 8), :] = ref[q, z, pl.ds(136, 8), :]
                ref[q, z, pl.ds(144, 8), :] = ref[q, z, pl.ds(8, 8), :]

    def block(ref, row):
        return [pair(ref[q, 0, pl.ds(row, 8), :], ref[q, 1, pl.ds(row, 8), :]) for q in range(Q)]

    def solid_at(row):
        return pair(mask[0, pl.ds(row, 8), :], mask[1, pl.ds(row, 8), :]) > 0

    line_solid = pair(line_of(38), line_of(39)) > 0.5

    def first(b, carry):
        row = pl.multiple_of(b * 8, 8)
        put(post, row + 8, collide(block(dist, row), solid_at(row), b))
        return carry

    lax.fori_loop(0, 16, first, 0)
    put(post, 136, collide([pair(line_of(2 * q), line_of(2 * q + 1)) for q in range(Q)], line_solid, None))
    wrap(post)
    for z in range(2):
        res = collide([strip_of(2 * q + z) for q in range(Q)], strip_of(38 + z) > 0.5, None)
        for q in range(Q):
            spost[z, q] = res[q]
    to_halo(lambda q, z, j: spost[z, q, pl.ds(j, 1), :], hpost, 1)
    to_halo(
        lambda q, z, j: pair(
            strip[0, pl.ds(j * IDX + 40 + 2 * q + z, 1), :], strip[1, pl.ds(j * IDX + 40 + 2 * q + z, 1), :]
        ),
        hcot,
        -1,
    )

    def second(b, carry):
        row = pl.multiple_of(b * 8, 8)
        u = streamed(post, hpost, row + 8, 1)
        g = streamed(gpad, hcot, row + 8, -1)
        put(gmid, row + 8, backward(u, g, solid_at(row), None, True))
        return carry

    lax.fori_loop(0, 16, second, 0)
    u = streamed(post, hpost, 136, 1)
    g = streamed(gpad, hcot, 136, -1)
    put(gmid, 136, backward(u, g, line_solid, None, False))
    wrap(gmid)
    for z in range(2):
        u = streamed_strip(lambda q, zs: spost[zs, q], 1, z)
        g = streamed_strip(lambda q, zs: strip_of(40 + 2 * q + zs), -1, z)
        res = backward(u, g, strip_of(38 + z) > 0.5, None, False)
        for q in range(Q):
            smid[z, q] = res[q]
    to_halo(lambda q, z, j: smid[z, q, pl.ds(j, 1), :], hmid, -1)

    def third(b, carry):
        row = pl.multiple_of(b * 8, 8)
        g = streamed(gmid, hmid, row + 8, -1)
        res = backward(block(dist, row), g, solid_at(row), hid[b], True)
        put(out, row, res)
        return carry

    lax.fori_loop(0, 16, third, 0)
    parts[pl.ds(0, 20), :] = acc[pl.ds(0, 20), pl.ds(0, 128)]
    parts[pl.ds(20, 20), :] = acc[pl.ds(20, 20), pl.ds(128, 128)]
    for q in range(Q):
        parts[pl.ds(40 + q, 1), :] = jnp.sum(accb[pl.ds(q * 8, 8), :], axis=0, keepdims=True)
    parts[pl.ds(59, 5), :] = jnp.zeros((5, 128), f32)


def main_call(*args):
    field = pltpu.VMEM((Q, 2, 152, 128), f32)
    halo = pltpu.VMEM((152, 128), f32)
    return pl.pallas_call(
        main_kernel,
        out_shape=[jax.ShapeDtypeStruct((Q, 2, 128, 128), f32), jax.ShapeDtypeStruct((64, 128), f32)],
        in_specs=vmem(len(args)),
        out_specs=vmem(2),
        scratch_shapes=[
            field, field, field,
            pltpu.VMEM((16, 1024, 256), f32),
            halo, halo, halo,
            pltpu.VMEM((2, 640, 128), f32),
            pltpu.VMEM((2, Q, 8, 256), f32),
            pltpu.VMEM((2, Q, 8, 256), f32),
            pltpu.VMEM((128, 256), f32),
            pltpu.VMEM((2, 320, 128), f32),
            pltpu.VMEM((40, 256), f32),
            pltpu.VMEM((152, 128), f32),
        ],
        compiler_params=pltpu.CompilerParams(vmem_limit_bytes=58 * 2**20),
    )(*args)


def neighbours(axis):
    size = lax.axis_size(axis)
    up = [(i, (i + 1) % size) for i in range(size)]
    return up, [(j, i) for i, j in up]


def summed(values):
    for axis in ("gx", "gy"):
        size = lax.axis_size(axis)
        step = 1
        while step < size:
            values = values + lax.ppermute(values, axis, [(i, i ^ step) for i in range(size)])
            step *= 2
    return values


def shards(dist, cot, mask, weight_in, bias_in, weight_out, bias_out):
    send_up, send_down, cols = pack(dist, cot, mask)
    up, down = neighbours("gx")
    from_up = lax.ppermute(send_up, "gx", up)
    from_down = lax.ppermute(send_down, "gx", down)
    nets = make_weights(weight_in, weight_out, bias_in)
    side_up, side_down, edge, lines = corners(from_up, from_down, cols)
    up, down = neighbours("gy")
    from_left = lax.ppermute(side_up, "gy", up)
    from_right = lax.ppermute(side_down, "gy", down)
    bias_rows = jnp.broadcast_to(jnp.repeat(bias_out, 8)[:, None], (152, 128))
    grad, parts = main_call(dist, cot, mask, cols, edge, from_left, from_right, lines, *nets, bias_rows)
    total = summed(parts)
    cells = mask.size * lax.axis_size("gx") * lax.axis_size("gy")
    total = total * (1.0 / math.sqrt(cells))
    return grad, total[:19], total[19], total[20:39].T, jnp.sum(total[40:59], axis=1)


def solution(mesh):
    field = P(None, None, "gx", "gy")
    return jax.shard_map(
        shards,
        mesh=mesh,
        in_specs=(field, field, P(None, "gx", "gy"), P(), P(), P(), P()),
        out_specs=(field, P(), P(), P(), P()),
        check_vma=False,
    )
```

profile of v0, /device:TPU:0, one launch (start us, length us, event | category | flops | bytes accessed | tf_op | source)
XLA Modules:
  0.0 114.9 jit_solution(18331976859466434348)
XLA Ops:
  0.7 9.2 %shard_map.110 = (bf16[160,128]{1,0:T(8,128)(2,1)}, bf16[160,128]{1,0:T(8,128)(2,1)}, f32[640,128]{1,0:T(8,128)}) custom-call(f32[4864,128]{1,0:T(8,128)} %bitcast.10, f32[4864,128]{1,0:T(8,128)} %bitcast.11, s32[256,128]{1,0:T(8,128)} %bitcast.12), custom_call_target="tpu_custom_call" | custom-call | tf_op jit(solution)/shard_map/pallas_call | solution.py:100
  9.9 1.6 %collective-permute-start = (bf16[160,128]{1,0:T(8,128)(2,1)}, bf16[160,128]{1,0:T(8,128)(2,1)S(1)}, u32[]{:S(2)}, u32[]{:S(2)}) collective-permute-start(bf16[160,128]{1,0:T(8,128)(2,1)} %get-tuple-element.19), channel_id=1, source_target_pairs={{0,16},{16,32},{32,48},{48,64},{64,80},{80,96},{96,112},{112,0},{1... | collective-permute-start | bytes 122888 | tf_op jit(solution)/shard_map/ppermute | solution.py:384
  11.5 2.6 %collective-permute-start.1 = (bf16[160,128]{1,0:T(8,128)(2,1)}, bf16[160,128]{1,0:T(8,128)(2,1)S(1)}, u32[]{:S(2)}, u32[]{:S(2)}) collective-permute-start(bf16[160,128]{1,0:T(8,128)(2,1)} %get-tuple-element.20), channel_id=1, source_target_pairs={{16,0},{32,16},{48,32},{64,48},{80,64},{96,80},{112,96},{0,112},{1... | collective-permute-start | bytes 122888 | tf_op jit(solution)/shard_map/ppermute | solution.py:385
  14.0 2.2 %collective-permute-done.from_up = bf16[160,128]{1,0:T(8,128)(2,1)S(1)} collective-permute-done((bf16[160,128]{1,0:T(8,128)(2,1)}, bf16[160,128]{1,0:T(8,128)(2,1)S(1)}, u32[]{:S(2)}, u32[]{:S(2)}) %collective-permute-start) | collective-permute-done | bytes 40992 | tf_op jit(solution)/shard_map/ppermute | solution.py:384
  16.2 0.6 copy-done.2
  16.8 0.0 copy-done.3
  16.9 2.1 %shard_map.111 = (bf16[160,256]{1,0:T(8,128)(2,1)}, bf16[160,256]{1,0:T(8,128)(2,1)}, f32[640,128]{1,0:T(8,128)}, f32[640,128]{1,0:T(8,128)}) custom-call(bf16[160,128]{1,0:T(8,128)(2,1)} %copy-done.2, bf16[160,128]{1,0:T(8,128)(2,1)} %copy-done.3, f32[640,128]{1,0:T(8,128)} %get-tuple-element.18.cols), custom_call_target="tpu_custom_call" | custom-call | tf_op jit(solution)/shard_map/pallas_call | solution.py:128
  18.9 5.4 %collective-permute-start.3 = (bf16[160,256]{1,0:T(8,128)(2,1)}, bf16[160,256]{1,0:T(8,128)(2,1)S(1)}, u32[]{:S(2)}, u32[]{:S(2)}) collective-permute-start(bf16[160,256]{1,0:T(8,128)(2,1)} %get-tuple-element.23), channel_id=1, source_target_pairs={{1,0},{2,1},{3,2},{4,3},{5,4},{6,5},{7,6},{8,7},{9,8},{10,9},{11,1... | collective-permute-start | bytes 245768 | tf_op jit(solution)/shard_map/ppermute | solution.py:390
  24.3 0.1 broadcast_in_dim.14
  24.3 0.1 broadcast_in_dim.15
  24.4 0.7 copy.15
  25.2 0.7 copy.16.wout
  25.9 0.7 copy.17.bias
  26.6 2.4 %shard_map.112 = (bf16[1024,160]{1,0:T(8,128)(2,1)}, bf16[1024,160]{1,0:T(8,128)(2,1)}, bf16[160,1024]{1,0:T(8,128)(2,1)}, bf16[160,1024]{1,0:T(8,128)(2,1)}) custom-call(bf16[128,19]{1,0:T(8,128)(2,1)} %bitcast.13, bf16[128,19]{1,0:T(8,128)(2,1)} %copy.16.wout, bf16[19,128]{1,0:T(8,128)(2,1)} %wtin.1, bf16[19,128]{1,0:T(8,128)(2,1)} %bitcast.14, ...), custom_call_target="tpu_custom_call" | custom-call | flops 100000000 | bytes 2000000 | tf_op jit(solution)/shard_map/pallas_call | solution.py:59
  29.1 0.7 broadcast_in_dim.16.bias_out
  29.8 53.1 %shard_map.113 = (f32[19,2,128,128]{3,2,1,0:T(8,128)}, f32[64,128]{1,0:T(8,128)}) custom-call(f32[19,2,128,128]{3,2,1,0:T(8,128)} %dist.1, f32[19,2,128,128]{3,2,1,0:T(8,128)} %cot.1, s32[2,128,128]{2,1,0:T(8,128)} %mask.1, f32[640,128]{1,0:T(8,128)} %get-tuple-element.18.cols, f32[640,128]{1,0:T(8,128)} %get-tuple-element.21.edge, ...), custom_call_target="tpu_custom_call" | custom-call | tf_op jit(solution)/shard_map/pallas_call | solution.py:344
  82.9 1.9 %collective-permute-start.4 = (f32[64,128]{1,0:T(8,128)}, f32[64,128]{1,0:T(8,128)S(1)}, u32[]{:S(2)}, u32[]{:S(2)}) collective-permute-start(f32[64,128]{1,0:T(8,128)} %get-tuple-element.30), channel_id=1, source_target_pairs={{0,16},{16,0},{32,48},{48,32},{64,80},{80,64},{96,112},{112,96},{1... | collective-permute-start | bytes 98312 | tf_op jit(solution)/shard_map/ppermute | solution.py:376
  84.8 2.2 %collective-permute-done.4 = f32[64,128]{1,0:T(8,128)S(1)} collective-permute-done((f32[64,128]{1,0:T(8,128)}, f32[64,128]{1,0:T(8,128)S(1)}, u32[]{:S(2)}, u32[]{:S(2)}) %collective-permute-start.4) | collective-permute-done | bytes 32800 | tf_op jit(solution)/shard_map/ppermute | solution.py:376
  87.1 0.8 add.21
  87.8 1.4 %collective-permute-start.5 = (f32[64,128]{1,0:T(8,128)S(1)}, f32[64,128]{1,0:T(8,128)S(1)}, u32[]{:S(2)}, u32[]{:S(2)}) collective-permute-start(f32[64,128]{1,0:T(8,128)S(1)} %add.21), channel_id=1, source_target_pairs={{0,32},{16,48},{32,0},{48,16},{64,96},{80,112},{96,64},{112,80},{1... | collective-permute-start | bytes 98312 | tf_op jit(solution)/shard_map/ppermute | solution.py:376
  89.3 2.5 %collective-permute-done.5 = f32[64,128]{1,0:T(8,128)S(1)} collective-permute-done((f32[64,128]{1,0:T(8,128)S(1)}, f32[64,128]{1,0:T(8,128)S(1)}, u32[]{:S(2)}, u32[]{:S(2)}) %collective-permute-start.5) | collective-permute-done | bytes 32800 | tf_op jit(solution)/shard_map/ppermute | solution.py:376
  91.8 2.8 %collective-permute-start.6 = (f32[64,128]{1,0:T(8,128)S(1)}, f32[64,128]{1,0:T(8,128)S(1)}, u32[]{:S(2)}, u32[]{:S(2)}) collective-permute-start(f32[64,128]{1,0:T(8,128)S(1)} %add.22), channel_id=1, source_target_pairs={{0,64},{16,80},{32,96},{48,112},{64,0},{80,16},{96,32},{112,48},{1... | collective-permute-start | bytes 98312 | tf_op jit(solution)/shard_map/ppermute | solution.py:376
  94.5 2.6 %collective-permute-done.6 = f32[64,128]{1,0:T(8,128)S(1)} collective-permute-done((f32[64,128]{1,0:T(8,128)S(1)}, f32[64,128]{1,0:T(8,128)S(1)}, u32[]{:S(2)}, u32[]{:S(2)}) %collective-permute-start.6) | collective-permute-done | bytes 32800 | tf_op jit(solution)/shard_map/ppermute | solution.py:376
  97.2 1.2 %collective-permute-done.7 = f32[64,128]{1,0:T(8,128)S(1)} collective-permute-done((f32[64,128]{1,0:T(8,128)S(1)}, f32[64,128]{1,0:T(8,128)S(1)}, u32[]{:S(2)}, u32[]{:S(2)}) %collective-permute-start.7) | collective-permute-done | bytes 32800 | tf_op jit(solution)/shard_map/ppermute | solution.py:376
  98.4 1.4 %collective-permute-start.8 = (f32[64,128]{1,0:T(8,128)S(1)}, f32[64,128]{1,0:T(8,128)S(1)}, u32[]{:S(2)}, u32[]{:S(2)}) collective-permute-start(f32[64,128]{1,0:T(8,128)S(1)} %add.24), channel_id=1, source_target_pairs={{0,2},{1,3},{2,0},{3,1},{4,6},{5,7},{6,4},{7,5},{8,10},{9,11},{10,... | collective-permute-start | bytes 98312 | tf_op jit(solution)/shard_map/ppermute | solution.py:376
  99.8 4.0 %collective-permute-done.8 = f32[64,128]{1,0:T(8,128)S(1)} collective-permute-done((f32[64,128]{1,0:T(8,128)S(1)}, f32[64,128]{1,0:T(8,128)S(1)}, u32[]{:S(2)}, u32[]{:S(2)}) %collective-permute-start.8) | collective-permute-done | bytes 32800 | tf_op jit(solution)/shard_map/ppermute | solution.py:376
  103.8 0.9 collective-permute-start.9
  104.7 3.0 %collective-permute-done.9 = f32[64,128]{1,0:T(8,128)S(1)} collective-permute-done((f32[64,128]{1,0:T(8,128)S(1)}, f32[64,128]{1,0:T(8,128)S(1)}, u32[]{:S(2)}, u32[]{:S(2)}) %collective-permute-start.9) | collective-permute-done | bytes 32800 | tf_op jit(solution)/shard_map/ppermute | solution.py:376
  107.7 2.8 %collective-permute-start.10 = (f32[64,128]{1,0:T(8,128)S(1)}, f32[64,128]{1,0:T(8,128)S(1)}, u32[]{:S(2)}, u32[]{:S(2)}) collective-permute-start(f32[64,128]{1,0:T(8,128)S(1)} %add.26), channel_id=1, source_target_pairs={{0,8},{1,9},{2,10},{3,11},{4,12},{5,13},{6,14},{7,15},{8,0},{9,1},... | collective-permute-start | bytes 98312 | tf_op jit(solution)/shard_map/ppermute | solution.py:376
  110.6 2.6 %collective-permute-done.10 = f32[64,128]{1,0:T(8,128)S(1)} collective-permute-done((f32[64,128]{1,0:T(8,128)S(1)}, f32[64,128]{1,0:T(8,128)S(1)}, u32[]{:S(2)}, u32[]{:S(2)}) %collective-permute-start.10) | collective-permute-done | bytes 32800 | tf_op jit(solution)/shard_map/ppermute | solution.py:376
  113.2 0.5 slice_bitcast_fusion.1
  113.7 1.2 %slice_reduce_fusion = (f32[19]{0:T(128)}, f32[128,19]{0,1:T(8,128)}, f32[19,128]{1,0:T(8,128)}) fusion(f32[64,128]{1,0:T(8,128)S(1)} %add_multiply_fusion), kind=kLoop, calls=%fused_computation.1 | loop fusion | flops 2413 | bytes 48716 | tf_op jit(solution)/shard_map/reduce_sum | solution.py:396
  (25 shorter events, 0.1 us)
Async XLA Ops:
  0.6 23.6 %copy-start.7 = (f32[19]{0:T(128)S(1)}, f32[19]{0:T(128)}, u32[]{:S(2)}) copy-start(f32[19]{0:T(128)} %param.13) | copy-start | bytes 232
  0.6 23.8 %copy-start.4 = (bf16[19,128]{1,0:T(8,128)(2,1)S(1)}, bf16[19,128]{1,0:T(8,128)(2,1)}, u32[]{:S(2)}) copy-start(bf16[19,128]{1,0:T(8,128)(2,1)} %wtin.1) | copy-start | bytes 14596
  0.7 24.5 %copy-start.5 = (bf16[128,19]{0,1:T(8,128)(2,1)S(1)}, bf16[128,19]{0,1:T(8,128)(2,1)}, u32[]{:S(2)}) copy-start(bf16[128,19]{0,1:T(8,128)(2,1)} %param.12) | copy-start | bytes 14596
  0.7 25.2 %copy-start.6 = (f32[128]{0:T(128)S(1)}, f32[128]{0:T(128)}, u32[]{:S(2)}) copy-start(f32[128]{0:T(128)} %param.11) | copy-start | bytes 1540
  9.9 6.3 %collective-permute-start = (bf16[160,128]{1,0:T(8,128)(2,1)}, bf16[160,128]{1,0:T(8,128)(2,1)S(1)}, u32[]{:S(2)}, u32[]{:S(2)}) collective-permute-start(bf16[160,128]{1,0:T(8,128)(2,1)} %get-tuple-element.19), channel_id=1, source_target_pairs={{0,16},{16,32},{32,48},{48,64},{64,80},{80,96},{96,112},{112,0},{1... | collective-permute-start | bytes 122888 | tf_op jit(solution)/shard_map/ppermute | solution.py:384
  11.5 4.8 %collective-permute-start.1 = (bf16[160,128]{1,0:T(8,128)(2,1)}, bf16[160,128]{1,0:T(8,128)(2,1)S(1)}, u32[]{:S(2)}, u32[]{:S(2)}) collective-permute-start(bf16[160,128]{1,0:T(8,128)(2,1)} %get-tuple-element.20), channel_id=1, source_target_pairs={{16,0},{32,16},{48,32},{64,48},{80,64},{96,80},{112,96},{0,112},{1... | collective-permute-start | bytes 122888 | tf_op jit(solution)/shard_map/ppermute | solution.py:385
  16.2 0.6 copy-start.2
  16.2 0.6 copy-start.3
  18.9 10.2 %collective-permute-start.2 = (bf16[160,256]{1,0:T(8,128)(2,1)}, bf16[160,256]{1,0:T(8,128)(2,1)S(1)}, u32[]{:S(2)}, u32[]{:S(2)}) collective-permute-start(bf16[160,256]{1,0:T(8,128)(2,1)} %get-tuple-element.22), channel_id=1, source_target_pairs={{0,1},{1,2},{2,3},{3,4},{4,5},{5,6},{6,7},{7,8},{8,9},{9,10},{10,1... | collective-permute-start | bytes 245768 | tf_op jit(solution)/shard_map/ppermute | solution.py:389
  18.9 10.2 %collective-permute-start.3 = (bf16[160,256]{1,0:T(8,128)(2,1)}, bf16[160,256]{1,0:T(8,128)(2,1)S(1)}, u32[]{:S(2)}, u32[]{:S(2)}) collective-permute-start(bf16[160,256]{1,0:T(8,128)(2,1)} %get-tuple-element.23), channel_id=1, source_target_pairs={{1,0},{2,1},{3,2},{4,3},{5,4},{6,5},{7,6},{8,7},{9,8},{10,9},{11,1... | collective-permute-start | bytes 245768 | tf_op jit(solution)/shard_map/ppermute | solution.py:390
  29.1 0.7 copy-start
  29.1 0.7 copy-start.1
  82.9 4.1 %collective-permute-start.4 = (f32[64,128]{1,0:T(8,128)}, f32[64,128]{1,0:T(8,128)S(1)}, u32[]{:S(2)}, u32[]{:S(2)}) collective-permute-start(f32[64,128]{1,0:T(8,128)} %get-tuple-element.30), channel_id=1, source_target_pairs={{0,16},{16,0},{32,48},{48,32},{64,80},{80,64},{96,112},{112,96},{1... | collective-permute-start | bytes 98312 | tf_op jit(solution)/shard_map/ppermute | solution.py:376
  87.8 3.9 %collective-permute-start.5 = (f32[64,128]{1,0:T(8,128)S(1)}, f32[64,128]{1,0:T(8,128)S(1)}, u32[]{:S(2)}, u32[]{:S(2)}) collective-permute-start(f32[64,128]{1,0:T(8,128)S(1)} %add.21), channel_id=1, source_target_pairs={{0,32},{16,48},{32,0},{48,16},{64,96},{80,112},{96,64},{112,80},{1... | collective-permute-start | bytes 98312 | tf_op jit(solution)/shard_map/ppermute | solution.py:376
  91.8 5.4 %collective-permute-start.6 = (f32[64,128]{1,0:T(8,128)S(1)}, f32[64,128]{1,0:T(8,128)S(1)}, u32[]{:S(2)}, u32[]{:S(2)}) collective-permute-start(f32[64,128]{1,0:T(8,128)S(1)} %add.22), channel_id=1, source_target_pairs={{0,64},{16,80},{32,96},{48,112},{64,0},{80,16},{96,32},{112,48},{1... | collective-permute-start | bytes 98312 | tf_op jit(solution)/shard_map/ppermute | solution.py:376
  97.2 1.2 %collective-permute-start.7 = (f32[64,128]{1,0:T(8,128)S(1)}, f32[64,128]{1,0:T(8,128)S(1)}, u32[]{:S(2)}, u32[]{:S(2)}) collective-permute-start(f32[64,128]{1,0:T(8,128)S(1)} %add.23), channel_id=1, source_target_pairs={{0,1},{1,0},{2,3},{3,2},{4,5},{5,4},{6,7},{7,6},{8,9},{9,8},{10,11... | collective-permute-start | bytes 98312 | tf_op jit(solution)/shard_map/ppermute | solution.py:376
  98.4 5.4 %collective-permute-start.8 = (f32[64,128]{1,0:T(8,128)S(1)}, f32[64,128]{1,0:T(8,128)S(1)}, u32[]{:S(2)}, u32[]{:S(2)}) collective-permute-start(f32[64,128]{1,0:T(8,128)S(1)} %add.24), channel_id=1, source_target_pairs={{0,2},{1,3},{2,0},{3,1},{4,6},{5,7},{6,4},{7,5},{8,10},{9,11},{10,... | collective-permute-start | bytes 98312 | tf_op jit(solution)/shard_map/ppermute | solution.py:376
  103.8 3.9 %collective-permute-start.9 = (f32[64,128]{1,0:T(8,128)S(1)}, f32[64,128]{1,0:T(8,128)S(1)}, u32[]{:S(2)}, u32[]{:S(2)}) collective-permute-start(f32[64,128]{1,0:T(8,128)S(1)} %add.25), channel_id=1, source_target_pairs={{0,4},{1,5},{2,6},{3,7},{4,0},{5,1},{6,2},{7,3},{8,12},{9,13},{10,... | collective-permute-start | bytes 98312 | tf_op jit(solution)/shard_map/ppermute | solution.py:376
  107.7 5.4 %collective-permute-start.10 = (f32[64,128]{1,0:T(8,128)S(1)}, f32[64,128]{1,0:T(8,128)S(1)}, u32[]{:S(2)}, u32[]{:S(2)}) collective-permute-start(f32[64,128]{1,0:T(8,128)S(1)} %add.26), channel_id=1, source_target_pairs={{0,8},{1,9},{2,10},{3,11},{4,12},{5,13},{6,14},{7,15},{8,0},{9,1},... | collective-permute-start | bytes 98312 | tf_op jit(solution)/shard_map/ppermute | solution.py:376
where the time goes:
time: 116 us; the launch traced here: 115 us
  Pallas kernels  66.8 us (58%)
  starting transfers between devices  20.8 us (18%)
  waiting for transfers between devices  20.3 us (18%)
  local copies, waits for them, and re-layouts  4.24 us (4%)
  other arithmetic  2.03 us (2%)
    pallas_call x1, Pallas kernels, main_call(): pl.pallas_call(main_kernel, out_shape=[jax.ShapeDtypeStruct((Q, 2, 128, 1...  53.1 us
    ppermute x7, waiting for transfers between devices, summed(): lax.ppermute(values, axis, [(i, i ^ step) for i in range(size)])  18.1 us
    ppermute x7, starting transfers between devices, summed(): lax.ppermute(values, axis, [(i, i ^ step) for i in range(size)])  11.3 us
    pallas_call x1, Pallas kernels, pack(): pl.pallas_call(pack_kernel, out_shape=[jax.ShapeDtypeStruct((160, 128), b...  9.23 us
    ppermute x1, starting transfers between devices, shards(): from_right = lax.ppermute(side_down, 'gy', down)  5.36 us
    ppermute x1, starting transfers between devices, shards(): from_down = lax.ppermute(send_down, 'gx', down)  2.56 us
    pallas_call x1, Pallas kernels, make_weights(): pl.pallas_call(weights_kernel, out_shape=[jax.ShapeDtypeStruct((1024, 160...  2.43 us
  transfers between devices with their start and end apart: 11, of which 8 were waited for; matrix products, arithmetic and copies ran while one was open for 2% of the time, Pallas kernels for 2%

commit v1 on v0

v1 whole, which is shorter than its diff:
```python
import math

import jax
import jax.numpy as jnp
from jax import lax
from jax.experimental import pallas as pl
from jax.experimental.pallas import tpu as pltpu
from jax.sharding import PartitionSpec as P

VEL = (
    (0, 0, 0), (1, 0, 0), (-1, 0, 0), (0, 1, 0), (0, -1, 0), (0, 0, 1), (0, 0, -1),
    (1, 1, 0), (-1, -1, 0), (1, -1, 0), (-1, 1, 0), (1, 0, 1), (-1, 0, -1), (1, 0, -1),
    (-1, 0, 1), (0, 1, 1), (0, -1, -1), (0, 1, -1), (0, -1, 1),
)
OPP = (0, 2, 1, 4, 3, 6, 5, 8, 7, 10, 9, 12, 11, 14, 13, 16, 15, 18, 17)
Q = 19
WIDE = 2
STEPS = 16 // WIDE
SIDE = tuple(q for q in range(Q) if VEL[q][1])
PLACE = {q: i for i, q in enumerate(SIDE)}
f32 = jnp.float32
bf16 = jnp.bfloat16
NT = (((1,), (1,)), ((), ()))
IDX = 80
COLS = (126, 127, 0, 0, 127, 127, 0, 1)


def iota(shape, dim):
    return lax.broadcasted_iota(jnp.int32, shape, dim)


def vmem(n):
    return [pl.BlockSpec(memory_space=pltpu.VMEM)] * n


def weights_kernel(win, wout, bias, bias_out, a_in, a_out, b_out, b_in, bias_rows):
    TN = (((0,), (0,)), ((), ()))
    rep = jnp.where(iota((Q, 160), 1) // 8 == iota((Q, 160), 0), 1.0, 0.0).astype(bf16)
    rept = jnp.where(iota((160, Q), 0) // 8 == iota((160, Q), 1), 1.0, 0.0).astype(bf16)
    wide_in = lax.dot_general(win[...], rep, TN, preferred_element_type=f32)
    wide_out = jnp.dot(wout[...], rep, preferred_element_type=f32)
    tall_out = lax.dot_general(rept, wout[...], NT, preferred_element_type=f32)
    tall_in = jnp.dot(rept, win[...], preferred_element_type=f32)
    b = jnp.broadcast_to(bias[...], (128, 128)).T
    b = jnp.concatenate([b, b[:, :32]], axis=1)
    high = b.astype(bf16).astype(f32)
    mid = (b - high).astype(bf16).astype(f32)
    low = b - high - mid
    col = iota((128, 160), 1)
    row = iota((160, 128), 0)
    biased = jnp.where(col == 152, high, jnp.where(col == 153, mid, jnp.where(col == 154, low, 0.0)))
    for k in range(8):
        own = (col % 8 == k) & (col < 152)
        own_row = (row % 8 == k) & (row < 152)
        part = slice(k * 128, k * 128 + 128)
        a_in[part, :] = jnp.where(own, wide_in, biased).astype(bf16)
        a_out[part, :] = jnp.where(own, wide_out, 0.0).astype(bf16)
        b_out[:, part] = jnp.where(own_row, tall_out, 0.0).astype(bf16)
        b_in[:, part] = jnp.where(own_row, tall_in, 0.0).astype(bf16)
    for q in range(Q):
        bias_rows[pl.ds(q * 8, 8), :] = jnp.broadcast_to(bias_out[0:1, q : q + 1], (8, 128))


def make_weights(weight_in, weight_out, bias_in, bias_out):
    return pl.pallas_call(
        weights_kernel,
        out_shape=[jax.ShapeDtypeStruct((1024, 160), bf16)] * 2
        + [jax.ShapeDtypeStruct((160, 1024), bf16)] * 2
        + [jax.ShapeDtypeStruct((152, 128), f32)],
        in_specs=vmem(4),
        out_specs=vmem(5),
        cost_estimate=pl.CostEstimate(flops=10**8, bytes_accessed=2 * 10**6, transcendentals=0),
    )(weight_in, weight_out, bias_in[None], bias_out[None])


def pack_kernel(dist, cot, mask, up, down, cols, line):
    for out, rows in ((up, (126, 127)), (down, (0, 1))):
        for i, r in enumerate(rows):
            line[pl.ds(0, 38), :] = dist[pl.ds(r, 38, stride=128), :]
            line[pl.ds(38, 2), :] = mask[pl.ds(r, 2, stride=128), :].astype(f32)
            line[pl.ds(40, 38), :] = cot[pl.ds(r, 38, stride=128), :]
            line[pl.ds(78, 2), :] = jnp.zeros((2, 128), f32)
            out[pl.ds(i * 80, 80), :] = line[...].astype(bf16)
    lane, row = iota((8, 128), 1), iota((8, 128), 0)
    pick = jnp.zeros((8, 128), f32)
    for j, y in enumerate(COLS):
        pick = jnp.where((row == j) & (lane == y), 1.0, pick)
    pick = pick.astype(bf16)

    def slabs(ref, first, count, place):
        values = ref[pl.ds(first * 128, count * 128), :].astype(f32).astype(bf16)
        got = lax.dot_general(pick, values, NT, preferred_element_type=f32)
        for i in range(count):
            cols[pl.ds(place + i, 8, stride=IDX), :] = got[:, i * 128 : i * 128 + 128]

    for half in range(2):
        slabs(dist, half * 19, 19, half * 19)
        slabs(cot, half * 19, 19, 40 + half * 19)
    slabs(mask, 0, 2, 38)
    for z in range(2):
        cols[pl.ds(78 + z, 8, stride=IDX), :] = jnp.zeros((8, 128), f32)


def pack(dist, cot, mask):
    return pl.pallas_call(
        pack_kernel,
        out_shape=[jax.ShapeDtypeStruct((160, 128), bf16)] * 2 + [jax.ShapeDtypeStruct((640, 128), f32)],
        in_specs=vmem(3),
        out_specs=vmem(3),
        scratch_shapes=[pltpu.VMEM((80, 128), f32)],
    )(dist.reshape(38 * 128, 128), cot.reshape(38 * 128, 128), mask.reshape(256, 128))


def corner_kernel(from_up, from_down, cols, send_up, send_down, edge, lines):
    sides = ((from_down, 0, 0), (from_down, 1, 1), (from_up, 0, 126), (from_up, 1, 127))
    lane = iota((80, 128), 1)
    got = [ref[pl.ds(i * 80, 80), :].astype(f32) for ref, i, _ in sides]
    for (_, _, place), values in zip(sides, got):
        lines[pl.ds(place % 8, 80, stride=8), :] = values
    for r in range(2, 6):
        lines[pl.ds(r, 80, stride=8), :] = jnp.zeros((80, 128), f32)
    for j, y in enumerate(COLS):
        out = jnp.zeros((80, 128), f32)
        for (_, _, place), values in zip(sides, got):
            out = jnp.where(lane == place, values[:, y : y + 1], out)
        edge[pl.ds(j * 80, 80), :] = out
    for out, first in ((send_up, 0), (send_down, 6)):
        out[:, :128] = cols[pl.ds(first * 80, 160), :].astype(bf16)
        out[:, 128:] = edge[pl.ds(first * 80, 160), :].astype(bf16)


def corners(from_up, from_down, cols):
    return pl.pallas_call(
        corner_kernel,
        out_shape=[jax.ShapeDtypeStruct((160, 256), bf16)] * 2
        + [jax.ShapeDtypeStruct((640, 128), f32)] * 2,
        in_specs=vmem(3),
        out_specs=vmem(4),
    )(from_up, from_down, cols)


def main_kernel(
    dist, cot, mask, cols, edge, from_left, from_right, lines,
    a_in, a_out, b_out, b_in, bias_out,
    out, parts,
    post, gmid, gpad, hid, hpost, hcot, hmid, strip, spost, smid, flip, uo, acc_in, acc_out, accb,
):
    lane = iota((8, 128), 1)
    row8 = iota((8, 128), 0)

    def join(*parts):
        return jnp.concatenate(parts, axis=1)

    strip[0] = cols[...]
    strip[1] = edge[...]
    strip[0, pl.ds(0, 160), :] = from_left[:, :128].astype(f32)
    strip[1, pl.ds(0, 160), :] = from_left[:, 128:].astype(f32)
    strip[0, pl.ds(480, 160), :] = from_right[:, :128].astype(f32)
    strip[1, pl.ds(480, 160), :] = from_right[:, 128:].astype(f32)

    def strip_of(i):
        return join(strip[0, pl.ds(i, 8, stride=IDX), :], strip[1, pl.ds(i, 8, stride=IDX), :])

    def line_of(i):
        return lines[pl.ds(i * 8, 8), :]

    for q in range(Q):
        for z in range(2):
            i = 2 * q + z
            gpad[q, z, pl.ds(8, 128), :] = cot[q, z]
            halo = line_of(40 + i)
            gpad[q, z, pl.ds(0, 8), :] = halo
            gpad[q, z, pl.ds(136, 8), :] = halo
            gpad[q, z, pl.ds(144, 8), :] = cot[q, z, pl.ds(0, 8), :]

    uo[:, pl.ds(152, 8), :] = jnp.ones((2 * WIDE, 8, 128), f32)
    uo[:, pl.ds(312, 8), :] = jnp.ones((2 * WIDE, 8, 128), f32)
    acc_in[...] = jnp.zeros_like(acc_in)
    acc_out[...] = jnp.zeros_like(acc_out)
    accb[...] = jnp.zeros_like(accb)
    flip[...] = jnp.zeros_like(flip)

    def operand(values):
        ones = jnp.ones(values[0].shape, f32)
        return jnp.concatenate(values + [ones], axis=0).astype(bf16)

    def hidden(values):
        return jnp.tanh(jnp.dot(a_in[...], operand(values), preferred_element_type=f32))

    def collide(d, solid, keep):
        t = hidden(d)
        if keep is not None:
            hid[keep] = t
        o = jnp.dot(b_out[...], t.astype(bf16), preferred_element_type=f32)
        res = []
        for q in range(Q):
            bias = bias_out[pl.ds(q * 8, 8), :]
            val = d[q] + o[q * 8 : q * 8 + 8] + join(*[bias] * (d[q].shape[1] // 128))
            val = jnp.where(solid, d[OPP[q]], val)
            res.append(val.astype(bf16).astype(f32))
        return res

    def backward(u, g, solid, t, partial):
        og = [jnp.where(solid, 0.0, v) for v in g]
        if t is None:
            t = hidden(u)
        hg = jnp.dot(a_out[...], operand(og), preferred_element_type=f32)
        hb = (hg * (1.0 - t * t)).astype(bf16)
        ig = jnp.dot(b_in[...], hb, preferred_element_type=f32)
        if partial:
            act = t.astype(bf16)
            halves = [slice(h * 128, h * 128 + 128) for h in range(2 * WIDE)]
            for q in range(Q):
                for h, part in enumerate(halves):
                    uo[h, pl.ds(q * 8, 8), :] = u[q][:, part]
                    uo[h, pl.ds(160 + q * 8, 8), :] = og[q][:, part]
                accb[pl.ds(q * 8, 8), :] += sum(og[q][:, part] for part in halves)

            def cells(first):
                return join(
                    *[uo[h, pl.ds(first + k, 20, stride=8), :] for k in range(8) for h in range(2 * WIDE)]
                ).astype(bf16)

            def units(values):
                return join(*[values[k * 128 : k * 128 + 128] for k in range(8)])

            acc_in[:, :20] += lax.dot_general(units(hb), cells(0), NT, preferred_element_type=f32)
            acc_out[...] += lax.dot_general(cells(160), units(act), NT, preferred_element_type=f32)
        return [
            og[q] + ig[q * 8 : q * 8 + 8] + jnp.where(solid, g[OPP[q]], 0.0) for q in range(Q)
        ]

    def streamed(ref, halo, rows, orient):
        res = []
        for q in range(Q):
            cx, cy, cz = (orient * c for c in VEL[q])
            pieces = []
            for row in rows:
                for z in range(2):
                    zs = (z - cz) % 2
                    v = ref[q, zs, pl.ds(row - cx, 8), :]
                    if cy:
                        k = PLACE[q] * 2 + zs
                        h = halo[pl.ds(row - cx, 8), :][:, k : k + 1]
                        v = pltpu.roll(v, 1 if cy == 1 else 127, 1)
                        v = jnp.where(lane == (0 if cy == 1 else 127), h, v)
                    pieces.append(v)
            res.append(join(*pieces))
        return res

    def streamed_strip(get, orient, z):
        res = []
        for q in range(Q):
            cx, cy, cz = (orient * c for c in VEL[q])
            v = get(q, (z - cz) % 2)
            if cy:
                v = pltpu.roll(v, cy % 8, 0)
            if cx:
                v = pltpu.roll(v, cx % 256, 1)
            res.append(v)
        return res

    def to_halo(get, halo, orient):
        for q in SIDE:
            j = 1 if orient * VEL[q][1] == 1 else 6
            for z in range(2):
                flip[pl.ds(PLACE[q] * 2 + z, 1), :] = get(q, z, j)
        low = flip[:, :128].T
        high = flip[:, 128:].T
        halo[pl.ds(8, 128), :] = low
        outer = jnp.where(row8 < 4, high[0:8], high[120:128])
        halo[pl.ds(136, 8), :] = outer
        halo[pl.ds(0, 8), :] = outer
        halo[pl.ds(144, 8), :] = low[0:8]

    def put(ref, rows, values):
        for q in range(Q):
            for i, row in enumerate(rows):
                for z in range(2):
                    at = i * 256 + z * 128
                    ref[q, z, pl.ds(row, 8), :] = values[q][:, at : at + 128]

    def put_outer(ref, side, values):
        for q in range(Q):
            for z in range(2):
                ref[q, z, pl.ds(136, 8), :] = values[q][:, z * 128 : z * 128 + 128]
                ref[q, z, pl.ds(0, 8), :] = values[q][:, z * 128 : z * 128 + 128]
                ref[q, z, pl.ds(144, 8), :] = ref[q, z, pl.ds(8, 8), :]
                side[z, q] = values[q][:, 256 + z * 256 : 512 + z * 256]

    def block(ref, rows):
        return [join(*[ref[q, z, pl.ds(r, 8), :] for r in rows for z in range(2)]) for q in range(Q)]

    def solid_at(rows):
        return join(*[mask[z, pl.ds(r, 8), :] for r in rows for z in range(2)]) > 0

    outer_solid = join(line_of(38), line_of(39), strip_of(38), strip_of(39)) > 0.5

    def rows_of(b, offset):
        return [pl.multiple_of((b + w * STEPS) * 8, 8) + offset for w in range(WIDE)]

    def first(b, carry):
        put(post, rows_of(b, 8), collide(block(dist, rows_of(b, 0)), solid_at(rows_of(b, 0)), b))
        return carry

    lax.fori_loop(0, STEPS, first, 0)
    d = [
        join(line_of(2 * q), line_of(2 * q + 1), strip_of(2 * q), strip_of(2 * q + 1)) for q in range(Q)
    ]
    put_outer(post, spost, collide(d, outer_solid, None))
    to_halo(lambda q, z, j: spost[z, q, pl.ds(j, 1), :], hpost, 1)
    to_halo(
        lambda q, z, j: join(
            strip[0, pl.ds(j * IDX + 40 + 2 * q + z, 1), :], strip[1, pl.ds(j * IDX + 40 + 2 * q + z, 1), :]
        ),
        hcot,
        -1,
    )

    def second(b, carry):
        u = streamed(post, hpost, rows_of(b, 8), 1)
        g = streamed(gpad, hcot, rows_of(b, 8), -1)
        put(gmid, rows_of(b, 8), backward(u, g, solid_at(rows_of(b, 0)), None, True))
        return carry

    lax.fori_loop(0, STEPS, second, 0)
    us = [streamed(post, hpost, [136], 1)] + [
        streamed_strip(lambda q, zs: spost[zs, q], 1, z) for z in range(2)
    ]
    gs = [streamed(gpad, hcot, [136], -1)] + [
        streamed_strip(lambda q, zs: strip_of(40 + 2 * q + zs), -1, z) for z in range(2)
    ]
    u = [join(*[v[q] for v in us]) for q in range(Q)]
    g = [join(*[v[q] for v in gs]) for q in range(Q)]
    put_outer(gmid, smid, backward(u, g, outer_solid, None, False))
    to_halo(lambda q, z, j: smid[z, q, pl.ds(j, 1), :], hmid, -1)

    def third(b, carry):
        g = streamed(gmid, hmid, rows_of(b, 8), -1)
        rows = rows_of(b, 0)
        put(out, rows, backward(block(dist, rows), g, solid_at(rows), hid[b], True))
        return carry

    lax.fori_loop(0, STEPS, third, 0)
    parts[pl.ds(0, 20), :] = acc_in[...].T[:20]
    parts[pl.ds(20, 20), :] = acc_out[...]
    for q in range(Q):
        parts[pl.ds(40 + q, 1), :] = jnp.sum(accb[pl.ds(q * 8, 8), :], axis=0, keepdims=True)
    parts[pl.ds(59, 5), :] = jnp.zeros((5, 128), f32)


def main_call(*args):
    field = pltpu.VMEM((Q, 2, 152, 128), f32)
    halo = pltpu.VMEM((152, 128), f32)
    return pl.pallas_call(
        main_kernel,
        out_shape=[jax.ShapeDtypeStruct((Q, 2, 128, 128), f32), jax.ShapeDtypeStruct((64, 128), f32)],
        in_specs=vmem(len(args)),
        out_specs=vmem(2),
        scratch_shapes=[
            field, field, field,
            pltpu.VMEM((STEPS, 1024, 256 * WIDE), f32),
            halo, halo, halo,
            pltpu.VMEM((2, 640, 128), f32),
            pltpu.VMEM((2, Q, 8, 256), f32),
            pltpu.VMEM((2, Q, 8, 256), f32),
            pltpu.VMEM((128, 256), f32),
            pltpu.VMEM((2 * WIDE, 320, 128), f32),
            pltpu.VMEM((128, 128), f32),
            pltpu.VMEM((20, 128), f32),
            pltpu.VMEM((152, 128), f32),
        ],
        compiler_params=pltpu.CompilerParams(vmem_limit_bytes=58 * 2**20),
    )(*args)


def neighbours(axis):
    size = lax.axis_size(axis)
    up = [(i, (i + 1) % size) for i in range(size)]
    return up, [(j, i) for i, j in up]


def summed(values):
    shape = {axis: lax.axis_size(axis) for axis in ("gx", "gy")}
    nx, ny = shape["gx"], shape["gy"]

    def flat(partner):
        pairs = []
        for x in range(nx):
            for y in range(ny):
                px, py = partner(x, y)
                pairs.append((x * ny + y, px * ny + py))
        return pairs

    stages = []
    if (nx, ny) == (8, 16):
        other = (3, 2, 1, 0)
        stages = [
            lambda x, y: (x, y ^ 1),
            lambda x, y: (x ^ 1, y),
            lambda x, y: (x ^ 1, y ^ 2),
            lambda x, y: (x ^ 2, y),
            lambda x, y: (other[x // 2] * 2 + x % 2, y),
            lambda x, y: (x, y ^ 4),
            lambda x, y: (x, other[y // 4] * 4 + y % 4),
        ]
    else:
        for k in range(nx.bit_length() - 1):
            stages.append(lambda x, y, k=k: (x ^ (1 << k), y))
        for k in range(ny.bit_length() - 1):
            stages.append(lambda x, y, k=k: (x, y ^ (1 << k)))
    for partner in stages:
        values = values + lax.ppermute(values, ("gx", "gy"), flat(partner))
    return values


def shards(dist, cot, mask, weight_in, bias_in, weight_out, bias_out):
    send_up, send_down, cols = pack(dist, cot, mask)
    up, down = neighbours("gx")
    from_up = lax.ppermute(send_up, "gx", up)
    from_down = lax.ppermute(send_down, "gx", down)
    nets = make_weights(weight_in, weight_out, bias_in, bias_out)
    side_up, side_down, edge, lines = corners(from_up, from_down, cols)
    up, down = neighbours("gy")
    from_left = lax.ppermute(side_up, "gy", up)
    from_right = lax.ppermute(side_down, "gy", down)
    grad, parts = main_call(dist, cot, mask, cols, edge, from_left, from_right, lines, *nets)
    total = summed(parts)
    cells = mask.size * lax.axis_size("gx") * lax.axis_size("gy")
    total = total * (1.0 / math.sqrt(cells))
    return grad, total[:19], total[19], total[20:39].T, jnp.sum(total[40:59], axis=1)


def solution(mesh):
    field = P(None, None, "gx", "gy")
    return jax.shard_map(
        shards,
        mesh=mesh,
        in_specs=(field, field, P(None, "gx", "gy"), P(), P(), P(), P()),
        out_specs=(field, P(), P(), P(), P()),
        check_vma=False,
    )
```

time: 116 us -> 91.2 us (0.79)
  Pallas kernels: 66.8 us -> 44.4 us
  starting transfers between devices: 20.8 us -> 25.3 us
  waiting for transfers between devices: 20.3 us -> 16 us
  local copies, waits for them, and re-layouts: 4.24 us -> 2.53 us
    pallas_call x1, Pallas kernels: 53.1 us -> 36 us  [main_call(): pl.pallas_call(main_kernel, out_shape=[jax.ShapeDtypeStruct((Q, 2, 128, 1...]
    pallas_call x1, Pallas kernels: 9.23 us -> 4.05 us  [pack(): pl.pallas_call(pack_kernel, out_shape=[jax.ShapeDtypeStruct((160, 128), b...]
    ppermute x7, starting transfers between devices: 11.3 us -> 15.8 us  [summed(): values = values + lax.ppermute(values, ('gx', 'gy'), flat(partner))]
    ppermute x7, waiting for transfers between devices: 18.1 us -> 13.8 us  [summed(): values = values + lax.ppermute(values, ('gx', 'gy'), flat(partner))]
    broadcast_in_dim x4 -> x0, local copies, waits for them, and re-layouts: 1.62 us -> none  [the longest x3 0.88 us: shards(): bias_rows = jnp.broadcast_to(jnp.repeat(bias_out, 8)[:, None], (152, 128))]
  transfers between devices with their start and end apart: 11 -> 11, of which waited for: 8 -> 8; matrix products, arithmetic and copies ran while one was open for 2% -> 1% of each run, Pallas kernels for 2% -> 3%
where the time goes in v1:
time: 91.2 us; the launch traced here: 91 us
  Pallas kernels  44.4 us (49%)
  starting transfers between devices  25.3 us (28%)
  waiting for transfers between devices  16 us (18%)
  local copies, waits for them, and re-layouts  2.53 us (3%)
  other arithmetic  2.03 us (2%)
    pallas_call x1, Pallas kernels, main_call(): pl.pallas_call(main_kernel, out_shape=[jax.ShapeDtypeStruct((Q, 2, 128, 1...  36 us
    ppermute x7, starting transfers between devices, summed(): values = values + lax.ppermute(values, ('gx', 'gy'), flat(partner))  15.8 us
    ppermute x7, waiting for transfers between devices, summed(): values = values + lax.ppermute(values, ('gx', 'gy'), flat(partner))  13.8 us
    ppermute x1, starting transfers between devices, shards(): from_right = lax.ppermute(side_down, 'gy', down)  5.36 us
    pallas_call x1, Pallas kernels, pack(): pl.pallas_call(pack_kernel, out_shape=[jax.ShapeDtypeStruct((160, 128), b...  4.05 us
    ppermute x1, starting transfers between devices, shards(): from_down = lax.ppermute(send_down, 'gx', down)  2.56 us
    pallas_call x1, Pallas kernels, make_weights(): pl.pallas_call(weights_kernel, out_shape=[jax.ShapeDtypeStruct((1024, 160...  2.28 us
    ppermute x1, waiting for transfers between devices, shards(): from_up = lax.ppermute(send_up, 'gx', up)  2.19 us
  transfers between devices with their start and end apart: 11, of which 8 were waited for; matrix products, arithmetic and copies ran while one was open for 1% of the time, Pallas kernels for 3%

profile of v1, /device:TPU:0, one launch (start us, length us, event | category | flops | bytes accessed | tf_op | source)
XLA Modules:
  0.0 91.0 jit_solution(16966661154191758320)
XLA Ops:
  0.6 4.0 %shard_map.110 = (bf16[160,128]{1,0:T(8,128)(2,1)}, bf16[160,128]{1,0:T(8,128)(2,1)}, f32[640,128]{1,0:T(8,128)}) custom-call(f32[4864,128]{1,0:T(8,128)} %bitcast.9, f32[4864,128]{1,0:T(8,128)} %bitcast.10, s32[256,128]{1,0:T(8,128)} %bitcast.11), custom_call_target="tpu_custom_call" | custom-call | tf_op jit(solution)/shard_map/pallas_call | solution.py:105
  4.7 1.6 %collective-permute-start = (bf16[160,128]{1,0:T(8,128)(2,1)}, bf16[160,128]{1,0:T(8,128)(2,1)S(1)}, u32[]{:S(2)}, u32[]{:S(2)}) collective-permute-start(bf16[160,128]{1,0:T(8,128)(2,1)} %get-tuple-element.20), channel_id=1, source_target_pairs={{0,16},{16,32},{32,48},{48,64},{64,80},{80,96},{96,112},{112,0},{1... | collective-permute-start | bytes 122888 | tf_op jit(solution)/shard_map/ppermute | solution.py:420
  6.3 2.6 %collective-permute-start.1 = (bf16[160,128]{1,0:T(8,128)(2,1)}, bf16[160,128]{1,0:T(8,128)(2,1)S(1)}, u32[]{:S(2)}, u32[]{:S(2)}) collective-permute-start(bf16[160,128]{1,0:T(8,128)(2,1)} %get-tuple-element.21), channel_id=1, source_target_pairs={{16,0},{32,16},{48,32},{64,48},{80,64},{96,80},{112,96},{0,112},{1... | collective-permute-start | bytes 122888 | tf_op jit(solution)/shard_map/ppermute | solution.py:421
  8.8 2.2 %collective-permute-done.from_up = bf16[160,128]{1,0:T(8,128)(2,1)S(1)} collective-permute-done((bf16[160,128]{1,0:T(8,128)(2,1)}, bf16[160,128]{1,0:T(8,128)(2,1)S(1)}, u32[]{:S(2)}, u32[]{:S(2)}) %collective-permute-start) | collective-permute-done | bytes 40992 | tf_op jit(solution)/shard_map/ppermute | solution.py:420
  11.0 0.0 collective-permute-done.1.from_down
  11.0 0.6 copy-done.2
  11.6 0.0 copy-done.3
  11.6 2.1 %shard_map.111 = (bf16[160,256]{1,0:T(8,128)(2,1)}, bf16[160,256]{1,0:T(8,128)(2,1)}, f32[640,128]{1,0:T(8,128)}, f32[640,128]{1,0:T(8,128)}) custom-call(bf16[160,128]{1,0:T(8,128)(2,1)} %copy-done.2, bf16[160,128]{1,0:T(8,128)(2,1)} %copy-done.3, f32[640,128]{1,0:T(8,128)} %get-tuple-element.19.cols), custom_call_target="tpu_custom_call" | custom-call | tf_op jit(solution)/shard_map/pallas_call | solution.py:133
  13.7 0.0 collective-permute-start.2
  13.7 5.4 %collective-permute-start.3 = (bf16[160,256]{1,0:T(8,128)(2,1)}, bf16[160,256]{1,0:T(8,128)(2,1)S(1)}, u32[]{:S(2)}, u32[]{:S(2)}) collective-permute-start(bf16[160,256]{1,0:T(8,128)(2,1)} %get-tuple-element.24), channel_id=1, source_target_pairs={{1,0},{2,1},{3,2},{4,3},{5,4},{6,5},{7,6},{8,7},{9,8},{10,9},{11,1... | collective-permute-start | bytes 245768 | tf_op jit(solution)/shard_map/ppermute | solution.py:426
  19.1 0.7 copy.12.wout
  19.8 2.3 %shard_map.112 = (bf16[1024,160]{1,0:T(8,128)(2,1)}, bf16[1024,160]{1,0:T(8,128)(2,1)}, bf16[160,1024]{1,0:T(8,128)(2,1)}, bf16[160,1024]{1,0:T(8,128)(2,1)}, f32[152,128]{1,0:T(8,128)}) custom-call(bf16[19,128]{1,0:T(8,128)(2,1)} %win.1, bf16[128,19]{1,0:T(8,128)(2,1)} %copy.12.wout, f32[1,128]{1,0:T(1,128)} %bitcast.12, f32[1,19]{1,0:T(1,128)} %bitcast.13), custom_call_target="tpu_custom_call" | custom-call | flops 100000000 | bytes 2000000 | tf_op jit(solution)/shard_map/pallas_call | solution.py:65
  22.1 0.6 copy-done
  22.7 0.1 copy-done.1
  22.8 36.0 %shard_map.113 = (f32[19,2,128,128]{3,2,1,0:T(8,128)}, f32[64,128]{1,0:T(8,128)}) custom-call(f32[19,2,128,128]{3,2,1,0:T(8,128)} %dist.1, f32[19,2,128,128]{3,2,1,0:T(8,128)} %cot.1, s32[2,128,128]{2,1,0:T(8,128)} %mask.1, f32[640,128]{1,0:T(8,128)} %get-tuple-element.19.cols, f32[640,128]{1,0:T(8,128)} %get-tuple-element.22.edge, ...), custom_call_target="tpu_custom_call" | custom-call | tf_op jit(solution)/shard_map/pallas_call | solution.py:355
  58.7 0.7 collective-permute-start.4
  59.4 1.1 %collective-permute-done.4 = f32[64,128]{1,0:T(8,128)S(1)} collective-permute-done((f32[64,128]{1,0:T(8,128)}, f32[64,128]{1,0:T(8,128)S(1)}, u32[]{:S(2)}, u32[]{:S(2)}) %collective-permute-start.4) | collective-permute-done | bytes 32800 | tf_op jit(solution)/shard_map/ppermute | solution.py:413
  60.5 0.8 add.21
  61.3 1.5 %collective-permute-start.5 = (f32[64,128]{1,0:T(8,128)S(1)}, f32[64,128]{1,0:T(8,128)S(1)}, u32[]{:S(2)}, u32[]{:S(2)}) collective-permute-start(f32[64,128]{1,0:T(8,128)S(1)} %add.21), channel_id=1, source_target_pairs={{0,16},{1,17},{2,18},{3,19},{4,20},{5,21},{6,22},{7,23},{8,24},{9,... | collective-permute-start | bytes 98312 | tf_op jit(solution)/shard_map/ppermute | solution.py:413
  62.8 2.4 %collective-permute-done.5 = f32[64,128]{1,0:T(8,128)S(1)} collective-permute-done((f32[64,128]{1,0:T(8,128)S(1)}, f32[64,128]{1,0:T(8,128)S(1)}, u32[]{:S(2)}, u32[]{:S(2)}) %collective-permute-start.5) | collective-permute-done | bytes 32800 | tf_op jit(solution)/shard_map/ppermute | solution.py:413
  65.2 3.4 %collective-permute-start.6 = (f32[64,128]{1,0:T(8,128)S(1)}, f32[64,128]{1,0:T(8,128)S(1)}, u32[]{:S(2)}, u32[]{:S(2)}) collective-permute-start(f32[64,128]{1,0:T(8,128)S(1)} %add.22), channel_id=1, source_target_pairs={{0,18},{1,19},{2,16},{3,17},{4,22},{5,23},{6,20},{7,21},{8,26},{9,... | collective-permute-start | bytes 98312 | tf_op jit(solution)/shard_map/ppermute | solution.py:413
  68.6 1.9 %collective-permute-done.6 = f32[64,128]{1,0:T(8,128)S(1)} collective-permute-done((f32[64,128]{1,0:T(8,128)S(1)}, f32[64,128]{1,0:T(8,128)S(1)}, u32[]{:S(2)}, u32[]{:S(2)}) %collective-permute-start.6) | collective-permute-done | bytes 32800 | tf_op jit(solution)/shard_map/ppermute | solution.py:413
  70.5 1.6 %collective-permute-start.7 = (f32[64,128]{1,0:T(8,128)S(1)}, f32[64,128]{1,0:T(8,128)S(1)}, u32[]{:S(2)}, u32[]{:S(2)}) collective-permute-start(f32[64,128]{1,0:T(8,128)S(1)} %add.23), channel_id=1, source_target_pairs={{0,32},{1,33},{2,34},{3,35},{4,36},{5,37},{6,38},{7,39},{8,40},{9,... | collective-permute-start | bytes 98312 | tf_op jit(solution)/shard_map/ppermute | solution.py:413
  72.1 2.3 %collective-permute-done.7 = f32[64,128]{1,0:T(8,128)S(1)} collective-permute-done((f32[64,128]{1,0:T(8,128)S(1)}, f32[64,128]{1,0:T(8,128)S(1)}, u32[]{:S(2)}, u32[]{:S(2)}) %collective-permute-start.7) | collective-permute-done | bytes 32800 | tf_op jit(solution)/shard_map/ppermute | solution.py:413
  74.4 2.9 %collective-permute-start.8 = (f32[64,128]{1,0:T(8,128)S(1)}, f32[64,128]{1,0:T(8,128)S(1)}, u32[]{:S(2)}, u32[]{:S(2)}) collective-permute-start(f32[64,128]{1,0:T(8,128)S(1)} %add.24), channel_id=1, source_target_pairs={{0,96},{1,97},{2,98},{3,99},{4,100},{5,101},{6,102},{7,103},{8,104... | collective-permute-start | bytes 98312 | tf_op jit(solution)/shard_map/ppermute | solution.py:413
  77.3 2.3 %collective-permute-done.8 = f32[64,128]{1,0:T(8,128)S(1)} collective-permute-done((f32[64,128]{1,0:T(8,128)S(1)}, f32[64,128]{1,0:T(8,128)S(1)}, u32[]{:S(2)}, u32[]{:S(2)}) %collective-permute-start.8) | collective-permute-done | bytes 32800 | tf_op jit(solution)/shard_map/ppermute | solution.py:413
  79.5 1.9 %collective-permute-start.9 = (f32[64,128]{1,0:T(8,128)S(1)}, f32[64,128]{1,0:T(8,128)S(1)}, u32[]{:S(2)}, u32[]{:S(2)}) collective-permute-start(f32[64,128]{1,0:T(8,128)S(1)} %add.25), channel_id=1, source_target_pairs={{0,4},{1,5},{2,6},{3,7},{4,0},{5,1},{6,2},{7,3},{8,12},{9,13},{10,... | collective-permute-start | bytes 98312 | tf_op jit(solution)/shard_map/ppermute | solution.py:413
  81.4 2.0 %collective-permute-done.9 = f32[64,128]{1,0:T(8,128)S(1)} collective-permute-done((f32[64,128]{1,0:T(8,128)S(1)}, f32[64,128]{1,0:T(8,128)S(1)}, u32[]{:S(2)}, u32[]{:S(2)}) %collective-permute-start.9) | collective-permute-done | bytes 32800 | tf_op jit(solution)/shard_map/ppermute | solution.py:413
  83.5 3.9 %collective-permute-start.10 = (f32[64,128]{1,0:T(8,128)S(1)}, f32[64,128]{1,0:T(8,128)S(1)}, u32[]{:S(2)}, u32[]{:S(2)}) collective-permute-start(f32[64,128]{1,0:T(8,128)S(1)} %add.26), channel_id=1, source_target_pairs={{0,12},{1,13},{2,14},{3,15},{4,8},{5,9},{6,10},{7,11},{8,4},{9,5},... | collective-permute-start | bytes 98312 | tf_op jit(solution)/shard_map/ppermute | solution.py:413
  87.3 1.9 %collective-permute-done.10 = f32[64,128]{1,0:T(8,128)S(1)} collective-permute-done((f32[64,128]{1,0:T(8,128)S(1)}, f32[64,128]{1,0:T(8,128)S(1)}, u32[]{:S(2)}, u32[]{:S(2)}) %collective-permute-start.10) | collective-permute-done | bytes 32800 | tf_op jit(solution)/shard_map/ppermute | solution.py:413
  89.2 0.5 slice_bitcast_fusion.1
  89.7 1.2 %slice_reduce_fusion = (f32[19]{0:T(128)}, f32[128,19]{0,1:T(8,128)}, f32[19,128]{1,0:T(8,128)}) fusion(f32[64,128]{1,0:T(8,128)S(1)} %add_multiply_fusion), kind=kLoop, calls=%fused_computation.1 | loop fusion | flops 2413 | bytes 48716 | tf_op jit(solution)/shard_map/reduce_sum | solution.py:431
  (14 shorter events, 0.0 us)
Async XLA Ops:
  0.6 18.4 %copy-start.4 = (bf16[128,19]{0,1:T(8,128)(2,1)S(1)}, bf16[128,19]{0,1:T(8,128)(2,1)}, u32[]{:S(2)}) copy-start(bf16[128,19]{0,1:T(8,128)(2,1)} %param.12) | copy-start | bytes 14596
  4.7 6.3 %collective-permute-start = (bf16[160,128]{1,0:T(8,128)(2,1)}, bf16[160,128]{1,0:T(8,128)(2,1)S(1)}, u32[]{:S(2)}, u32[]{:S(2)}) collective-permute-start(bf16[160,128]{1,0:T(8,128)(2,1)} %get-tuple-element.20), channel_id=1, source_target_pairs={{0,16},{16,32},{32,48},{48,64},{64,80},{80,96},{96,112},{112,0},{1... | collective-permute-start | bytes 122888 | tf_op jit(solution)/shard_map/ppermute | solution.py:420
  6.3 4.8 %collective-permute-start.1 = (bf16[160,128]{1,0:T(8,128)(2,1)}, bf16[160,128]{1,0:T(8,128)(2,1)S(1)}, u32[]{:S(2)}, u32[]{:S(2)}) collective-permute-start(bf16[160,128]{1,0:T(8,128)(2,1)} %get-tuple-element.21), channel_id=1, source_target_pairs={{16,0},{32,16},{48,32},{64,48},{80,64},{96,80},{112,96},{0,112},{1... | collective-permute-start | bytes 122888 | tf_op jit(solution)/shard_map/ppermute | solution.py:421
  11.0 0.6 copy-start.2
  11.0 0.6 copy-start.3
  13.7 8.4 %collective-permute-start.2 = (bf16[160,256]{1,0:T(8,128)(2,1)}, bf16[160,256]{1,0:T(8,128)(2,1)S(1)}, u32[]{:S(2)}, u32[]{:S(2)}) collective-permute-start(bf16[160,256]{1,0:T(8,128)(2,1)} %get-tuple-element.23), channel_id=1, source_target_pairs={{0,1},{1,2},{2,3},{3,4},{4,5},{5,6},{6,7},{7,8},{8,9},{9,10},{10,1... | collective-permute-start | bytes 245768 | tf_op jit(solution)/shard_map/ppermute | solution.py:425
  13.7 8.4 %collective-permute-start.3 = (bf16[160,256]{1,0:T(8,128)(2,1)}, bf16[160,256]{1,0:T(8,128)(2,1)S(1)}, u32[]{:S(2)}, u32[]{:S(2)}) collective-permute-start(bf16[160,256]{1,0:T(8,128)(2,1)} %get-tuple-element.24), channel_id=1, source_target_pairs={{1,0},{2,1},{3,2},{4,3},{5,4},{6,5},{7,6},{8,7},{9,8},{10,9},{11,1... | collective-permute-start | bytes 245768 | tf_op jit(solution)/shard_map/ppermute | solution.py:426
  22.1 0.6 copy-start
  22.1 0.7 copy-start.1
  58.7 1.8 %collective-permute-start.4 = (f32[64,128]{1,0:T(8,128)}, f32[64,128]{1,0:T(8,128)S(1)}, u32[]{:S(2)}, u32[]{:S(2)}) collective-permute-start(f32[64,128]{1,0:T(8,128)} %get-tuple-element.32), channel_id=1, source_target_pairs={{0,1},{1,0},{2,3},{3,2},{4,5},{5,4},{6,7},{7,6},{8,9},{9,8},{10,11... | collective-permute-start | bytes 98312 | tf_op jit(solution)/shard_map/ppermute | solution.py:413
  61.3 3.9 %collective-permute-start.5 = (f32[64,128]{1,0:T(8,128)S(1)}, f32[64,128]{1,0:T(8,128)S(1)}, u32[]{:S(2)}, u32[]{:S(2)}) collective-permute-start(f32[64,128]{1,0:T(8,128)S(1)} %add.21), channel_id=1, source_target_pairs={{0,16},{1,17},{2,18},{3,19},{4,20},{5,21},{6,22},{7,23},{8,24},{9,... | collective-permute-start | bytes 98312 | tf_op jit(solution)/shard_map/ppermute | solution.py:413
  65.2 5.3 %collective-permute-start.6 = (f32[64,128]{1,0:T(8,128)S(1)}, f32[64,128]{1,0:T(8,128)S(1)}, u32[]{:S(2)}, u32[]{:S(2)}) collective-permute-start(f32[64,128]{1,0:T(8,128)S(1)} %add.22), channel_id=1, source_target_pairs={{0,18},{1,19},{2,16},{3,17},{4,22},{5,23},{6,20},{7,21},{8,26},{9,... | collective-permute-start | bytes 98312 | tf_op jit(solution)/shard_map/ppermute | solution.py:413
  70.5 3.9 %collective-permute-start.7 = (f32[64,128]{1,0:T(8,128)S(1)}, f32[64,128]{1,0:T(8,128)S(1)}, u32[]{:S(2)}, u32[]{:S(2)}) collective-permute-start(f32[64,128]{1,0:T(8,128)S(1)} %add.23), channel_id=1, source_target_pairs={{0,32},{1,33},{2,34},{3,35},{4,36},{5,37},{6,38},{7,39},{8,40},{9,... | collective-permute-start | bytes 98312 | tf_op jit(solution)/shard_map/ppermute | solution.py:413
  74.4 5.1 %collective-permute-start.8 = (f32[64,128]{1,0:T(8,128)S(1)}, f32[64,128]{1,0:T(8,128)S(1)}, u32[]{:S(2)}, u32[]{:S(2)}) collective-permute-start(f32[64,128]{1,0:T(8,128)S(1)} %add.24), channel_id=1, source_target_pairs={{0,96},{1,97},{2,98},{3,99},{4,100},{5,101},{6,102},{7,103},{8,104... | collective-permute-start | bytes 98312 | tf_op jit(solution)/shard_map/ppermute | solution.py:413
  79.5 3.9 %collective-permute-start.9 = (f32[64,128]{1,0:T(8,128)S(1)}, f32[64,128]{1,0:T(8,128)S(1)}, u32[]{:S(2)}, u32[]{:S(2)}) collective-permute-start(f32[64,128]{1,0:T(8,128)S(1)} %add.25), channel_id=1, source_target_pairs={{0,4},{1,5},{2,6},{3,7},{4,0},{5,1},{6,2},{7,3},{8,12},{9,13},{10,... | collective-permute-start | bytes 98312 | tf_op jit(solution)/shard_map/ppermute | solution.py:413
  83.5 5.8 %collective-permute-start.10 = (f32[64,128]{1,0:T(8,128)S(1)}, f32[64,128]{1,0:T(8,128)S(1)}, u32[]{:S(2)}, u32[]{:S(2)}) collective-permute-start(f32[64,128]{1,0:T(8,128)S(1)} %add.26), channel_id=1, source_target_pairs={{0,12},{1,13},{2,14},{3,15},{4,8},{5,9},{6,10},{7,11},{8,4},{9,5},... | collective-permute-start | bytes 98312 | tf_op jit(solution)/shard_map/ppermute | solution.py:413

commit v2 on v1

--- a/solution.py
+++ b/solution.py
@@ -14,7 +14,7 @@
 )
 OPP = (0, 2, 1, 4, 3, 6, 5, 8, 7, 10, 9, 12, 11, 14, 13, 16, 15, 18, 17)
 Q = 19
-WIDE = 2
+WIDE = 4
 STEPS = 16 // WIDE
 SIDE = tuple(q for q in range(Q) if VEL[q][1])
 PLACE = {q: i for i, q in enumerate(SIDE)}
@@ -173,8 +173,8 @@
             gpad[q, z, pl.ds(136, 8), :] = halo
             gpad[q, z, pl.ds(144, 8), :] = cot[q, z, pl.ds(0, 8), :]
 
-    uo[:, pl.ds(152, 8), :] = jnp.ones((2 * WIDE, 8, 128), f32)
-    uo[:, pl.ds(312, 8), :] = jnp.ones((2 * WIDE, 8, 128), f32)
+    uo[...] = jnp.zeros_like(uo)
+    uo[:, pl.ds(19 * 9, 9), :] = jnp.ones((2 * WIDE, 9, 128), f32)
     acc_in[...] = jnp.zeros_like(acc_in)
     acc_out[...] = jnp.zeros_like(acc_out)
     accb[...] = jnp.zeros_like(accb)
@@ -212,20 +212,24 @@
             halves = [slice(h * 128, h * 128 + 128) for h in range(2 * WIDE)]
             for q in range(Q):
                 for h, part in enumerate(halves):
-                    uo[h, pl.ds(q * 8, 8), :] = u[q][:, part]
-                    uo[h, pl.ds(160 + q * 8, 8), :] = og[q][:, part]
+                    uo[h, pl.ds(q * 9, 8), :] = u[q][:, part]
+                    uo[h, pl.ds(216 + q * 9, 8), :] = og[q][:, part]
                 accb[pl.ds(q * 8, 8), :] += sum(og[q][:, part] for part in halves)
 
             def cells(first):
-                return join(
-                    *[uo[h, pl.ds(first + k, 20, stride=8), :] for k in range(8) for h in range(2 * WIDE)]
-                ).astype(bf16)
+                lines24 = join(
+                    *[uo[h, pl.ds(first + k, 24, stride=9), :] for k in range(8) for h in range(2 * WIDE)]
+                )
+                return jnp.concatenate([lines24, jnp.zeros((8, lines24.shape[1]), f32)], axis=0).astype(bf16)
 
             def units(values):
                 return join(*[values[k * 128 : k * 128 + 128] for k in range(8)])
 
-            acc_in[:, :20] += lax.dot_general(units(hb), cells(0), NT, preferred_element_type=f32)
-            acc_out[...] += lax.dot_general(cells(160), units(act), NT, preferred_element_type=f32)
+            left = jnp.concatenate([units(hb), cells(216)], axis=0)
+            right = jnp.concatenate([units(act), cells(0)], axis=0)
+            both = lax.dot_general(left, right, NT, preferred_element_type=f32)
+            acc_in[:, :32] += both[:128, 128:]
+            acc_out[...] += both[128:, :128]
         return [
             og[q] + ig[q * 8 : q * 8 + 8] + jnp.where(solid, g[OPP[q]], 0.0) for q in range(Q)
         ]
@@ -343,10 +347,11 @@
 
     lax.fori_loop(0, STEPS, third, 0)
     parts[pl.ds(0, 20), :] = acc_in[...].T[:20]
-    parts[pl.ds(20, 20), :] = acc_out[...]
+    parts[pl.ds(20, 20), :] = acc_out[pl.ds(0, 20), :]
+    flip[...] = jnp.zeros_like(flip)
     for q in range(Q):
-        parts[pl.ds(40 + q, 1), :] = jnp.sum(accb[pl.ds(q * 8, 8), :], axis=0, keepdims=True)
-    parts[pl.ds(59, 5), :] = jnp.zeros((5, 128), f32)
+        flip[pl.ds(q, 1), :128] = jnp.sum(accb[pl.ds(q * 8, 8), :], axis=0, keepdims=True)
+    parts[pl.ds(40, 8), :] = jnp.broadcast_to(jnp.sum(flip[:, :128].T, axis=0, keepdims=True), (8, 128))
 
 
 def main_call(*args):
@@ -354,7 +359,7 @@
     halo = pltpu.VMEM((152, 128), f32)
     return pl.pallas_call(
         main_kernel,
-        out_shape=[jax.ShapeDtypeStruct((Q, 2, 128, 128), f32), jax.ShapeDtypeStruct((64, 128), f32)],
+        out_shape=[jax.ShapeDtypeStruct((Q, 2, 128, 128), f32), jax.ShapeDtypeStruct((48, 128), f32)],
         in_specs=vmem(len(args)),
         out_specs=vmem(2),
         scratch_shapes=[
@@ -365,9 +370,9 @@
             pltpu.VMEM((2, Q, 8, 256), f32),
             pltpu.VMEM((2, Q, 8, 256), f32),
             pltpu.VMEM((128, 256), f32),
-            pltpu.VMEM((2 * WIDE, 320, 128), f32),
+            pltpu.VMEM((2 * WIDE, 432, 128), f32),
             pltpu.VMEM((128, 128), f32),
-            pltpu.VMEM((20, 128), f32),
+            pltpu.VMEM((32, 128), f32),
             pltpu.VMEM((152, 128), f32),
         ],
         compiler_params=pltpu.CompilerParams(vmem_limit_bytes=58 * 2**20),
@@ -381,37 +386,34 @@
 
 
 def summed(values):
-    shape = {axis: lax.axis_size(axis) for axis in ("gx", "gy")}
-    nx, ny = shape["gx"], shape["gy"]
-
-    def flat(partner):
+    nx, ny = lax.axis_size("gx"), lax.axis_size("gy")
+
+    def from_partner(values, partner):
         pairs = []
         for x in range(nx):
             for y in range(ny):
                 px, py = partner(x, y)
                 pairs.append((x * ny + y, px * ny + py))
-        return pairs
-
-    stages = []
-    if (nx, ny) == (8, 16):
-        other = (3, 2, 1, 0)
-        stages = [
-            lambda x, y: (x, y ^ 1),
-            lambda x, y: (x ^ 1, y),
-            lambda x, y: (x ^ 1, y ^ 2),
-            lambda x, y: (x ^ 2, y),
-            lambda x, y: (other[x // 2] * 2 + x % 2, y),
-            lambda x, y: (x, y ^ 4),
-            lambda x, y: (x, other[y // 4] * 4 + y % 4),
-        ]
-    else:
+        return lax.ppermute(values, ("gx", "gy"), pairs)
+
+    if (nx, ny) != (8, 16):
         for k in range(nx.bit_length() - 1):
-            stages.append(lambda x, y, k=k: (x ^ (1 << k), y))
+            values = values + from_partner(values, lambda x, y: (x ^ (1 << k), y))
         for k in range(ny.bit_length() - 1):
-            stages.append(lambda x, y, k=k: (x, y ^ (1 << k)))
-    for partner in stages:
-        values = values + lax.ppermute(values, ("gx", "gy"), flat(partner))
-    return values
+            values = values + from_partner(values, lambda x, y: (x, y ^ (1 << k)))
+        return values
+    got = [values] + [
+        from_partner(values, lambda x, y: (x ^ ((d >> 1) & 1), y ^ (d & 1) ^ (((d >> 2) & 1) << 1))) for d in range(1, 8)
+    ]
+    while len(got) > 1:
+        got = [got[i] + got[i + 1] for i in range(0, len(got), 2)]
+    copies = jnp.broadcast_to(got[0][None], (4,) + values.shape)
+    groups = [[2 * y + low for y in range(4)] for low in range(2)]
+    values = lax.all_to_all(copies, "gx", 0, 0, tiled=True, axis_index_groups=groups)
+    values = (values[0] + values[1]) + (values[2] + values[3])
+    other = (3, 2, 1, 0)
+    values = values + from_partner(values, lambda x, y: (x, y ^ 4))
+    return values + from_partner(values, lambda x, y: (x, other[y // 4] * 4 + y % 4))
 
 
 def shards(dist, cot, mask, weight_in, bias_in, weight_out, bias_out):
@@ -428,7 +430,7 @@
     total = summed(parts)
     cells = mask.size * lax.axis_size("gx") * lax.axis_size("gy")
     total = total * (1.0 / math.sqrt(cells))
-    return grad, total[:19], total[19], total[20:39].T, jnp.sum(total[40:59], axis=1)
+    return grad, total[:19], total[19], total[20:39].T, total[40, :19]
 
 
 def solution(mesh):

time: 91.2 us -> 87 us (0.954)
  blocking collectives: 0 us -> 9.77 us
  waiting for transfers between devices: 16 us -> 9.27 us
  Pallas kernels: 44.4 us -> 38.8 us
  starting transfers between devices: 25.3 us -> 23 us
  other arithmetic: 2.03 us -> 0.78 us
  local copies, waits for them, and re-layouts: 2.53 us -> 3.64 us
    all_to_all x0 -> x1, blocking collectives: none -> 9.77 us  [summed(): lax.all_to_all(copies, 'gx', 0, 0, tiled=True, axis_index_groups=groups)]
    ppermute x7 -> x9, waiting for transfers between devices: 13.8 us -> 7.08 us  [from_partner(): return lax.ppermute(values, ('gx', 'gy'), pairs)]
    pallas_call x1, Pallas kernels: 36 us -> 30.4 us  [main_call(): pl.pallas_call(main_kernel, out_shape=[jax.ShapeDtypeStruct((Q, 2, 128, 1...]
    ppermute x7 -> x9, starting transfers between devices: 15.8 us -> 13.5 us  [from_partner(): return lax.ppermute(values, ('gx', 'gy'), pairs)]
    reduce_sum x1 -> x0, other arithmetic: 1.23 us -> none  [shards(): jnp.sum(total[40:59], axis=1)]
  transfers between devices with their start and end apart: 11 -> 13, of which waited for: 8 -> 6; matrix products, arithmetic and copies ran while one was open for 1% -> 1% of each run, Pallas kernels for 3% -> 3%
where the time goes in v2:
time: 87 us; the launch traced here: 85.9 us
  Pallas kernels  38.8 us (45%)
  starting transfers between devices  23 us (26%)
  blocking collectives  9.77 us (11%)
  waiting for transfers between devices  9.27 us (11%)
  local copies, waits for them, and re-layouts  3.64 us (4%)
    pallas_call x1, Pallas kernels, main_call(): pl.pallas_call(main_kernel, out_shape=[jax.ShapeDtypeStruct((Q, 2, 128, 1...  30.4 us
    ppermute x9, starting transfers between devices, from_partner(): return lax.ppermute(values, ('gx', 'gy'), pairs)  13.5 us
    all_to_all x1, blocking collectives, summed(): lax.all_to_all(copies, 'gx', 0, 0, tiled=True, axis_index_groups=groups)  9.77 us
    ppermute x9, waiting for transfers between devices, from_partner(): return lax.ppermute(values, ('gx', 'gy'), pairs)  7.08 us
    ppermute x1, starting transfers between devices, shards(): from_right = lax.ppermute(side_down, 'gy', down)  5.36 us
    pallas_call x1, Pallas kernels, pack(): pl.pallas_call(pack_kernel, out_shape=[jax.ShapeDtypeStruct((160, 128), b...  4.05 us
    ppermute x1, starting transfers between devices, shards(): from_down = lax.ppermute(send_down, 'gx', down)  2.56 us
    pallas_call x1, Pallas kernels, make_weights(): pl.pallas_call(weights_kernel, out_shape=[jax.ShapeDtypeStruct((1024, 160...  2.27 us
  transfers between devices with their start and end apart: 13, of which 6 were waited for; matrix products, arithmetic and copies ran while one was open for 1% of the time, Pallas kernels for 3%

profile of v2, /device:TPU:0, one launch (start us, length us, event | category | flops | bytes accessed | tf_op | source)
XLA Modules:
  0.0 85.9 jit_solution(13717218399221728924)
XLA Ops:
  0.6 4.1 %shard_map.110 = (bf16[160,128]{1,0:T(8,128)(2,1)}, bf16[160,128]{1,0:T(8,128)(2,1)}, f32[640,128]{1,0:T(8,128)}) custom-call(f32[4864,128]{1,0:T(8,128)} %bitcast.15, f32[4864,128]{1,0:T(8,128)} %bitcast.16, s32[256,128]{1,0:T(8,128)} %bitcast.17), custom_call_target="tpu_custom_call" | custom-call | tf_op jit(solution)/shard_map/pallas_call | solution.py:105
  4.7 1.6 %collective-permute-start = (bf16[160,128]{1,0:T(8,128)(2,1)}, bf16[160,128]{1,0:T(8,128)(2,1)S(1)}, u32[]{:S(2)}, u32[]{:S(2)}) collective-permute-start(bf16[160,128]{1,0:T(8,128)(2,1)} %get-tuple-element.20), channel_id=1, source_target_pairs={{0,16},{16,32},{32,48},{48,64},{64,80},{80,96},{96,112},{112,0},{1... | collective-permute-start | bytes 122888 | tf_op jit(solution)/shard_map/ppermute | solution.py:422
  6.3 2.6 %collective-permute-start.1 = (bf16[160,128]{1,0:T(8,128)(2,1)}, bf16[160,128]{1,0:T(8,128)(2,1)S(1)}, u32[]{:S(2)}, u32[]{:S(2)}) collective-permute-start(bf16[160,128]{1,0:T(8,128)(2,1)} %get-tuple-element.21), channel_id=1, source_target_pairs={{16,0},{32,16},{48,32},{64,48},{80,64},{96,80},{112,96},{0,112},{1... | collective-permute-start | bytes 122888 | tf_op jit(solution)/shard_map/ppermute | solution.py:423
  8.8 2.2 %collective-permute-done.from_up = bf16[160,128]{1,0:T(8,128)(2,1)S(1)} collective-permute-done((bf16[160,128]{1,0:T(8,128)(2,1)}, bf16[160,128]{1,0:T(8,128)(2,1)S(1)}, u32[]{:S(2)}, u32[]{:S(2)}) %collective-permute-start) | collective-permute-done | bytes 40992 | tf_op jit(solution)/shard_map/ppermute | solution.py:422
  11.0 0.0 collective-permute-done.1.from_down
  11.0 0.6 copy-done.2
  11.6 0.0 copy-done.3
  11.7 2.1 %shard_map.111 = (bf16[160,256]{1,0:T(8,128)(2,1)}, bf16[160,256]{1,0:T(8,128)(2,1)}, f32[640,128]{1,0:T(8,128)}, f32[640,128]{1,0:T(8,128)}) custom-call(bf16[160,128]{1,0:T(8,128)(2,1)} %copy-done.2, bf16[160,128]{1,0:T(8,128)(2,1)} %copy-done.3, f32[640,128]{1,0:T(8,128)} %get-tuple-element.19.cols), custom_call_target="tpu_custom_call" | custom-call | tf_op jit(solution)/shard_map/pallas_call | solution.py:133
  13.7 0.0 collective-permute-start.2
  13.7 5.4 %collective-permute-start.3 = (bf16[160,256]{1,0:T(8,128)(2,1)}, bf16[160,256]{1,0:T(8,128)(2,1)S(1)}, u32[]{:S(2)}, u32[]{:S(2)}) collective-permute-start(bf16[160,256]{1,0:T(8,128)(2,1)} %get-tuple-element.24), channel_id=1, source_target_pairs={{1,0},{2,1},{3,2},{4,3},{5,4},{6,5},{7,6},{8,7},{9,8},{10,9},{11,1... | collective-permute-start | bytes 245768 | tf_op jit(solution)/shard_map/ppermute | solution.py:428
  19.1 0.7 copy.12.wout
  19.8 2.3 %shard_map.112 = (bf16[1024,160]{1,0:T(8,128)(2,1)}, bf16[1024,160]{1,0:T(8,128)(2,1)}, bf16[160,1024]{1,0:T(8,128)(2,1)}, bf16[160,1024]{1,0:T(8,128)(2,1)}, f32[152,128]{1,0:T(8,128)}) custom-call(bf16[19,128]{1,0:T(8,128)(2,1)} %win.1, bf16[128,19]{1,0:T(8,128)(2,1)} %copy.12.wout, f32[1,128]{1,0:T(1,128)} %bitcast.18, f32[1,19]{1,0:T(1,128)} %bitcast.19), custom_call_target="tpu_custom_call" | custom-call | flops 100000000 | bytes 2000000 | tf_op jit(solution)/shard_map/pallas_call | solution.py:65
  22.1 0.0 collective-permute-done.2.from_left
  22.1 0.6 copy-done
  22.7 0.0 copy-done.1
  22.8 30.4 %shard_map.113 = (f32[19,2,128,128]{3,2,1,0:T(8,128)}, f32[48,128]{1,0:T(8,128)}) custom-call(f32[19,2,128,128]{3,2,1,0:T(8,128)} %dist.1, f32[19,2,128,128]{3,2,1,0:T(8,128)} %cot.1, s32[2,128,128]{2,1,0:T(8,128)} %mask.1, f32[640,128]{1,0:T(8,128)} %get-tuple-element.19.cols, f32[640,128]{1,0:T(8,128)} %get-tuple-element.22.edge, ...), custom_call_target="tpu_custom_call" | custom-call | tf_op jit(solution)/shard_map/pallas_call | solution.py:360
  53.1 3.7 %collective-permute-start.10 = (f32[48,128]{1,0:T(8,128)}, f32[48,128]{1,0:T(8,128)S(1)}, u32[]{:S(2)}, u32[]{:S(2)}) collective-permute-start(f32[48,128]{1,0:T(8,128)} %get-tuple-element.32), channel_id=1, source_target_pairs={{0,19},{1,18},{2,17},{3,16},{4,23},{5,22},{6,21},{7,20},{8,27},{9,... | collective-permute-start | bytes 73736 | tf_op jit(solution)/shard_map/ppermute | solution.py:397
  56.8 3.3 %collective-permute-start.7 = (f32[48,128]{1,0:T(8,128)}, f32[48,128]{1,0:T(8,128)S(1)}, u32[]{:S(2)}, u32[]{:S(2)}) collective-permute-start(f32[48,128]{1,0:T(8,128)} %get-tuple-element.32), channel_id=1, source_target_pairs={{0,2},{1,3},{2,0},{3,1},{4,6},{5,7},{6,4},{7,5},{8,10},{9,11},{10,... | collective-permute-start | bytes 73736 | tf_op jit(solution)/shard_map/ppermute | solution.py:397
  60.2 0.5 collective-permute-start.6
  60.7 1.2 %collective-permute-start.5 = (f32[48,128]{1,0:T(8,128)}, f32[48,128]{1,0:T(8,128)S(1)}, u32[]{:S(2)}, u32[]{:S(2)}) collective-permute-start(f32[48,128]{1,0:T(8,128)} %get-tuple-element.32), channel_id=1, source_target_pairs={{0,16},{1,17},{2,18},{3,19},{4,20},{5,21},{6,22},{7,23},{8,24},{9,... | collective-permute-start | bytes 73736 | tf_op jit(solution)/shard_map/ppermute | solution.py:397
  61.8 1.0 %collective-permute-done.9 = f32[48,128]{1,0:T(8,128)S(1)} collective-permute-done((f32[48,128]{1,0:T(8,128)}, f32[48,128]{1,0:T(8,128)S(1)}, u32[]{:S(2)}, u32[]{:S(2)}) %collective-permute-start.9) | collective-permute-done | bytes 24608 | tf_op jit(solution)/shard_map/ppermute | solution.py:397
  62.9 0.8 collective-permute-done.6
  63.7 1.0 %collective-permute-done.5 = f32[48,128]{1,0:T(8,128)S(1)} collective-permute-done((f32[48,128]{1,0:T(8,128)}, f32[48,128]{1,0:T(8,128)S(1)}, u32[]{:S(2)}, u32[]{:S(2)}) %collective-permute-start.5) | collective-permute-done | bytes 24608 | tf_op jit(solution)/shard_map/ppermute | solution.py:397
  64.7 0.8 add_add_fusion
  65.5 9.8 %all_to_all.5 = f32[4,48,128]{2,1,0:T(8,128)S(1)} all-to-all(f32[4,48,128]{2,1,0:T(8,128)S(1)} %broadcast_in_dim.14), channel_id=1, replica_groups={{0,32,64,96},{16,48,80,112},{1,33,65,97},{17,49,81,113},{2,34,66,98},{1..., dimensions={0} | all-to-all | bytes 196608 | tf_op jit(solution)/shard_map/all_to_all | solution.py:412
  75.3 2.0 %collective-permute-start.11 = (f32[48,128]{1,0:T(8,128)S(1)}, f32[48,128]{1,0:T(8,128)S(1)}, u32[]{:S(2)}, u32[]{:S(2)}) collective-permute-start(f32[48,128]{1,0:T(8,128)S(1)} %fusion.1), channel_id=1, source_target_pairs={{0,4},{1,5},{2,6},{3,7},{4,0},{5,1},{6,2},{7,3},{8,12},{9,13},{10,... | collective-permute-start | bytes 73736 | tf_op jit(solution)/shard_map/ppermute | solution.py:397
  77.3 1.9 %collective-permute-done.11 = f32[48,128]{1,0:T(8,128)S(1)} collective-permute-done((f32[48,128]{1,0:T(8,128)S(1)}, f32[48,128]{1,0:T(8,128)S(1)}, u32[]{:S(2)}, u32[]{:S(2)}) %collective-permute-start.11) | collective-permute-done | bytes 24608 | tf_op jit(solution)/shard_map/ppermute | solution.py:397
  79.2 2.8 %collective-permute-start.12 = (f32[48,128]{1,0:T(8,128)S(1)}, f32[48,128]{1,0:T(8,128)S(1)}, u32[]{:S(2)}, u32[]{:S(2)}) collective-permute-start(f32[48,128]{1,0:T(8,128)S(1)} %fusion.2), channel_id=1, source_target_pairs={{0,12},{1,13},{2,14},{3,15},{4,8},{5,9},{6,10},{7,11},{8,4},{9,5},... | collective-permute-start | bytes 73736 | tf_op jit(solution)/shard_map/ppermute | solution.py:397
  82.0 2.3 %collective-permute-done.12 = f32[48,128]{1,0:T(8,128)S(1)} collective-permute-done((f32[48,128]{1,0:T(8,128)S(1)}, f32[48,128]{1,0:T(8,128)S(1)}, u32[]{:S(2)}, u32[]{:S(2)}) %collective-permute-start.12) | collective-permute-done | bytes 24608 | tf_op jit(solution)/shard_map/ppermute | solution.py:397
  84.3 0.5 slice_bitcast_fusion.2
  84.8 0.5 slice_bitcast_fusion.1
  85.3 0.6 slice_bitcast_fusion
  (18 shorter events, 0.1 us)
Async XLA Ops:
  0.6 18.5 %copy-start.4 = (bf16[128,19]{0,1:T(8,128)(2,1)S(1)}, bf16[128,19]{0,1:T(8,128)(2,1)}, u32[]{:S(2)}) copy-start(bf16[128,19]{0,1:T(8,128)(2,1)} %param.12) | copy-start | bytes 14596
  4.7 6.3 %collective-permute-start = (bf16[160,128]{1,0:T(8,128)(2,1)}, bf16[160,128]{1,0:T(8,128)(2,1)S(1)}, u32[]{:S(2)}, u32[]{:S(2)}) collective-permute-start(bf16[160,128]{1,0:T(8,128)(2,1)} %get-tuple-element.20), channel_id=1, source_target_pairs={{0,16},{16,32},{32,48},{48,64},{64,80},{80,96},{96,112},{112,0},{1... | collective-permute-start | bytes 122888 | tf_op jit(solution)/shard_map/ppermute | solution.py:422
  6.3 4.8 %collective-permute-start.1 = (bf16[160,128]{1,0:T(8,128)(2,1)}, bf16[160,128]{1,0:T(8,128)(2,1)S(1)}, u32[]{:S(2)}, u32[]{:S(2)}) collective-permute-start(bf16[160,128]{1,0:T(8,128)(2,1)} %get-tuple-element.21), channel_id=1, source_target_pairs={{16,0},{32,16},{48,32},{64,48},{80,64},{96,80},{112,96},{0,112},{1... | collective-permute-start | bytes 122888 | tf_op jit(solution)/shard_map/ppermute | solution.py:423
  11.0 0.6 copy-start.2
  11.0 0.6 copy-start.3
  13.7 8.3 %collective-permute-start.2 = (bf16[160,256]{1,0:T(8,128)(2,1)}, bf16[160,256]{1,0:T(8,128)(2,1)S(1)}, u32[]{:S(2)}, u32[]{:S(2)}) collective-permute-start(bf16[160,256]{1,0:T(8,128)(2,1)} %get-tuple-element.23), channel_id=1, source_target_pairs={{0,1},{1,2},{2,3},{3,4},{4,5},{5,6},{6,7},{7,8},{8,9},{9,10},{10,1... | collective-permute-start | bytes 245768 | tf_op jit(solution)/shard_map/ppermute | solution.py:427
  13.7 8.4 %collective-permute-start.3 = (bf16[160,256]{1,0:T(8,128)(2,1)}, bf16[160,256]{1,0:T(8,128)(2,1)S(1)}, u32[]{:S(2)}, u32[]{:S(2)}) collective-permute-start(bf16[160,256]{1,0:T(8,128)(2,1)} %get-tuple-element.24), channel_id=1, source_target_pairs={{1,0},{2,1},{3,2},{4,3},{5,4},{6,5},{7,6},{8,7},{9,8},{10,9},{11,1... | collective-permute-start | bytes 245768 | tf_op jit(solution)/shard_map/ppermute | solution.py:428
  22.1 0.6 copy-start
  22.1 0.7 copy-start.1
  53.1 7.5 %collective-permute-start.10 = (f32[48,128]{1,0:T(8,128)}, f32[48,128]{1,0:T(8,128)S(1)}, u32[]{:S(2)}, u32[]{:S(2)}) collective-permute-start(f32[48,128]{1,0:T(8,128)} %get-tuple-element.32), channel_id=1, source_target_pairs={{0,19},{1,18},{2,17},{3,16},{4,23},{5,22},{6,21},{7,20},{8,27},{9,... | collective-permute-start | bytes 73736 | tf_op jit(solution)/shard_map/ppermute | solution.py:397
  56.8 6.0 %collective-permute-start.9 = (f32[48,128]{1,0:T(8,128)}, f32[48,128]{1,0:T(8,128)S(1)}, u32[]{:S(2)}, u32[]{:S(2)}) collective-permute-start(f32[48,128]{1,0:T(8,128)} %get-tuple-element.32), channel_id=1, source_target_pairs={{0,18},{1,19},{2,16},{3,17},{4,22},{5,23},{6,20},{7,21},{8,26},{9,... | collective-permute-start | bytes 73736 | tf_op jit(solution)/shard_map/ppermute | solution.py:397
  56.8 6.0 %collective-permute-start.8 = (f32[48,128]{1,0:T(8,128)}, f32[48,128]{1,0:T(8,128)S(1)}, u32[]{:S(2)}, u32[]{:S(2)}) collective-permute-start(f32[48,128]{1,0:T(8,128)} %get-tuple-element.32), channel_id=1, source_target_pairs={{0,3},{1,2},{2,1},{3,0},{4,7},{5,6},{6,5},{7,4},{8,11},{9,10},{10,... | collective-permute-start | bytes 73736 | tf_op jit(solution)/shard_map/ppermute | solution.py:397
  56.8 6.0 %collective-permute-start.7 = (f32[48,128]{1,0:T(8,128)}, f32[48,128]{1,0:T(8,128)S(1)}, u32[]{:S(2)}, u32[]{:S(2)}) collective-permute-start(f32[48,128]{1,0:T(8,128)} %get-tuple-element.32), channel_id=1, source_target_pairs={{0,2},{1,3},{2,0},{3,1},{4,6},{5,7},{6,4},{7,5},{8,10},{9,11},{10,... | collective-permute-start | bytes 73736 | tf_op jit(solution)/shard_map/ppermute | solution.py:397
  60.2 3.5 %collective-permute-start.6 = (f32[48,128]{1,0:T(8,128)}, f32[48,128]{1,0:T(8,128)S(1)}, u32[]{:S(2)}, u32[]{:S(2)}) collective-permute-start(f32[48,128]{1,0:T(8,128)} %get-tuple-element.32), channel_id=1, source_target_pairs={{0,17},{1,16},{2,19},{3,18},{4,21},{5,20},{6,23},{7,22},{8,25},{9,... | collective-permute-start | bytes 73736 | tf_op jit(solution)/shard_map/ppermute | solution.py:397
  60.7 4.0 %collective-permute-start.5 = (f32[48,128]{1,0:T(8,128)}, f32[48,128]{1,0:T(8,128)S(1)}, u32[]{:S(2)}, u32[]{:S(2)}) collective-permute-start(f32[48,128]{1,0:T(8,128)} %get-tuple-element.32), channel_id=1, source_target_pairs={{0,16},{1,17},{2,18},{3,19},{4,20},{5,21},{6,22},{7,23},{8,24},{9,... | collective-permute-start | bytes 73736 | tf_op jit(solution)/shard_map/ppermute | solution.py:397
  62.9 1.8 %collective-permute-start.4 = (f32[48,128]{1,0:T(8,128)}, f32[48,128]{1,0:T(8,128)S(1)}, u32[]{:S(2)}, u32[]{:S(2)}) collective-permute-start(f32[48,128]{1,0:T(8,128)} %get-tuple-element.32), channel_id=1, source_target_pairs={{0,1},{1,0},{2,3},{3,2},{4,5},{5,4},{6,7},{7,6},{8,9},{9,8},{10,11... | collective-permute-start | bytes 73736 | tf_op jit(solution)/shard_map/ppermute | solution.py:397
  75.3 3.9 %collective-permute-start.11 = (f32[48,128]{1,0:T(8,128)S(1)}, f32[48,128]{1,0:T(8,128)S(1)}, u32[]{:S(2)}, u32[]{:S(2)}) collective-permute-start(f32[48,128]{1,0:T(8,128)S(1)} %fusion.1), channel_id=1, source_target_pairs={{0,4},{1,5},{2,6},{3,7},{4,0},{5,1},{6,2},{7,3},{8,12},{9,13},{10,... | collective-permute-start | bytes 73736 | tf_op jit(solution)/shard_map/ppermute | solution.py:397
  79.2 5.1 %collective-permute-start.12 = (f32[48,128]{1,0:T(8,128)S(1)}, f32[48,128]{1,0:T(8,128)S(1)}, u32[]{:S(2)}, u32[]{:S(2)}) collective-permute-start(f32[48,128]{1,0:T(8,128)S(1)} %fusion.2), channel_id=1, source_target_pairs={{0,12},{1,13},{2,14},{3,15},{4,8},{5,9},{6,10},{7,11},{8,4},{9,5},... | collective-permute-start | bytes 73736 | tf_op jit(solution)/shard_map/ppermute | solution.py:397

commit v3 on v2

--- a/solution.py
+++ b/solution.py
@@ -1,3 +1,4 @@
+import functools
 import math
 
 import jax
@@ -33,13 +34,13 @@
     return [pl.BlockSpec(memory_space=pltpu.VMEM)] * n
 
 
-def weights_kernel(win, wout, bias, bias_out, a_in, a_out, b_out, b_in, bias_rows):
+def weights_kernel(win, wtout, bias, bias_out, a_in, a_out, b_out, b_in, bias_rows):
     TN = (((0,), (0,)), ((), ()))
     rep = jnp.where(iota((Q, 160), 1) // 8 == iota((Q, 160), 0), 1.0, 0.0).astype(bf16)
     rept = jnp.where(iota((160, Q), 0) // 8 == iota((160, Q), 1), 1.0, 0.0).astype(bf16)
     wide_in = lax.dot_general(win[...], rep, TN, preferred_element_type=f32)
-    wide_out = jnp.dot(wout[...], rep, preferred_element_type=f32)
-    tall_out = lax.dot_general(rept, wout[...], NT, preferred_element_type=f32)
+    wide_out = lax.dot_general(wtout[...], rep, TN, preferred_element_type=f32)
+    tall_out = jnp.dot(rept, wtout[...], preferred_element_type=f32)
     tall_in = jnp.dot(rept, win[...], preferred_element_type=f32)
     b = jnp.broadcast_to(bias[...], (128, 128)).T
     b = jnp.concatenate([b, b[:, :32]], axis=1)
@@ -70,7 +71,7 @@
         in_specs=vmem(4),
         out_specs=vmem(5),
         cost_estimate=pl.CostEstimate(flops=10**8, bytes_accessed=2 * 10**6, transcendentals=0),
-    )(weight_in, weight_out, bias_in[None], bias_out[None])
+    )(weight_in, weight_out.T, bias_in[None], bias_out[None])
 
 
 def pack_kernel(dist, cot, mask, up, down, cols, line):
@@ -140,16 +141,41 @@
 
 
 def main_kernel(
-    dist, cot, mask, cols, edge, from_left, from_right, lines,
+    dist_far, cot_far, mask, cols, edge, from_left, from_right, lines,
     a_in, a_out, b_out, b_in, bias_out,
-    out, parts,
-    post, gmid, gpad, hid, hpost, hcot, hmid, strip, spost, smid, flip, uo, acc_in, acc_out, accb,
+    out_far, parts,
+    dist, out, in_sem, cot_sem, out_sem, post, gmid, gpad, hid, hpost, hcot, hmid, strip, spost, smid, flip, uo, acc_in, acc_out, accb,
 ):
     lane = iota((8, 128), 1)
     row8 = iota((8, 128), 0)
 
     def join(*parts):
         return jnp.concatenate(parts, axis=1)
+
+    def rows_of(b, offset):
+        return [pl.multiple_of((b + w * STEPS) * 8, 8) + offset for w in range(WIDE)]
+
+    def in_copies(b):
+        return [
+            pltpu.make_async_copy(
+                dist_far.at[:, :, pl.ds(r, 8), :], dist.at[:, :, pl.ds(r, 8), :], in_sem.at[b * WIDE + w]
+            )
+            for w, r in enumerate(rows_of(b, 0))
+        ]
+
+    def out_copies(b):
+        return [
+            pltpu.make_async_copy(
+                out.at[:, :, pl.ds(r, 8), :], out_far.at[:, :, pl.ds(r, 8), :], out_sem.at[b * WIDE + w]
+            )
+            for w, r in enumerate(rows_of(b, 0))
+        ]
+
+    for b in range(STEPS):
+        for copy in in_copies(b):
+            copy.start()
+    cot_copy = pltpu.make_async_copy(cot_far, gpad.at[:, :, pl.ds(8, 128), :], cot_sem)
+    cot_copy.start()
 
     strip[0] = cols[...]
     strip[1] = edge[...]
@@ -163,15 +189,6 @@
 
     def line_of(i):
         return lines[pl.ds(i * 8, 8), :]
-
-    for q in range(Q):
-        for z in range(2):
-            i = 2 * q + z
-            gpad[q, z, pl.ds(8, 128), :] = cot[q, z]
-            halo = line_of(40 + i)
-            gpad[q, z, pl.ds(0, 8), :] = halo
-            gpad[q, z, pl.ds(136, 8), :] = halo
-            gpad[q, z, pl.ds(144, 8), :] = cot[q, z, pl.ds(0, 8), :]
 
     uo[...] = jnp.zeros_like(uo)
     uo[:, pl.ds(19 * 9, 9), :] = jnp.ones((2 * WIDE, 9, 128), f32)
@@ -300,10 +317,9 @@
 
     outer_solid = join(line_of(38), line_of(39), strip_of(38), strip_of(39)) > 0.5
 
-    def rows_of(b, offset):
-        return [pl.multiple_of((b + w * STEPS) * 8, 8) + offset for w in range(WIDE)]
-
     def first(b, carry):
+        for copy in in_copies(b):
+            copy.wait()
         put(post, rows_of(b, 8), collide(block(dist, rows_of(b, 0)), solid_at(rows_of(b, 0)), b))
         return carry
 
@@ -321,6 +337,14 @@
         -1,
     )
 
+    cot_copy.wait()
+    for q in range(Q):
+        for z in range(2):
+            halo = line_of(40 + 2 * q + z)
+            gpad[q, z, pl.ds(0, 8), :] = halo
+            gpad[q, z, pl.ds(136, 8), :] = halo
+            gpad[q, z, pl.ds(144, 8), :] = gpad[q, z, pl.ds(8, 8), :]
+
     def second(b, carry):
         u = streamed(post, hpost, rows_of(b, 8), 1)
         g = streamed(gpad, hcot, rows_of(b, 8), -1)
@@ -343,15 +367,23 @@
         g = streamed(gmid, hmid, rows_of(b, 8), -1)
         rows = rows_of(b, 0)
         put(out, rows, backward(block(dist, rows), g, solid_at(rows), hid[b], True))
+        for copy in out_copies(b):
+            copy.start()
         return carry
 
     lax.fori_loop(0, STEPS, third, 0)
-    parts[pl.ds(0, 20), :] = acc_in[...].T[:20]
-    parts[pl.ds(20, 20), :] = acc_out[pl.ds(0, 20), :]
+    for b in range(STEPS):
+        for copy in out_copies(b):
+            copy.wait()
     flip[...] = jnp.zeros_like(flip)
+    flip[pl.ds(20, 20), :128] = acc_out[pl.ds(0, 20), :]
     for q in range(Q):
-        flip[pl.ds(q, 1), :128] = jnp.sum(accb[pl.ds(q * 8, 8), :], axis=0, keepdims=True)
-    parts[pl.ds(40, 8), :] = jnp.broadcast_to(jnp.sum(flip[:, :128].T, axis=0, keepdims=True), (8, 128))
+        flip[pl.ds(q, 1), 128:] = jnp.sum(accb[pl.ds(q * 8, 8), :], axis=0, keepdims=True)
+    own = acc_in[...]
+    lane128 = iota((128, 128), 1)
+    biases = jnp.broadcast_to(jnp.sum(flip[:, 128:], axis=1, keepdims=True), (128, 128))
+    own = jnp.where(lane128 < 20, own, jnp.where(lane128 == 40, biases, flip[:, :128].T))
+    parts[...] = own[:, :48]
 
 
 def main_call(*args):
@@ -359,10 +391,15 @@
     halo = pltpu.VMEM((152, 128), f32)
     return pl.pallas_call(
         main_kernel,
-        out_shape=[jax.ShapeDtypeStruct((Q, 2, 128, 128), f32), jax.ShapeDtypeStruct((48, 128), f32)],
-        in_specs=vmem(len(args)),
-        out_specs=vmem(2),
+        out_shape=[jax.ShapeDtypeStruct((Q, 2, 128, 128), f32), jax.ShapeDtypeStruct((128, 48), f32)],
+        in_specs=[pl.BlockSpec(memory_space=pl.ANY)] * 2 + vmem(len(args) - 2),
+        out_specs=[pl.BlockSpec(memory_space=pl.ANY)] + vmem(1),
         scratch_shapes=[
+            pltpu.VMEM((Q, 2, 128, 128), f32),
+            pltpu.VMEM((Q, 2, 128, 128), f32),
+            pltpu.SemaphoreType.DMA((16,)),
+            pltpu.SemaphoreType.DMA,
+            pltpu.SemaphoreType.DMA((16,)),
             field, field, field,
             pltpu.VMEM((STEPS, 1024, 256 * WIDE), f32),
             halo, halo, halo,
@@ -386,34 +423,30 @@
 
 
 def summed(values):
-    nx, ny = lax.axis_size("gx"), lax.axis_size("gy")
-
-    def from_partner(values, partner):
-        pairs = []
-        for x in range(nx):
-            for y in range(ny):
-                px, py = partner(x, y)
-                pairs.append((x * ny + y, px * ny + py))
-        return lax.ppermute(values, ("gx", "gy"), pairs)
-
-    if (nx, ny) != (8, 16):
-        for k in range(nx.bit_length() - 1):
-            values = values + from_partner(values, lambda x, y: (x ^ (1 << k), y))
-        for k in range(ny.bit_length() - 1):
-            values = values + from_partner(values, lambda x, y: (x, y ^ (1 << k)))
-        return values
-    got = [values] + [
-        from_partner(values, lambda x, y: (x ^ ((d >> 1) & 1), y ^ (d & 1) ^ (((d >> 2) & 1) << 1))) for d in range(1, 8)
-    ]
-    while len(got) > 1:
-        got = [got[i] + got[i + 1] for i in range(0, len(got), 2)]
-    copies = jnp.broadcast_to(got[0][None], (4,) + values.shape)
-    groups = [[2 * y + low for y in range(4)] for low in range(2)]
-    values = lax.all_to_all(copies, "gx", 0, 0, tiled=True, axis_index_groups=groups)
-    values = (values[0] + values[1]) + (values[2] + values[3])
-    other = (3, 2, 1, 0)
-    values = values + from_partner(values, lambda x, y: (x, y ^ 4))
-    return values + from_partner(values, lambda x, y: (x, other[y // 4] * 4 + y % 4))
+    axes = ("gx", "gy")
+    count = lax.axis_size("gx") * lax.axis_size("gy")
+    rows = values.shape[0] // count
+    got = lax.all_to_all(values, axes, 0, 0, tiled=True)
+    mine = jnp.sum(got.reshape(count, rows, values.shape[1]), axis=0)
+    return lax.all_to_all(jnp.tile(mine, (count, 1)), axes, 0, 0, tiled=True)
+
+
+def finish_kernel(factor, total, d_in, d_bias_in, d_out, d_bias_out):
+    wide = jnp.concatenate([total[...], jnp.zeros((128, 80), f32)], axis=1)
+    rows = wide.T * factor
+    d_in[...] = rows[:19]
+    d_bias_in[...] = rows[19:20]
+    d_out[...] = rows[20:39]
+    d_bias_out[...] = rows[40:41, :19]
+
+
+def finish(total, factor):
+    return pl.pallas_call(
+        functools.partial(finish_kernel, factor),
+        out_shape=[jax.ShapeDtypeStruct(s, f32) for s in ((19, 128), (1, 128), (19, 128), (1, 19))],
+        in_specs=vmem(1),
+        out_specs=vmem(4),
+    )(total)
 
 
 def shards(dist, cot, mask, weight_in, bias_in, weight_out, bias_out):
@@ -429,8 +462,8 @@
     grad, parts = main_call(dist, cot, mask, cols, edge, from_left, from_right, lines, *nets)
     total = summed(parts)
     cells = mask.size * lax.axis_size("gx") * lax.axis_size("gy")
-    total = total * (1.0 / math.sqrt(cells))
-    return grad, total[:19], total[19], total[20:39].T, total[40, :19]
+    d_in, d_bias_in, d_out, d_bias_out = finish(total, 1.0 / math.sqrt(cells))
+    return grad, d_in, d_bias_in[0], d_out.T, d_bias_out[0]
 
 
 def solution(mesh):

time: 87 us -> 90.3 us (1.038)
  blocking collectives: 9.77 us -> 35.6 us
  starting transfers between devices: 23 us -> 9.49 us
  waiting for transfers between devices: 9.27 us -> 2.24 us
  local copies, waits for them, and re-layouts: 3.64 us -> 1.28 us
  Pallas kernels: 38.8 us -> 40.2 us
    all_to_all x1 -> x2, blocking collectives: 9.77 us -> 35.6 us  [the longest x1 21.1 us: summed(): got = lax.all_to_all(values, axes, 0, 0, tiled=True)]
    ppermute x9 -> x0, starting transfers between devices: 13.5 us -> none  [from_partner(): return lax.ppermute(values, ('gx', 'gy'), pairs)]
    ppermute x9 -> x0, waiting for transfers between devices: 7.08 us -> none  [from_partner(): return lax.ppermute(values, ('gx', 'gy'), pairs)]
    pallas_call x0 -> x1, Pallas kernels: none -> 1.52 us  [finish(): pl.pallas_call(functools.partial(finish_kernel, factor), out_shape=[jax.S...]
    squeeze x2 -> x0, local copies, waits for them, and re-layouts: 1.03 us -> none  [shards(): return (grad, total[:19], total[19], total[20:39].T, total[40, :19])]
    unnamed x11 -> x8, local copies, waits for them, and re-layouts: 2 us -> 1.24 us
  transfers between devices with their start and end apart: 13 -> 4, of which waited for: 6 -> 1; matrix products, arithmetic and copies ran while one was open for 1% -> 0% of each run, Pallas kernels for 3% -> 3%
where the time goes in v3:
time: 90.3 us; the launch traced here: 89.6 us
  Pallas kernels  40.2 us (45%)
  blocking collectives  35.6 us (39%)
  starting transfers between devices  9.49 us (11%)
  waiting for transfers between devices  2.24 us (2%)
  local copies, waits for them, and re-layouts  1.28 us (1%)
    pallas_call x1, Pallas kernels, main_call(): pl.pallas_call(main_kernel, out_shape=[jax.ShapeDtypeStruct((Q, 2, 128, 1...  30.2 us
    all_to_all x1, blocking collectives, summed(): got = lax.all_to_all(values, axes, 0, 0, tiled=True)  21.1 us
    all_to_all x1, blocking collectives, summed(): return lax.all_to_all(jnp.tile(mine, (count, 1)), axes, 0, 0, tiled=True)  14.5 us
    ppermute x1, starting transfers between devices, shards(): from_right = lax.ppermute(side_down, 'gy', down)  5.36 us
    pallas_call x1, Pallas kernels, pack(): pl.pallas_call(pack_kernel, out_shape=[jax.ShapeDtypeStruct((160, 128), b...  4.07 us
    ppermute x1, starting transfers between devices, shards(): from_down = lax.ppermute(send_down, 'gx', down)  2.56 us
    pallas_call x1, Pallas kernels, make_weights(): pl.pallas_call(weights_kernel, out_shape=[jax.ShapeDtypeStruct((1024, 160...  2.32 us
    ppermute x1, waiting for transfers between devices, shards(): from_up = lax.ppermute(send_up, 'gx', up)  2.19 us
  transfers between devices with their start and end apart: 4, of which 1 were waited for; matrix products, arithmetic and copies ran while one was open for 0% of the time, Pallas kernels for 3%

profile of v3, /device:TPU:0, one launch (start us, length us, event | category | flops | bytes accessed | tf_op | source)
XLA Modules:
  0.0 89.6 jit_solution(15421782305951915983)
XLA Ops:
  0.6 4.1 %shard_map.110 = (bf16[160,128]{1,0:T(8,128)(2,1)}, bf16[160,128]{1,0:T(8,128)(2,1)}, f32[640,128]{1,0:T(8,128)}) custom-call(f32[4864,128]{1,0:T(8,128)} %bitcast.13, f32[4864,128]{1,0:T(8,128)} %bitcast.14, s32[256,128]{1,0:T(8,128)} %bitcast.15), custom_call_target="tpu_custom_call" | custom-call | tf_op jit(solution)/shard_map/pallas_call | solution.py:106
  4.7 1.6 %collective-permute-start = (bf16[160,128]{1,0:T(8,128)(2,1)}, bf16[160,128]{1,0:T(8,128)(2,1)S(1)}, u32[]{:S(2)}, u32[]{:S(2)}) collective-permute-start(bf16[160,128]{1,0:T(8,128)(2,1)} %get-tuple-element.24), channel_id=1, source_target_pairs={{0,16},{16,32},{32,48},{48,64},{64,80},{80,96},{96,112},{112,0},{1... | collective-permute-start | bytes 122888 | tf_op jit(solution)/shard_map/ppermute | solution.py:455
  6.3 2.6 %collective-permute-start.1 = (bf16[160,128]{1,0:T(8,128)(2,1)}, bf16[160,128]{1,0:T(8,128)(2,1)S(1)}, u32[]{:S(2)}, u32[]{:S(2)}) collective-permute-start(bf16[160,128]{1,0:T(8,128)(2,1)} %get-tuple-element.25), channel_id=1, source_target_pairs={{16,0},{32,16},{48,32},{64,48},{80,64},{96,80},{112,96},{0,112},{1... | collective-permute-start | bytes 122888 | tf_op jit(solution)/shard_map/ppermute | solution.py:456
  8.8 2.2 %collective-permute-done.from_up = bf16[160,128]{1,0:T(8,128)(2,1)S(1)} collective-permute-done((bf16[160,128]{1,0:T(8,128)(2,1)}, bf16[160,128]{1,0:T(8,128)(2,1)S(1)}, u32[]{:S(2)}, u32[]{:S(2)}) %collective-permute-start) | collective-permute-done | bytes 40992 | tf_op jit(solution)/shard_map/ppermute | solution.py:455
  11.0 0.0 copy-start.2
  11.0 0.0 collective-permute-done.1.from_down
  11.0 0.0 copy-start.3
  11.0 0.6 copy-done.2
  11.6 0.0 copy-done.3
  11.6 2.0 %shard_map.111 = (bf16[160,256]{1,0:T(8,128)(2,1)}, bf16[160,256]{1,0:T(8,128)(2,1)}, f32[640,128]{1,0:T(8,128)}, f32[640,128]{1,0:T(8,128)}) custom-call(bf16[160,128]{1,0:T(8,128)(2,1)} %copy-done.2, bf16[160,128]{1,0:T(8,128)(2,1)} %copy-done.3, f32[640,128]{1,0:T(8,128)} %get-tuple-element.23.cols), custom_call_target="tpu_custom_call" | custom-call | tf_op jit(solution)/shard_map/pallas_call | solution.py:134
  13.7 0.0 collective-permute-start.2
  13.7 5.4 %collective-permute-start.3 = (bf16[160,256]{1,0:T(8,128)(2,1)}, bf16[160,256]{1,0:T(8,128)(2,1)S(1)}, u32[]{:S(2)}, u32[]{:S(2)}) collective-permute-start(bf16[160,256]{1,0:T(8,128)(2,1)} %get-tuple-element.28), channel_id=1, source_target_pairs={{1,0},{2,1},{3,2},{4,3},{5,4},{6,5},{7,6},{8,7},{9,8},{10,9},{11,1... | collective-permute-start | bytes 245768 | tf_op jit(solution)/shard_map/ppermute | solution.py:461
  19.1 2.3 %shard_map.112 = (bf16[1024,160]{1,0:T(8,128)(2,1)}, bf16[1024,160]{1,0:T(8,128)(2,1)}, bf16[160,1024]{1,0:T(8,128)(2,1)}, bf16[160,1024]{1,0:T(8,128)(2,1)}, f32[152,128]{1,0:T(8,128)}) custom-call(bf16[19,128]{1,0:T(8,128)(2,1)} %win.1, bf16[19,128]{1,0:T(8,128)(2,1)} %bitcast.19, f32[1,128]{1,0:T(1,128)} %bitcast.20, f32[1,19]{1,0:T(1,128)} %bitcast.21), custom_call_target="tpu_custom_call" | custom-call | flops 100000000 | bytes 2000000 | tf_op jit(solution)/shard_map/pallas_call | solution.py:66
  21.4 0.0 collective-permute-done.2.from_left
  21.4 0.0 copy-start
  21.4 0.0 collective-permute-done.3.from_right
  21.4 0.0 copy-start.1
  21.4 0.6 copy-done
  22.0 0.0 copy-done.1
  22.1 30.2 %shard_map.113 = (f32[19,2,128,128]{3,2,1,0:T(8,128)}, f32[128,48]{1,0:T(8,128)}) custom-call(f32[19,2,128,128]{3,2,1,0:T(8,128)} %dist_far.1, f32[19,2,128,128]{3,2,1,0:T(8,128)} %cot_far.1, s32[2,128,128]{2,1,0:T(8,128)} %mask.1, f32[640,128]{1,0:T(8,128)} %get-tuple-element.23.cols, f32[640,128]{1,0:T(8,128)} %get-tuple-element.26.edge, ...), custom_call_target="tpu_custom_call" | custom-call | tf_op jit(solution)/shard_map/pallas_call | solution.py:392
  52.3 21.1 %all_to_all.17 = f32[128,1,48]{2,1,0:T(1,128)S(1)} all-to-all(f32[128,1,48]{2,1,0:T(1,128)} %bitcast.17), channel_id=1, replica_groups=mesh['gx'=8,'gy'=16] {'gx','gy'}, dimensions={0} | all-to-all | bytes 49152 | tf_op jit(solution)/shard_map/all_to_all | solution.py:429
  73.4 0.2 reduce_sum.9
  73.6 14.5 %all_to_all.18 = f32[128,1,48]{2,1,0:T(1,128)} all-to-all(f32[128,1,48]{2,1,0:T(1,128)S(1)} %tile.2), channel_id=1, replica_groups=mesh['gx'=8,'gy'=16] {'gx','gy'}, dimensions={0} | all-to-all | bytes 49152 | tf_op jit(solution)/shard_map/all_to_all | solution.py:431
  88.1 1.5 %shard_map.114 = (f32[19,128]{1,0:T(8,128)}, f32[1,128]{1,0:T(1,128)}, f32[19,128]{1,0:T(8,128)}, f32[1,19]{1,0:T(1,128)}) custom-call(f32[128,48]{1,0:T(8,128)} %bitcast.16), custom_call_target="tpu_custom_call" | custom-call | tf_op jit(solution)/shard_map/pallas_call | solution.py:444
  (1 shorter events, 0.0 us)
Async XLA Ops:
  4.7 6.3 %collective-permute-start = (bf16[160,128]{1,0:T(8,128)(2,1)}, bf16[160,128]{1,0:T(8,128)(2,1)S(1)}, u32[]{:S(2)}, u32[]{:S(2)}) collective-permute-start(bf16[160,128]{1,0:T(8,128)(2,1)} %get-tuple-element.24), channel_id=1, source_target_pairs={{0,16},{16,32},{32,48},{48,64},{64,80},{80,96},{96,112},{112,0},{1... | collective-permute-start | bytes 122888 | tf_op jit(solution)/shard_map/ppermute | solution.py:455
  6.3 4.8 %collective-permute-start.1 = (bf16[160,128]{1,0:T(8,128)(2,1)}, bf16[160,128]{1,0:T(8,128)(2,1)S(1)}, u32[]{:S(2)}, u32[]{:S(2)}) collective-permute-start(bf16[160,128]{1,0:T(8,128)(2,1)} %get-tuple-element.25), channel_id=1, source_target_pairs={{16,0},{32,16},{48,32},{64,48},{80,64},{96,80},{112,96},{0,112},{1... | collective-permute-start | bytes 122888 | tf_op jit(solution)/shard_map/ppermute | solution.py:456
  11.0 0.6 copy-start.2
  11.0 0.6 copy-start.3
  13.7 7.7 %collective-permute-start.2 = (bf16[160,256]{1,0:T(8,128)(2,1)}, bf16[160,256]{1,0:T(8,128)(2,1)S(1)}, u32[]{:S(2)}, u32[]{:S(2)}) collective-permute-start(bf16[160,256]{1,0:T(8,128)(2,1)} %get-tuple-element.27), channel_id=1, source_target_pairs={{0,1},{1,2},{2,3},{3,4},{4,5},{5,6},{6,7},{7,8},{8,9},{9,10},{10,1... | collective-permute-start | bytes 245768 | tf_op jit(solution)/shard_map/ppermute | solution.py:460
  13.7 7.7 %collective-permute-start.3 = (bf16[160,256]{1,0:T(8,128)(2,1)}, bf16[160,256]{1,0:T(8,128)(2,1)S(1)}, u32[]{:S(2)}, u32[]{:S(2)}) collective-permute-start(bf16[160,256]{1,0:T(8,128)(2,1)} %get-tuple-element.28), channel_id=1, source_target_pairs={{1,0},{2,1},{3,2},{4,3},{5,4},{6,5},{7,6},{8,7},{9,8},{10,9},{11,1... | collective-permute-start | bytes 245768 | tf_op jit(solution)/shard_map/ppermute | solution.py:461
  21.4 0.6 copy-start
  21.4 0.6 copy-start.1

commit v4 on v2

--- a/solution.py
+++ b/solution.py
@@ -14,7 +14,7 @@
 )
 OPP = (0, 2, 1, 4, 3, 6, 5, 8, 7, 10, 9, 12, 11, 14, 13, 16, 15, 18, 17)
 Q = 19
-WIDE = 4
+WIDE = 8
 STEPS = 16 // WIDE
 SIDE = tuple(q for q in range(Q) if VEL[q][1])
 PLACE = {q: i for i, q in enumerate(SIDE)}
@@ -33,13 +33,13 @@
     return [pl.BlockSpec(memory_space=pltpu.VMEM)] * n
 
 
-def weights_kernel(win, wout, bias, bias_out, a_in, a_out, b_out, b_in, bias_rows):
+def weights_kernel(win, wtout, bias, bias_out, a_in, a_out, b_out, b_in, bias_rows):
     TN = (((0,), (0,)), ((), ()))
     rep = jnp.where(iota((Q, 160), 1) // 8 == iota((Q, 160), 0), 1.0, 0.0).astype(bf16)
     rept = jnp.where(iota((160, Q), 0) // 8 == iota((160, Q), 1), 1.0, 0.0).astype(bf16)
     wide_in = lax.dot_general(win[...], rep, TN, preferred_element_type=f32)
-    wide_out = jnp.dot(wout[...], rep, preferred_element_type=f32)
-    tall_out = lax.dot_general(rept, wout[...], NT, preferred_element_type=f32)
+    wide_out = lax.dot_general(wtout[...], rep, TN, preferred_element_type=f32)
+    tall_out = jnp.dot(rept, wtout[...], preferred_element_type=f32)
     tall_in = jnp.dot(rept, win[...], preferred_element_type=f32)
     b = jnp.broadcast_to(bias[...], (128, 128)).T
     b = jnp.concatenate([b, b[:, :32]], axis=1)
@@ -70,7 +70,7 @@
         in_specs=vmem(4),
         out_specs=vmem(5),
         cost_estimate=pl.CostEstimate(flops=10**8, bytes_accessed=2 * 10**6, transcendentals=0),
-    )(weight_in, weight_out, bias_in[None], bias_out[None])
+    )(weight_in, weight_out.T, bias_in[None], bias_out[None])
 
 
 def pack_kernel(dist, cot, mask, up, down, cols, line):
@@ -422,6 +422,7 @@
     from_up = lax.ppermute(send_up, "gx", up)
     from_down = lax.ppermute(send_down, "gx", down)
     nets = make_weights(weight_in, weight_out, bias_in, bias_out)
+    cols, nets = lax.optimization_barrier((cols, nets))
     side_up, side_down, edge, lines = corners(from_up, from_down, cols)
     up, down = neighbours("gy")
     from_left = lax.ppermute(side_up, "gy", up)

time: 87 us -> 86.2 us (level)
    ppermute x1, waiting for transfers between devices: 0.01 us -> 2.33 us  [shards(): from_left = lax.ppermute(side_up, 'gy', up)]
    ppermute x1, waiting for transfers between devices: 2.19 us -> 0.01 us  [shards(): from_up = lax.ppermute(send_up, 'gx', up)]
    unnamed x11 -> x8, local copies, waits for them, and re-layouts: 2 us -> 1.86 us
  transfers between devices with their start and end apart: 13 -> 13, of which waited for: 6 -> 7; matrix products, arithmetic and copies ran while one was open for 1% -> 0% of each run, Pallas kernels for 3% -> 3%
where the time goes in v4:
time: 86.2 us; the launch traced here: 85.2 us
  Pallas kernels  38.1 us (44%)
  starting transfers between devices  23.4 us (27%)
  blocking collectives  9.77 us (11%)
  waiting for transfers between devices  8.98 us (10%)
  local copies, waits for them, and re-layouts  3.5 us (4%)
    pallas_call x1, Pallas kernels, main_call(): pl.pallas_call(main_kernel, out_shape=[jax.ShapeDtypeStruct((Q, 2, 128, 1...  29.7 us
    ppermute x9, starting transfers between devices, from_partner(): return lax.ppermute(values, ('gx', 'gy'), pairs)  13.8 us
    all_to_all x1, blocking collectives, summed(): lax.all_to_all(copies, 'gx', 0, 0, tiled=True, axis_index_groups=groups)  9.77 us
    ppermute x9, waiting for transfers between devices, from_partner(): return lax.ppermute(values, ('gx', 'gy'), pairs)  6.6 us
    ppermute x1, starting transfers between devices, shards(): from_right = lax.ppermute(side_down, 'gy', down)  5.46 us
    pallas_call x1, Pallas kernels, pack(): pl.pallas_call(pack_kernel, out_shape=[jax.ShapeDtypeStruct((160, 128), b...  4.05 us
    ppermute x1, starting transfers between devices, shards(): from_down = lax.ppermute(send_down, 'gx', down)  2.56 us
    ppermute x1, waiting for transfers between devices, shards(): from_left = lax.ppermute(side_up, 'gy', up)  2.33 us
  transfers between devices with their start and end apart: 13, of which 7 were waited for; matrix products, arithmetic and copies ran while one was open for 0% of the time, Pallas kernels for 3%

profile of v4, /device:TPU:0, one launch (start us, length us, event | category | flops | bytes accessed | tf_op | source)
XLA Modules:
  0.0 85.2 jit_solution(13270597825671370346)
XLA Ops:
  0.6 4.0 %shard_map.110 = (bf16[160,128]{1,0:T(8,128)(2,1)}, bf16[160,128]{1,0:T(8,128)(2,1)}, f32[640,128]{1,0:T(8,128)}) custom-call(f32[4864,128]{1,0:T(8,128)} %bitcast.16, f32[4864,128]{1,0:T(8,128)} %bitcast.17, s32[256,128]{1,0:T(8,128)} %bitcast.18), custom_call_target="tpu_custom_call" | custom-call | tf_op jit(solution)/shard_map/pallas_call | solution.py:105
  4.7 1.6 %collective-permute-start = (bf16[160,128]{1,0:T(8,128)(2,1)}, bf16[160,128]{1,0:T(8,128)(2,1)S(1)}, u32[]{:S(2)}, u32[]{:S(2)}) collective-permute-start(bf16[160,128]{1,0:T(8,128)(2,1)} %get-tuple-element.32), channel_id=1, source_target_pairs={{0,16},{16,32},{32,48},{48,64},{64,80},{80,96},{96,112},{112,0},{1... | collective-permute-start | bytes 122888 | tf_op jit(solution)/shard_map/ppermute | solution.py:422
  6.3 2.6 %collective-permute-start.1 = (bf16[160,128]{1,0:T(8,128)(2,1)}, bf16[160,128]{1,0:T(8,128)(2,1)S(1)}, u32[]{:S(2)}, u32[]{:S(2)}) collective-permute-start(bf16[160,128]{1,0:T(8,128)(2,1)} %get-tuple-element.33), channel_id=1, source_target_pairs={{16,0},{32,16},{48,32},{64,48},{80,64},{96,80},{112,96},{0,112},{1... | collective-permute-start | bytes 122888 | tf_op jit(solution)/shard_map/ppermute | solution.py:423
  8.8 2.3 %shard_map.111 = (bf16[1024,160]{1,0:T(8,128)(2,1)}, bf16[1024,160]{1,0:T(8,128)(2,1)}, bf16[160,1024]{1,0:T(8,128)(2,1)}, bf16[160,1024]{1,0:T(8,128)(2,1)}, f32[152,128]{1,0:T(8,128)}) custom-call(bf16[19,128]{1,0:T(8,128)(2,1)} %win.1, bf16[19,128]{1,0:T(8,128)(2,1)} %bitcast.19, f32[1,128]{1,0:T(1,128)} %bitcast.20, f32[1,19]{1,0:T(1,128)} %bitcast.21), custom_call_target="tpu_custom_call" | custom-call | flops 100000000 | bytes 2000000 | tf_op jit(solution)/shard_map/pallas_call | solution.py:65
  11.1 0.0 collective-permute-done.from_up
  11.1 0.6 copy-done.2
  11.7 0.6 copy-done.3
  12.4 2.1 %shard_map.112 = (bf16[160,256]{1,0:T(8,128)(2,1)}, bf16[160,256]{1,0:T(8,128)(2,1)}, f32[640,128]{1,0:T(8,128)}, f32[640,128]{1,0:T(8,128)}) custom-call(bf16[160,128]{1,0:T(8,128)(2,1)} %copy-done.2, bf16[160,128]{1,0:T(8,128)(2,1)} %copy-done.3, f32[640,128]{1,0:T(8,128)} %get-tuple-element.31.cols), custom_call_target="tpu_custom_call" | custom-call | tf_op jit(solution)/shard_map/pallas_call | solution.py:133
  14.4 5.5 %collective-permute-start.3 = (bf16[160,256]{1,0:T(8,128)(2,1)}, bf16[160,256]{1,0:T(8,128)(2,1)S(1)}, u32[]{:S(2)}, u32[]{:S(2)}) collective-permute-start(bf16[160,256]{1,0:T(8,128)(2,1)} %get-tuple-element.36), channel_id=1, source_target_pairs={{1,0},{2,1},{3,2},{4,3},{5,4},{6,5},{7,6},{8,7},{9,8},{10,9},{11,1... | collective-permute-start | bytes 245768 | tf_op jit(solution)/shard_map/ppermute | solution.py:429
  19.9 2.3 %collective-permute-done.2.from_left = bf16[160,256]{1,0:T(8,128)(2,1)S(1)} collective-permute-done((bf16[160,256]{1,0:T(8,128)(2,1)}, bf16[160,256]{1,0:T(8,128)(2,1)S(1)}, u32[]{:S(2)}, u32[]{:S(2)}) %collective-permute-start.2) | collective-permute-done | bytes 81952 | tf_op jit(solution)/shard_map/ppermute | solution.py:428
  22.2 0.0 collective-permute-done.3.from_right
  22.3 0.6 copy-done
  22.8 0.0 copy-done.1
  22.9 29.7 %shard_map.113 = (f32[19,2,128,128]{3,2,1,0:T(8,128)}, f32[48,128]{1,0:T(8,128)}) custom-call(f32[19,2,128,128]{3,2,1,0:T(8,128)} %dist.1, f32[19,2,128,128]{3,2,1,0:T(8,128)} %cot.1, s32[2,128,128]{2,1,0:T(8,128)} %mask.1, f32[640,128]{1,0:T(8,128)} %get-tuple-element.31.cols, f32[640,128]{1,0:T(8,128)} %get-tuple-element.34.edge, ...), custom_call_target="tpu_custom_call" | custom-call | tf_op jit(solution)/shard_map/pallas_call | solution.py:360
  52.6 3.6 %collective-permute-start.10 = (f32[48,128]{1,0:T(8,128)}, f32[48,128]{1,0:T(8,128)S(1)}, u32[]{:S(2)}, u32[]{:S(2)}) collective-permute-start(f32[48,128]{1,0:T(8,128)} %get-tuple-element.44), channel_id=1, source_target_pairs={{0,19},{1,18},{2,17},{3,16},{4,23},{5,22},{6,21},{7,20},{8,27},{9,... | collective-permute-start | bytes 73736 | tf_op jit(solution)/shard_map/ppermute | solution.py:397
  56.1 0.4 collective-permute-start.9
  56.6 2.8 %collective-permute-start.7 = (f32[48,128]{1,0:T(8,128)}, f32[48,128]{1,0:T(8,128)S(1)}, u32[]{:S(2)}, u32[]{:S(2)}) collective-permute-start(f32[48,128]{1,0:T(8,128)} %get-tuple-element.44), channel_id=1, source_target_pairs={{0,2},{1,3},{2,0},{3,1},{4,6},{5,7},{6,4},{7,5},{8,10},{9,11},{10,... | collective-permute-start | bytes 73736 | tf_op jit(solution)/shard_map/ppermute | solution.py:397
  59.4 0.5 collective-permute-start.6
  59.9 1.6 %collective-permute-start.5 = (f32[48,128]{1,0:T(8,128)}, f32[48,128]{1,0:T(8,128)S(1)}, u32[]{:S(2)}, u32[]{:S(2)}) collective-permute-start(f32[48,128]{1,0:T(8,128)} %get-tuple-element.44), channel_id=1, source_target_pairs={{0,16},{1,17},{2,18},{3,19},{4,20},{5,21},{6,22},{7,23},{8,24},{9,... | collective-permute-start | bytes 73736 | tf_op jit(solution)/shard_map/ppermute | solution.py:397
  61.6 0.5 collective-permute-done.9
  62.1 0.1 collective-permute-done.7
  62.2 0.7 collective-permute-done.6
  62.9 1.1 %collective-permute-done.5 = f32[48,128]{1,0:T(8,128)S(1)} collective-permute-done((f32[48,128]{1,0:T(8,128)}, f32[48,128]{1,0:T(8,128)S(1)}, u32[]{:S(2)}, u32[]{:S(2)}) %collective-permute-start.5) | collective-permute-done | bytes 24608 | tf_op jit(solution)/shard_map/ppermute | solution.py:397
  64.0 0.8 add_add_fusion
  64.8 9.8 %all_to_all.5 = f32[4,48,128]{2,1,0:T(8,128)S(1)} all-to-all(f32[4,48,128]{2,1,0:T(8,128)S(1)} %broadcast_in_dim.14), channel_id=1, replica_groups={{0,32,64,96},{16,48,80,112},{1,33,65,97},{17,49,81,113},{2,34,66,98},{1..., dimensions={0} | all-to-all | bytes 196608 | tf_op jit(solution)/shard_map/all_to_all | solution.py:412
  74.5 2.0 %collective-permute-start.11 = (f32[48,128]{1,0:T(8,128)S(1)}, f32[48,128]{1,0:T(8,128)S(1)}, u32[]{:S(2)}, u32[]{:S(2)}) collective-permute-start(f32[48,128]{1,0:T(8,128)S(1)} %fusion.1), channel_id=1, source_target_pairs={{0,4},{1,5},{2,6},{3,7},{4,0},{5,1},{6,2},{7,3},{8,12},{9,13},{10,... | collective-permute-start | bytes 73736 | tf_op jit(solution)/shard_map/ppermute | solution.py:397
  76.5 1.9 %collective-permute-done.11 = f32[48,128]{1,0:T(8,128)S(1)} collective-permute-done((f32[48,128]{1,0:T(8,128)S(1)}, f32[48,128]{1,0:T(8,128)S(1)}, u32[]{:S(2)}, u32[]{:S(2)}) %collective-permute-start.11) | collective-permute-done | bytes 24608 | tf_op jit(solution)/shard_map/ppermute | solution.py:397
  78.5 2.9 %collective-permute-start.12 = (f32[48,128]{1,0:T(8,128)S(1)}, f32[48,128]{1,0:T(8,128)S(1)}, u32[]{:S(2)}, u32[]{:S(2)}) collective-permute-start(f32[48,128]{1,0:T(8,128)S(1)} %fusion.2), channel_id=1, source_target_pairs={{0,12},{1,13},{2,14},{3,15},{4,8},{5,9},{6,10},{7,11},{8,4},{9,5},... | collective-permute-start | bytes 73736 | tf_op jit(solution)/shard_map/ppermute | solution.py:397
  81.3 2.3 %collective-permute-done.12 = f32[48,128]{1,0:T(8,128)S(1)} collective-permute-done((f32[48,128]{1,0:T(8,128)S(1)}, f32[48,128]{1,0:T(8,128)S(1)}, u32[]{:S(2)}, u32[]{:S(2)}) %collective-permute-start.12) | collective-permute-done | bytes 24608 | tf_op jit(solution)/shard_map/ppermute | solution.py:397
  83.6 0.5 slice_bitcast_fusion.2
  84.1 0.5 slice_bitcast_fusion.1
  84.6 0.6 slice_bitcast_fusion
  (15 shorter events, 0.1 us)
Async XLA Ops:
  4.7 6.4 %collective-permute-start = (bf16[160,128]{1,0:T(8,128)(2,1)}, bf16[160,128]{1,0:T(8,128)(2,1)S(1)}, u32[]{:S(2)}, u32[]{:S(2)}) collective-permute-start(bf16[160,128]{1,0:T(8,128)(2,1)} %get-tuple-element.32), channel_id=1, source_target_pairs={{0,16},{16,32},{32,48},{48,64},{64,80},{80,96},{96,112},{112,0},{1... | collective-permute-start | bytes 122888 | tf_op jit(solution)/shard_map/ppermute | solution.py:422
  6.3 4.9 %collective-permute-start.1 = (bf16[160,128]{1,0:T(8,128)(2,1)}, bf16[160,128]{1,0:T(8,128)(2,1)S(1)}, u32[]{:S(2)}, u32[]{:S(2)}) collective-permute-start(bf16[160,128]{1,0:T(8,128)(2,1)} %get-tuple-element.33), channel_id=1, source_target_pairs={{16,0},{32,16},{48,32},{64,48},{80,64},{96,80},{112,96},{0,112},{1... | collective-permute-start | bytes 122888 | tf_op jit(solution)/shard_map/ppermute | solution.py:423
  11.1 0.6 copy-start.2
  11.7 0.6 copy-start.3
  14.4 7.8 %collective-permute-start.2 = (bf16[160,256]{1,0:T(8,128)(2,1)}, bf16[160,256]{1,0:T(8,128)(2,1)S(1)}, u32[]{:S(2)}, u32[]{:S(2)}) collective-permute-start(bf16[160,256]{1,0:T(8,128)(2,1)} %get-tuple-element.35), channel_id=1, source_target_pairs={{0,1},{1,2},{2,3},{3,4},{4,5},{5,6},{6,7},{7,8},{8,9},{9,10},{10,1... | collective-permute-start | bytes 245768 | tf_op jit(solution)/shard_map/ppermute | solution.py:428
  14.4 7.8 %collective-permute-start.3 = (bf16[160,256]{1,0:T(8,128)(2,1)}, bf16[160,256]{1,0:T(8,128)(2,1)S(1)}, u32[]{:S(2)}, u32[]{:S(2)}) collective-permute-start(bf16[160,256]{1,0:T(8,128)(2,1)} %get-tuple-element.36), channel_id=1, source_target_pairs={{1,0},{2,1},{3,2},{4,3},{5,4},{6,5},{7,6},{8,7},{9,8},{10,9},{11,1... | collective-permute-start | bytes 245768 | tf_op jit(solution)/shard_map/ppermute | solution.py:429
  22.2 0.6 copy-start
  22.3 0.6 copy-start.1
  52.6 7.4 %collective-permute-start.10 = (f32[48,128]{1,0:T(8,128)}, f32[48,128]{1,0:T(8,128)S(1)}, u32[]{:S(2)}, u32[]{:S(2)}) collective-permute-start(f32[48,128]{1,0:T(8,128)} %get-tuple-element.44), channel_id=1, source_target_pairs={{0,19},{1,18},{2,17},{3,16},{4,23},{5,22},{6,21},{7,20},{8,27},{9,... | collective-permute-start | bytes 73736 | tf_op jit(solution)/shard_map/ppermute | solution.py:397
  56.1 6.0 %collective-permute-start.9 = (f32[48,128]{1,0:T(8,128)}, f32[48,128]{1,0:T(8,128)S(1)}, u32[]{:S(2)}, u32[]{:S(2)}) collective-permute-start(f32[48,128]{1,0:T(8,128)} %get-tuple-element.44), channel_id=1, source_target_pairs={{0,18},{1,19},{2,16},{3,17},{4,22},{5,23},{6,20},{7,21},{8,26},{9,... | collective-permute-start | bytes 73736 | tf_op jit(solution)/shard_map/ppermute | solution.py:397
  56.6 5.5 %collective-permute-start.8 = (f32[48,128]{1,0:T(8,128)}, f32[48,128]{1,0:T(8,128)S(1)}, u32[]{:S(2)}, u32[]{:S(2)}) collective-permute-start(f32[48,128]{1,0:T(8,128)} %get-tuple-element.44), channel_id=1, source_target_pairs={{0,3},{1,2},{2,1},{3,0},{4,7},{5,6},{6,5},{7,4},{8,11},{9,10},{10,... | collective-permute-start | bytes 73736 | tf_op jit(solution)/shard_map/ppermute | solution.py:397
  56.6 5.6 %collective-permute-start.7 = (f32[48,128]{1,0:T(8,128)}, f32[48,128]{1,0:T(8,128)S(1)}, u32[]{:S(2)}, u32[]{:S(2)}) collective-permute-start(f32[48,128]{1,0:T(8,128)} %get-tuple-element.44), channel_id=1, source_target_pairs={{0,2},{1,3},{2,0},{3,1},{4,6},{5,7},{6,4},{7,5},{8,10},{9,11},{10,... | collective-permute-start | bytes 73736 | tf_op jit(solution)/shard_map/ppermute | solution.py:397
  59.4 3.5 %collective-permute-start.6 = (f32[48,128]{1,0:T(8,128)}, f32[48,128]{1,0:T(8,128)S(1)}, u32[]{:S(2)}, u32[]{:S(2)}) collective-permute-start(f32[48,128]{1,0:T(8,128)} %get-tuple-element.44), channel_id=1, source_target_pairs={{0,17},{1,16},{2,19},{3,18},{4,21},{5,20},{6,23},{7,22},{8,25},{9,... | collective-permute-start | bytes 73736 | tf_op jit(solution)/shard_map/ppermute | solution.py:397
  59.9 4.0 %collective-permute-start.5 = (f32[48,128]{1,0:T(8,128)}, f32[48,128]{1,0:T(8,128)S(1)}, u32[]{:S(2)}, u32[]{:S(2)}) collective-permute-start(f32[48,128]{1,0:T(8,128)} %get-tuple-element.44), channel_id=1, source_target_pairs={{0,16},{1,17},{2,18},{3,19},{4,20},{5,21},{6,22},{7,23},{8,24},{9,... | collective-permute-start | bytes 73736 | tf_op jit(solution)/shard_map/ppermute | solution.py:397
  62.1 1.9 %collective-permute-start.4 = (f32[48,128]{1,0:T(8,128)}, f32[48,128]{1,0:T(8,128)S(1)}, u32[]{:S(2)}, u32[]{:S(2)}) collective-permute-start(f32[48,128]{1,0:T(8,128)} %get-tuple-element.44), channel_id=1, source_target_pairs={{0,1},{1,0},{2,3},{3,2},{4,5},{5,4},{6,7},{7,6},{8,9},{9,8},{10,11... | collective-permute-start | bytes 73736 | tf_op jit(solution)/shard_map/ppermute | solution.py:397
  74.5 3.9 %collective-permute-start.11 = (f32[48,128]{1,0:T(8,128)S(1)}, f32[48,128]{1,0:T(8,128)S(1)}, u32[]{:S(2)}, u32[]{:S(2)}) collective-permute-start(f32[48,128]{1,0:T(8,128)S(1)} %fusion.1), channel_id=1, source_target_pairs={{0,4},{1,5},{2,6},{3,7},{4,0},{5,1},{6,2},{7,3},{8,12},{9,13},{10,... | collective-permute-start | bytes 73736 | tf_op jit(solution)/shard_map/ppermute | solution.py:397
  78.5 5.1 %collective-permute-start.12 = (f32[48,128]{1,0:T(8,128)S(1)}, f32[48,128]{1,0:T(8,128)S(1)}, u32[]{:S(2)}, u32[]{:S(2)}) collective-permute-start(f32[48,128]{1,0:T(8,128)S(1)} %fusion.2), channel_id=1, source_target_pairs={{0,12},{1,13},{2,14},{3,15},{4,8},{5,9},{6,10},{7,11},{8,4},{9,5},... | collective-permute-start | bytes 73736 | tf_op jit(solution)/shard_map/ppermute | solution.py:397

commit v5 on v4

--- a/solution.py
+++ b/solution.py
@@ -387,33 +387,22 @@
 
 def summed(values):
     nx, ny = lax.axis_size("gx"), lax.axis_size("gy")
-
-    def from_partner(values, partner):
-        pairs = []
-        for x in range(nx):
-            for y in range(ny):
-                px, py = partner(x, y)
-                pairs.append((x * ny + y, px * ny + py))
-        return lax.ppermute(values, ("gx", "gy"), pairs)
-
-    if (nx, ny) != (8, 16):
-        for k in range(nx.bit_length() - 1):
-            values = values + from_partner(values, lambda x, y: (x ^ (1 << k), y))
-        for k in range(ny.bit_length() - 1):
-            values = values + from_partner(values, lambda x, y: (x, y ^ (1 << k)))
-        return values
-    got = [values] + [
-        from_partner(values, lambda x, y: (x ^ ((d >> 1) & 1), y ^ (d & 1) ^ (((d >> 2) & 1) << 1))) for d in range(1, 8)
-    ]
-    while len(got) > 1:
-        got = [got[i] + got[i + 1] for i in range(0, len(got), 2)]
-    copies = jnp.broadcast_to(got[0][None], (4,) + values.shape)
-    groups = [[2 * y + low for y in range(4)] for low in range(2)]
-    values = lax.all_to_all(copies, "gx", 0, 0, tiled=True, axis_index_groups=groups)
-    values = (values[0] + values[1]) + (values[2] + values[3])
-    other = (3, 2, 1, 0)
-    values = values + from_partner(values, lambda x, y: (x, y ^ 4))
-    return values + from_partner(values, lambda x, y: (x, other[y // 4] * 4 + y % 4))
+    if (nx, ny) == (8, 16):
+        stages = (((0, 1), (1, 0), (0, 2)), ((2, 0), (4, 0)), ((0, 4), (0, 8)))
+    else:
+        stages = [((1 << k, 0),) for k in range(nx.bit_length() - 1)]
+        stages += [((0, 1 << k),) for k in range(ny.bit_length() - 1)]
+    for bits in stages:
+        got = [values]
+        for d in range(1, 1 << len(bits)):
+            fx = sum(bx for k, (bx, _) in enumerate(bits) if d >> k & 1)
+            fy = sum(by for k, (_, by) in enumerate(bits) if d >> k & 1)
+            pairs = [(x * ny + y, (x ^ fx) * ny + (y ^ fy)) for x in range(nx) for y in range(ny)]
+            got.append(lax.ppermute(values, ("gx", "gy"), pairs))
+        while len(got) > 1:
+            got = [got[i] + got[i + 1] for i in range(0, len(got), 2)]
+        values = got[0]
+    return values
 
 
 def shards(dist, cot, mask, weight_in, bias_in, weight_out, bias_out):

time: 86.2 us -> 83.6 us (0.970)
  blocking collectives: 9.77 us -> 0 us
  waiting for transfers between devices: 8.98 us -> 12.8 us
  starting transfers between devices: 23.4 us -> 26.9 us
    all_to_all x1 -> x0, blocking collectives: 9.77 us -> none  [summed(): lax.all_to_all(copies, 'gx', 0, 0, tiled=True, axis_index_groups=groups)]
    ppermute x9 -> x13, waiting for transfers between devices: 6.6 us -> 10.5 us  [summed(): got.append(lax.ppermute(values, ('gx', 'gy'), pairs))]
    ppermute x9 -> x13, starting transfers between devices: 13.8 us -> 17.3 us  [summed(): got.append(lax.ppermute(values, ('gx', 'gy'), pairs))]
  transfers between devices with their start and end apart: 13 -> 17, of which waited for: 7 -> 9; matrix products, arithmetic and copies ran while one was open for 0% -> 0% of each run, Pallas kernels for 3% -> 3%
where the time goes in v5:
time: 83.6 us; the launch traced here: 82.8 us
  Pallas kernels  38.1 us (46%)
  starting transfers between devices  26.9 us (32%)
  waiting for transfers between devices  12.8 us (15%)
  local copies, waits for them, and re-layouts  3.48 us (4%)
    pallas_call x1, Pallas kernels, main_call(): pl.pallas_call(main_kernel, out_shape=[jax.ShapeDtypeStruct((Q, 2, 128, 1...  29.7 us
    ppermute x13, starting transfers between devices, summed(): got.append(lax.ppermute(values, ('gx', 'gy'), pairs))  17.3 us
    ppermute x13, waiting for transfers between devices, summed(): got.append(lax.ppermute(values, ('gx', 'gy'), pairs))  10.5 us
    ppermute x1, starting transfers between devices, shards(): from_right = lax.ppermute(side_down, 'gy', down)  5.46 us
    pallas_call x1, Pallas kernels, pack(): pl.pallas_call(pack_kernel, out_shape=[jax.ShapeDtypeStruct((160, 128), b...  4.05 us
    ppermute x1, starting transfers between devices, shards(): from_down = lax.ppermute(send_down, 'gx', down)  2.56 us
    ppermute x1, waiting for transfers between devices, shards(): from_left = lax.ppermute(side_up, 'gy', up)  2.33 us
    pallas_call x1, Pallas kernels, make_weights(): pl.pallas_call(weights_kernel, out_shape=[jax.ShapeDtypeStruct((1024, 160...  2.31 us
  transfers between devices with their start and end apart: 17, of which 9 were waited for; matrix products, arithmetic and copies ran while one was open for 0% of the time, Pallas kernels for 3%

profile of v5, /device:TPU:0, one launch (start us, length us, event | category | flops | bytes accessed | tf_op | source)
XLA Modules:
  0.0 82.8 jit_solution(5644824814684656606)
XLA Ops:
  0.6 4.1 %shard_map.110 = (bf16[160,128]{1,0:T(8,128)(2,1)}, bf16[160,128]{1,0:T(8,128)(2,1)}, f32[640,128]{1,0:T(8,128)}) custom-call(f32[4864,128]{1,0:T(8,128)} %bitcast.12, f32[4864,128]{1,0:T(8,128)} %bitcast.13, s32[256,128]{1,0:T(8,128)} %bitcast.14), custom_call_target="tpu_custom_call" | custom-call | tf_op jit(solution)/shard_map/pallas_call | solution.py:105
  4.7 1.6 %collective-permute-start = (bf16[160,128]{1,0:T(8,128)(2,1)}, bf16[160,128]{1,0:T(8,128)(2,1)S(1)}, u32[]{:S(2)}, u32[]{:S(2)}) collective-permute-start(bf16[160,128]{1,0:T(8,128)(2,1)} %get-tuple-element.32), channel_id=1, source_target_pairs={{0,16},{16,32},{32,48},{48,64},{64,80},{80,96},{96,112},{112,0},{1... | collective-permute-start | bytes 122888 | tf_op jit(solution)/shard_map/ppermute | solution.py:411
  6.3 2.6 %collective-permute-start.1 = (bf16[160,128]{1,0:T(8,128)(2,1)}, bf16[160,128]{1,0:T(8,128)(2,1)S(1)}, u32[]{:S(2)}, u32[]{:S(2)}) collective-permute-start(bf16[160,128]{1,0:T(8,128)(2,1)} %get-tuple-element.33), channel_id=1, source_target_pairs={{16,0},{32,16},{48,32},{64,48},{80,64},{96,80},{112,96},{0,112},{1... | collective-permute-start | bytes 122888 | tf_op jit(solution)/shard_map/ppermute | solution.py:412
  8.8 2.3 %shard_map.111 = (bf16[1024,160]{1,0:T(8,128)(2,1)}, bf16[1024,160]{1,0:T(8,128)(2,1)}, bf16[160,1024]{1,0:T(8,128)(2,1)}, bf16[160,1024]{1,0:T(8,128)(2,1)}, f32[152,128]{1,0:T(8,128)}) custom-call(bf16[19,128]{1,0:T(8,128)(2,1)} %win.1, bf16[19,128]{1,0:T(8,128)(2,1)} %bitcast.15, f32[1,128]{1,0:T(1,128)} %bitcast.16, f32[1,19]{1,0:T(1,128)} %bitcast.17), custom_call_target="tpu_custom_call" | custom-call | flops 100000000 | bytes 2000000 | tf_op jit(solution)/shard_map/pallas_call | solution.py:65
  11.1 0.6 copy-done.2
  11.8 0.6 copy-done.3
  12.4 2.1 %shard_map.112 = (bf16[160,256]{1,0:T(8,128)(2,1)}, bf16[160,256]{1,0:T(8,128)(2,1)}, f32[640,128]{1,0:T(8,128)}, f32[640,128]{1,0:T(8,128)}) custom-call(bf16[160,128]{1,0:T(8,128)(2,1)} %copy-done.2, bf16[160,128]{1,0:T(8,128)(2,1)} %copy-done.3, f32[640,128]{1,0:T(8,128)} %get-tuple-element.31.cols), custom_call_target="tpu_custom_call" | custom-call | tf_op jit(solution)/shard_map/pallas_call | solution.py:133
  14.4 5.5 %collective-permute-start.3 = (bf16[160,256]{1,0:T(8,128)(2,1)}, bf16[160,256]{1,0:T(8,128)(2,1)S(1)}, u32[]{:S(2)}, u32[]{:S(2)}) collective-permute-start(bf16[160,256]{1,0:T(8,128)(2,1)} %get-tuple-element.36), channel_id=1, source_target_pairs={{1,0},{2,1},{3,2},{4,3},{5,4},{6,5},{7,6},{8,7},{9,8},{10,9},{11,1... | collective-permute-start | bytes 245768 | tf_op jit(solution)/shard_map/ppermute | solution.py:418
  19.9 2.3 %collective-permute-done.2.from_left = bf16[160,256]{1,0:T(8,128)(2,1)S(1)} collective-permute-done((bf16[160,256]{1,0:T(8,128)(2,1)}, bf16[160,256]{1,0:T(8,128)(2,1)S(1)}, u32[]{:S(2)}, u32[]{:S(2)}) %collective-permute-start.2) | collective-permute-done | bytes 81952 | tf_op jit(solution)/shard_map/ppermute | solution.py:417
  22.3 0.6 copy-done
  22.9 29.7 %shard_map.113 = (f32[19,2,128,128]{3,2,1,0:T(8,128)}, f32[48,128]{1,0:T(8,128)}) custom-call(f32[19,2,128,128]{3,2,1,0:T(8,128)} %dist.1, f32[19,2,128,128]{3,2,1,0:T(8,128)} %cot.1, s32[2,128,128]{2,1,0:T(8,128)} %mask.1, f32[640,128]{1,0:T(8,128)} %get-tuple-element.31.cols, f32[640,128]{1,0:T(8,128)} %get-tuple-element.34.edge, ...), custom_call_target="tpu_custom_call" | custom-call | tf_op jit(solution)/shard_map/pallas_call | solution.py:360
  52.6 3.5 %collective-permute-start.10 = (f32[48,128]{1,0:T(8,128)}, f32[48,128]{1,0:T(8,128)S(1)}, u32[]{:S(2)}, u32[]{:S(2)}) collective-permute-start(f32[48,128]{1,0:T(8,128)} %get-tuple-element.44), channel_id=1, source_target_pairs={{0,19},{1,18},{2,17},{3,16},{4,23},{5,22},{6,21},{7,20},{8,27},{9,... | collective-permute-start | bytes 73736 | tf_op jit(solution)/shard_map/ppermute | solution.py:401
  56.1 0.4 collective-permute-start.9
  56.6 2.8 %collective-permute-start.7 = (f32[48,128]{1,0:T(8,128)}, f32[48,128]{1,0:T(8,128)S(1)}, u32[]{:S(2)}, u32[]{:S(2)}) collective-permute-start(f32[48,128]{1,0:T(8,128)} %get-tuple-element.44), channel_id=1, source_target_pairs={{0,2},{1,3},{2,0},{3,1},{4,6},{5,7},{6,4},{7,5},{8,10},{9,11},{10,... | collective-permute-start | bytes 73736 | tf_op jit(solution)/shard_map/ppermute | solution.py:401
  59.4 0.5 collective-permute-start.6
  60.0 1.6 %collective-permute-start.5 = (f32[48,128]{1,0:T(8,128)}, f32[48,128]{1,0:T(8,128)S(1)}, u32[]{:S(2)}, u32[]{:S(2)}) collective-permute-start(f32[48,128]{1,0:T(8,128)} %get-tuple-element.44), channel_id=1, source_target_pairs={{0,16},{1,17},{2,18},{3,19},{4,20},{5,21},{6,22},{7,23},{8,24},{9,... | collective-permute-start | bytes 73736 | tf_op jit(solution)/shard_map/ppermute | solution.py:401
  61.6 0.5 collective-permute-done.9
  62.2 0.7 collective-permute-done.6
  62.9 1.1 %collective-permute-done.5 = f32[48,128]{1,0:T(8,128)S(1)} collective-permute-done((f32[48,128]{1,0:T(8,128)}, f32[48,128]{1,0:T(8,128)S(1)}, u32[]{:S(2)}, u32[]{:S(2)}) %collective-permute-start.5) | collective-permute-done | bytes 24608 | tf_op jit(solution)/shard_map/ppermute | solution.py:401
  64.0 0.8 add_add_fusion.1
  64.8 3.0 %collective-permute-start.13 = (f32[48,128]{1,0:T(8,128)S(1)}, f32[48,128]{1,0:T(8,128)S(1)}, u32[]{:S(2)}, u32[]{:S(2)}) collective-permute-start(f32[48,128]{1,0:T(8,128)S(1)} %add_add_fusion.1), channel_id=1, source_target_pairs={{0,96},{1,97},{2,98},{3,99},{4,100},{5,101},{6,102},{7,103},{8,104... | collective-permute-start | bytes 73736 | tf_op jit(solution)/shard_map/ppermute | solution.py:401
  67.7 0.8 collective-permute-start.12
  68.5 0.4 collective-permute-start.11
  68.9 0.9 %collective-permute-done.13 = f32[48,128]{1,0:T(8,128)S(1)} collective-permute-done((f32[48,128]{1,0:T(8,128)S(1)}, f32[48,128]{1,0:T(8,128)S(1)}, u32[]{:S(2)}, u32[]{:S(2)}) %collective-permute-start.13) | collective-permute-done | bytes 24608 | tf_op jit(solution)/shard_map/ppermute | solution.py:401
  69.9 3.2 %collective-permute-done.12 = f32[48,128]{1,0:T(8,128)S(1)} collective-permute-done((f32[48,128]{1,0:T(8,128)S(1)}, f32[48,128]{1,0:T(8,128)S(1)}, u32[]{:S(2)}, u32[]{:S(2)}) %collective-permute-start.12) | collective-permute-done | bytes 24608 | tf_op jit(solution)/shard_map/ppermute | solution.py:401
  73.1 2.8 %collective-permute-start.16 = (f32[48,128]{1,0:T(8,128)S(1)}, f32[48,128]{1,0:T(8,128)S(1)}, u32[]{:S(2)}, u32[]{:S(2)}) collective-permute-start(f32[48,128]{1,0:T(8,128)S(1)} %add_add_fusion), channel_id=1, source_target_pairs={{0,12},{1,13},{2,14},{3,15},{4,8},{5,9},{6,10},{7,11},{8,4},{9,5},... | collective-permute-start | bytes 73736 | tf_op jit(solution)/shard_map/ppermute | solution.py:401
  75.8 1.3 %collective-permute-start.15 = (f32[48,128]{1,0:T(8,128)S(1)}, f32[48,128]{1,0:T(8,128)S(1)}, u32[]{:S(2)}, u32[]{:S(2)}) collective-permute-start(f32[48,128]{1,0:T(8,128)S(1)} %add_add_fusion), channel_id=1, source_target_pairs={{0,8},{1,9},{2,10},{3,11},{4,12},{5,13},{6,14},{7,15},{8,0},{9,1},... | collective-permute-start | bytes 73736 | tf_op jit(solution)/shard_map/ppermute | solution.py:401
  77.2 1.0 %collective-permute-done.16 = f32[48,128]{1,0:T(8,128)S(1)} collective-permute-done((f32[48,128]{1,0:T(8,128)S(1)}, f32[48,128]{1,0:T(8,128)S(1)}, u32[]{:S(2)}, u32[]{:S(2)}) %collective-permute-start.16) | collective-permute-done | bytes 24608 | tf_op jit(solution)/shard_map/ppermute | solution.py:401
  78.3 2.9 %collective-permute-done.15 = f32[48,128]{1,0:T(8,128)S(1)} collective-permute-done((f32[48,128]{1,0:T(8,128)S(1)}, f32[48,128]{1,0:T(8,128)S(1)}, u32[]{:S(2)}, u32[]{:S(2)}) %collective-permute-start.15) | collective-permute-done | bytes 24608 | tf_op jit(solution)/shard_map/ppermute | solution.py:401
  81.2 0.5 slice_bitcast_fusion.2
  81.7 0.5 slice_bitcast_fusion.1
  82.2 0.6 slice_bitcast_fusion
  (20 shorter events, 0.4 us)
Async XLA Ops:
  4.7 6.4 %collective-permute-start = (bf16[160,128]{1,0:T(8,128)(2,1)}, bf16[160,128]{1,0:T(8,128)(2,1)S(1)}, u32[]{:S(2)}, u32[]{:S(2)}) collective-permute-start(bf16[160,128]{1,0:T(8,128)(2,1)} %get-tuple-element.32), channel_id=1, source_target_pairs={{0,16},{16,32},{32,48},{48,64},{64,80},{80,96},{96,112},{112,0},{1... | collective-permute-start | bytes 122888 | tf_op jit(solution)/shard_map/ppermute | solution.py:411
  6.3 4.9 %collective-permute-start.1 = (bf16[160,128]{1,0:T(8,128)(2,1)}, bf16[160,128]{1,0:T(8,128)(2,1)S(1)}, u32[]{:S(2)}, u32[]{:S(2)}) collective-permute-start(bf16[160,128]{1,0:T(8,128)(2,1)} %get-tuple-element.33), channel_id=1, source_target_pairs={{16,0},{32,16},{48,32},{64,48},{80,64},{96,80},{112,96},{0,112},{1... | collective-permute-start | bytes 122888 | tf_op jit(solution)/shard_map/ppermute | solution.py:412
  11.1 0.6 copy-start.2
  11.8 0.6 copy-start.3
  14.4 7.8 %collective-permute-start.2 = (bf16[160,256]{1,0:T(8,128)(2,1)}, bf16[160,256]{1,0:T(8,128)(2,1)S(1)}, u32[]{:S(2)}, u32[]{:S(2)}) collective-permute-start(bf16[160,256]{1,0:T(8,128)(2,1)} %get-tuple-element.35), channel_id=1, source_target_pairs={{0,1},{1,2},{2,3},{3,4},{4,5},{5,6},{6,7},{7,8},{8,9},{9,10},{10,1... | collective-permute-start | bytes 245768 | tf_op jit(solution)/shard_map/ppermute | solution.py:417
  14.4 7.8 %collective-permute-start.3 = (bf16[160,256]{1,0:T(8,128)(2,1)}, bf16[160,256]{1,0:T(8,128)(2,1)S(1)}, u32[]{:S(2)}, u32[]{:S(2)}) collective-permute-start(bf16[160,256]{1,0:T(8,128)(2,1)} %get-tuple-element.36), channel_id=1, source_target_pairs={{1,0},{2,1},{3,2},{4,3},{5,4},{6,5},{7,6},{8,7},{9,8},{10,9},{11,1... | collective-permute-start | bytes 245768 | tf_op jit(solution)/shard_map/ppermute | solution.py:418
  22.2 0.6 copy-start
  22.3 0.6 copy-start.1
  52.6 7.4 %collective-permute-start.10 = (f32[48,128]{1,0:T(8,128)}, f32[48,128]{1,0:T(8,128)S(1)}, u32[]{:S(2)}, u32[]{:S(2)}) collective-permute-start(f32[48,128]{1,0:T(8,128)} %get-tuple-element.44), channel_id=1, source_target_pairs={{0,19},{1,18},{2,17},{3,16},{4,23},{5,22},{6,21},{7,20},{8,27},{9,... | collective-permute-start | bytes 73736 | tf_op jit(solution)/shard_map/ppermute | solution.py:401
  56.1 5.9 %collective-permute-start.9 = (f32[48,128]{1,0:T(8,128)}, f32[48,128]{1,0:T(8,128)S(1)}, u32[]{:S(2)}, u32[]{:S(2)}) collective-permute-start(f32[48,128]{1,0:T(8,128)} %get-tuple-element.44), channel_id=1, source_target_pairs={{0,18},{1,19},{2,16},{3,17},{4,22},{5,23},{6,20},{7,21},{8,26},{9,... | collective-permute-start | bytes 73736 | tf_op jit(solution)/shard_map/ppermute | solution.py:401
  56.6 5.5 %collective-permute-start.8 = (f32[48,128]{1,0:T(8,128)}, f32[48,128]{1,0:T(8,128)S(1)}, u32[]{:S(2)}, u32[]{:S(2)}) collective-permute-start(f32[48,128]{1,0:T(8,128)} %get-tuple-element.44), channel_id=1, source_target_pairs={{0,3},{1,2},{2,1},{3,0},{4,7},{5,6},{6,5},{7,4},{8,11},{9,10},{10,... | collective-permute-start | bytes 73736 | tf_op jit(solution)/shard_map/ppermute | solution.py:401
  56.6 5.6 %collective-permute-start.7 = (f32[48,128]{1,0:T(8,128)}, f32[48,128]{1,0:T(8,128)S(1)}, u32[]{:S(2)}, u32[]{:S(2)}) collective-permute-start(f32[48,128]{1,0:T(8,128)} %get-tuple-element.44), channel_id=1, source_target_pairs={{0,2},{1,3},{2,0},{3,1},{4,6},{5,7},{6,4},{7,5},{8,10},{9,11},{10,... | collective-permute-start | bytes 73736 | tf_op jit(solution)/shard_map/ppermute | solution.py:401
  59.4 3.5 %collective-permute-start.6 = (f32[48,128]{1,0:T(8,128)}, f32[48,128]{1,0:T(8,128)S(1)}, u32[]{:S(2)}, u32[]{:S(2)}) collective-permute-start(f32[48,128]{1,0:T(8,128)} %get-tuple-element.44), channel_id=1, source_target_pairs={{0,17},{1,16},{2,19},{3,18},{4,21},{5,20},{6,23},{7,22},{8,25},{9,... | collective-permute-start | bytes 73736 | tf_op jit(solution)/shard_map/ppermute | solution.py:401
  60.0 4.0 %collective-permute-start.5 = (f32[48,128]{1,0:T(8,128)}, f32[48,128]{1,0:T(8,128)S(1)}, u32[]{:S(2)}, u32[]{:S(2)}) collective-permute-start(f32[48,128]{1,0:T(8,128)} %get-tuple-element.44), channel_id=1, source_target_pairs={{0,16},{1,17},{2,18},{3,19},{4,20},{5,21},{6,22},{7,23},{8,24},{9,... | collective-permute-start | bytes 73736 | tf_op jit(solution)/shard_map/ppermute | solution.py:401
  62.1 1.9 %collective-permute-start.4 = (f32[48,128]{1,0:T(8,128)}, f32[48,128]{1,0:T(8,128)S(1)}, u32[]{:S(2)}, u32[]{:S(2)}) collective-permute-start(f32[48,128]{1,0:T(8,128)} %get-tuple-element.44), channel_id=1, source_target_pairs={{0,1},{1,0},{2,3},{3,2},{4,5},{5,4},{6,7},{7,6},{8,9},{9,8},{10,11... | collective-permute-start | bytes 73736 | tf_op jit(solution)/shard_map/ppermute | solution.py:401
  64.8 5.1 %collective-permute-start.13 = (f32[48,128]{1,0:T(8,128)S(1)}, f32[48,128]{1,0:T(8,128)S(1)}, u32[]{:S(2)}, u32[]{:S(2)}) collective-permute-start(f32[48,128]{1,0:T(8,128)S(1)} %add_add_fusion.1), channel_id=1, source_target_pairs={{0,96},{1,97},{2,98},{3,99},{4,100},{5,101},{6,102},{7,103},{8,104... | collective-permute-start | bytes 73736 | tf_op jit(solution)/shard_map/ppermute | solution.py:401
  67.7 5.3 %collective-permute-start.12 = (f32[48,128]{1,0:T(8,128)S(1)}, f32[48,128]{1,0:T(8,128)S(1)}, u32[]{:S(2)}, u32[]{:S(2)}) collective-permute-start(f32[48,128]{1,0:T(8,128)S(1)} %add_add_fusion.1), channel_id=1, source_target_pairs={{0,64},{1,65},{2,66},{3,67},{4,68},{5,69},{6,70},{7,71},{8,72},{9,... | collective-permute-start | bytes 73736 | tf_op jit(solution)/shard_map/ppermute | solution.py:401
  68.5 4.6 %collective-permute-start.11 = (f32[48,128]{1,0:T(8,128)S(1)}, f32[48,128]{1,0:T(8,128)S(1)}, u32[]{:S(2)}, u32[]{:S(2)}) collective-permute-start(f32[48,128]{1,0:T(8,128)S(1)} %add_add_fusion.1), channel_id=1, source_target_pairs={{0,32},{1,33},{2,34},{3,35},{4,36},{5,37},{6,38},{7,39},{8,40},{9,... | collective-permute-start | bytes 73736 | tf_op jit(solution)/shard_map/ppermute | solution.py:401
  73.1 5.2 %collective-permute-start.16 = (f32[48,128]{1,0:T(8,128)S(1)}, f32[48,128]{1,0:T(8,128)S(1)}, u32[]{:S(2)}, u32[]{:S(2)}) collective-permute-start(f32[48,128]{1,0:T(8,128)S(1)} %add_add_fusion), channel_id=1, source_target_pairs={{0,12},{1,13},{2,14},{3,15},{4,8},{5,9},{6,10},{7,11},{8,4},{9,5},... | collective-permute-start | bytes 73736 | tf_op jit(solution)/shard_map/ppermute | solution.py:401
  75.8 5.3 %collective-permute-start.15 = (f32[48,128]{1,0:T(8,128)S(1)}, f32[48,128]{1,0:T(8,128)S(1)}, u32[]{:S(2)}, u32[]{:S(2)}) collective-permute-start(f32[48,128]{1,0:T(8,128)S(1)} %add_add_fusion), channel_id=1, source_target_pairs={{0,8},{1,9},{2,10},{3,11},{4,12},{5,13},{6,14},{7,15},{8,0},{9,1},... | collective-permute-start | bytes 73736 | tf_op jit(solution)/shard_map/ppermute | solution.py:401
  77.1 4.1 %collective-permute-start.14 = (f32[48,128]{1,0:T(8,128)S(1)}, f32[48,128]{1,0:T(8,128)S(1)}, u32[]{:S(2)}, u32[]{:S(2)}) collective-permute-start(f32[48,128]{1,0:T(8,128)S(1)} %add_add_fusion), channel_id=1, source_target_pairs={{0,4},{1,5},{2,6},{3,7},{4,0},{5,1},{6,2},{7,3},{8,12},{9,13},{10,... | collective-permute-start | bytes 73736 | tf_op jit(solution)/shard_map/ppermute | solution.py:401

commit v6 on v5

--- a/solution.py
+++ b/solution.py
@@ -73,14 +73,36 @@
     )(weight_in, weight_out.T, bias_in[None], bias_out[None])
 
 
-def pack_kernel(dist, cot, mask, up, down, cols, line):
-    for out, rows in ((up, (126, 127)), (down, (0, 1))):
+def lines_kernel(dist_low, dist_high, cot_low, cot_high, mask_low, mask_high, up, down, line):
+    for out, dist, cot, mask, rows in (
+        (up, dist_high, cot_high, mask_high, (6, 7)),
+        (down, dist_low, cot_low, mask_low, (0, 1)),
+    ):
         for i, r in enumerate(rows):
-            line[pl.ds(0, 38), :] = dist[pl.ds(r, 38, stride=128), :]
-            line[pl.ds(38, 2), :] = mask[pl.ds(r, 2, stride=128), :].astype(f32)
-            line[pl.ds(40, 38), :] = cot[pl.ds(r, 38, stride=128), :]
+            line[pl.ds(0, 38), :] = dist[:, r, :]
+            line[pl.ds(38, 2), :] = mask[:, r, :].astype(f32)
+            line[pl.ds(40, 38), :] = cot[:, r, :]
             line[pl.ds(78, 2), :] = jnp.zeros((2, 128), f32)
             out[pl.ds(i * 80, 80), :] = line[...].astype(bf16)
+
+
+def outer_lines(dist, cot, mask):
+    dist, cot = dist.reshape(38, 128, 128), cot.reshape(38, 128, 128)
+
+    def ends(count):
+        return [pl.BlockSpec((count, 8, 128), lambda i: (0, 0, 0)), pl.BlockSpec((count, 8, 128), lambda i: (0, 15, 0))]
+
+    return pl.pallas_call(
+        lines_kernel,
+        grid=(1,),
+        out_shape=[jax.ShapeDtypeStruct((160, 128), bf16)] * 2,
+        in_specs=ends(38) + ends(38) + ends(2),
+        out_specs=[pl.BlockSpec((160, 128), lambda i: (0, 0))] * 2,
+        scratch_shapes=[pltpu.VMEM((80, 128), f32)],
+    )(dist, dist, cot, cot, mask, mask)
+
+
+def pack_kernel(dist, cot, mask, cols):
     lane, row = iota((8, 128), 1), iota((8, 128), 0)
     pick = jnp.zeros((8, 128), f32)
     for j, y in enumerate(COLS):
@@ -104,10 +126,10 @@
 def pack(dist, cot, mask):
     return pl.pallas_call(
         pack_kernel,
-        out_shape=[jax.ShapeDtypeStruct((160, 128), bf16)] * 2 + [jax.ShapeDtypeStruct((640, 128), f32)],
+        out_shape=jax.ShapeDtypeStruct((640, 128), f32),
         in_specs=vmem(3),
-        out_specs=vmem(3),
-        scratch_shapes=[pltpu.VMEM((80, 128), f32)],
+        out_specs=vmem(1)[0],
+        cost_estimate=pl.CostEstimate(flops=10**8, bytes_accessed=6 * 10**6, transcendentals=0),
     )(dist.reshape(38 * 128, 128), cot.reshape(38 * 128, 128), mask.reshape(256, 128))
 
 
@@ -406,16 +428,17 @@
 
 
 def shards(dist, cot, mask, weight_in, bias_in, weight_out, bias_out):
-    send_up, send_down, cols = pack(dist, cot, mask)
+    send_up, send_down = outer_lines(dist, cot, mask)
     up, down = neighbours("gx")
     from_up = lax.ppermute(send_up, "gx", up)
     from_down = lax.ppermute(send_down, "gx", down)
-    nets = make_weights(weight_in, weight_out, bias_in, bias_out)
-    cols, nets = lax.optimization_barrier((cols, nets))
+    cols = pack(dist, cot, mask)
     side_up, side_down, edge, lines = corners(from_up, from_down, cols)
     up, down = neighbours("gy")
     from_left = lax.ppermute(side_up, "gy", up)
     from_right = lax.ppermute(side_down, "gy", down)
+    weight_in, _ = lax.optimization_barrier((weight_in, edge))
+    nets = make_weights(weight_in, weight_out, bias_in, bias_out)
     grad, parts = main_call(dist, cot, mask, cols, edge, from_left, from_right, lines, *nets)
     total = summed(parts)
     cells = mask.size * lax.axis_size("gx") * lax.axis_size("gy")

time: 83.6 us -> 82.7 us (0.989)
  waiting for transfers between devices: 12.8 us -> 9.76 us
  Pallas kernels: 38.1 us -> 39.9 us
    ppermute x1, waiting for transfers between devices: 2.33 us -> 0.02 us  [shards(): from_left = lax.ppermute(side_up, 'gy', up)]
    pallas_call x1 -> x2, Pallas kernels: 4.05 us -> 5.89 us  [the longest x1 4.01 us: pack(): pl.pallas_call(pack_kernel, out_shape=jax.ShapeDtypeStruct((640, 128), f3...]
  transfers between devices with their start and end apart: 17 -> 17, of which waited for: 9 -> 7; matrix products, arithmetic and copies ran while one was open for 0% -> 0% of each run, Pallas kernels for 3% -> 8%
where the time goes in v6:
time: 82.7 us; the launch traced here: 82.3 us
  Pallas kernels  39.9 us (48%)
  starting transfers between devices  27.6 us (33%)
  waiting for transfers between devices  9.76 us (12%)
  local copies, waits for them, and re-layouts  3.48 us (4%)
    pallas_call x1, Pallas kernels, main_call(): pl.pallas_call(main_kernel, out_shape=[jax.ShapeDtypeStruct((Q, 2, 128, 1...  29.7 us
    ppermute x13, starting transfers between devices, summed(): got.append(lax.ppermute(values, ('gx', 'gy'), pairs))  18 us
    ppermute x13, waiting for transfers between devices, summed(): got.append(lax.ppermute(values, ('gx', 'gy'), pairs))  9.69 us
    ppermute x1, starting transfers between devices, shards(): from_right = lax.ppermute(side_down, 'gy', down)  5.46 us
    pallas_call x1, Pallas kernels, pack(): pl.pallas_call(pack_kernel, out_shape=jax.ShapeDtypeStruct((640, 128), f3...  4.01 us
    ppermute x1, starting transfers between devices, shards(): from_down = lax.ppermute(send_down, 'gx', down)  2.56 us
    pallas_call x1, Pallas kernels, make_weights(): pl.pallas_call(weights_kernel, out_shape=[jax.ShapeDtypeStruct((1024, 160...  2.3 us
    pallas_call x1, Pallas kernels, corners(): pl.pallas_call(corner_kernel, out_shape=[jax.ShapeDtypeStruct((160, 256),...  2.06 us
  transfers between devices with their start and end apart: 17, of which 7 were waited for; matrix products, arithmetic and copies ran while one was open for 0% of the time, Pallas kernels for 8%

profile of v6, /device:TPU:0, one launch (start us, length us, event | category | flops | bytes accessed | tf_op | source)
XLA Modules:
  0.0 82.3 jit_solution(861100702523600723)
XLA Ops:
  0.6 1.9 %shard_map.111 = (bf16[160,128]{1,0:T(8,128)(2,1)}, bf16[160,128]{1,0:T(8,128)(2,1)}) custom-call(f32[38,128,128]{2,1,0:T(8,128)} %bitcast.14, f32[38,128,128]{2,1,0:T(8,128)} %bitcast.15, f32[38,128,128]{2,1,0:T(8,128)} %bitcast.17, f32[38,128,128]{2,1,0:T(8,128)} %bitcast.18, s32[2,128,128]{2,1,0:T(8,128)} %mask.1, s32[2,128,128]{2,1,0:T(8,128)} %mask.1), custom_call_target="tpu_custom_call" | custom-call | tf_op jit(solution)/shard_map/pallas_call | solution.py:95
  2.5 1.6 %collective-permute-start = (bf16[160,128]{1,0:T(8,128)(2,1)}, bf16[160,128]{1,0:T(8,128)(2,1)S(1)}, u32[]{:S(2)}, u32[]{:S(2)}) collective-permute-start(bf16[160,128]{1,0:T(8,128)(2,1)} %get-tuple-element.19), channel_id=1, source_target_pairs={{0,16},{16,32},{32,48},{48,64},{64,80},{80,96},{96,112},{112,0},{1... | collective-permute-start | bytes 122888 | tf_op jit(solution)/shard_map/ppermute | solution.py:433
  4.1 2.6 %collective-permute-start.1 = (bf16[160,128]{1,0:T(8,128)(2,1)}, bf16[160,128]{1,0:T(8,128)(2,1)S(1)}, u32[]{:S(2)}, u32[]{:S(2)}) collective-permute-start(bf16[160,128]{1,0:T(8,128)(2,1)} %get-tuple-element.20), channel_id=1, source_target_pairs={{16,0},{32,16},{48,32},{64,48},{80,64},{96,80},{112,96},{0,112},{1... | collective-permute-start | bytes 122888 | tf_op jit(solution)/shard_map/ppermute | solution.py:434
  6.6 4.0 %shard_map.110.cols = f32[640,128]{1,0:T(8,128)} custom-call(f32[4864,128]{1,0:T(8,128)} %bitcast.16, f32[4864,128]{1,0:T(8,128)} %bitcast.19, s32[256,128]{1,0:T(8,128)} %bitcast.20), custom_call_target="tpu_custom_call" | custom-call | flops 100000000 | bytes 6000000 | tf_op jit(solution)/shard_map/pallas_call | solution.py:127
  10.7 0.6 copy-done.2
  11.3 0.6 copy-done.3
  11.9 2.1 %shard_map.112 = (bf16[160,256]{1,0:T(8,128)(2,1)}, bf16[160,256]{1,0:T(8,128)(2,1)}, f32[640,128]{1,0:T(8,128)}, f32[640,128]{1,0:T(8,128)}) custom-call(bf16[160,128]{1,0:T(8,128)(2,1)} %copy-done.2, bf16[160,128]{1,0:T(8,128)(2,1)} %copy-done.3, f32[640,128]{1,0:T(8,128)} %shard_map.110.cols), custom_call_target="tpu_custom_call" | custom-call | tf_op jit(solution)/shard_map/pallas_call | solution.py:155
  13.9 5.5 %collective-permute-start.3 = (bf16[160,256]{1,0:T(8,128)(2,1)}, bf16[160,256]{1,0:T(8,128)(2,1)S(1)}, u32[]{:S(2)}, u32[]{:S(2)}) collective-permute-start(bf16[160,256]{1,0:T(8,128)(2,1)} %get-tuple-element.23), channel_id=1, source_target_pairs={{1,0},{2,1},{3,2},{4,3},{5,4},{6,5},{7,6},{8,7},{9,8},{10,9},{11,1... | collective-permute-start | bytes 245768 | tf_op jit(solution)/shard_map/ppermute | solution.py:439
  19.4 2.3 %shard_map.113 = (bf16[1024,160]{1,0:T(8,128)(2,1)}, bf16[1024,160]{1,0:T(8,128)(2,1)}, bf16[160,1024]{1,0:T(8,128)(2,1)}, bf16[160,1024]{1,0:T(8,128)(2,1)}, f32[152,128]{1,0:T(8,128)}) custom-call(bf16[19,128]{1,0:T(8,128)(2,1)} %win, bf16[19,128]{1,0:T(8,128)(2,1)} %bitcast.21, f32[1,128]{1,0:T(1,128)} %bitcast.22, f32[1,19]{1,0:T(1,128)} %bitcast.23), custom_call_target="tpu_custom_call" | custom-call | flops 100000000 | bytes 2000000 | tf_op jit(solution)/shard_map/pallas_call | solution.py:65
  21.8 0.6 copy-done
  22.4 29.7 %shard_map.114 = (f32[19,2,128,128]{3,2,1,0:T(8,128)}, f32[48,128]{1,0:T(8,128)}) custom-call(f32[19,2,128,128]{3,2,1,0:T(8,128)} %dist.1, f32[19,2,128,128]{3,2,1,0:T(8,128)} %cot.1, s32[2,128,128]{2,1,0:T(8,128)} %mask.1, f32[640,128]{1,0:T(8,128)} %shard_map.110.cols, f32[640,128]{1,0:T(8,128)} %get-tuple-element.21.edge, bf16[160,256]{1,0:T(8,128)(2,1)} %copy-done, ...), custom_call_target="tpu_custom_call" | custom-call | tf_op jit(solution)/shard_map/pallas_call | solution.py:382
  52.1 1.9 %collective-permute-start.10 = (f32[48,128]{1,0:T(8,128)}, f32[48,128]{1,0:T(8,128)S(1)}, u32[]{:S(2)}, u32[]{:S(2)}) collective-permute-start(f32[48,128]{1,0:T(8,128)} %get-tuple-element.32), channel_id=1, source_target_pairs={{0,19},{1,18},{2,17},{3,16},{4,23},{5,22},{6,21},{7,20},{8,27},{9,... | collective-permute-start | bytes 73736 | tf_op jit(solution)/shard_map/ppermute | solution.py:423
  54.0 2.0 %collective-permute-start.9 = (f32[48,128]{1,0:T(8,128)}, f32[48,128]{1,0:T(8,128)S(1)}, u32[]{:S(2)}, u32[]{:S(2)}) collective-permute-start(f32[48,128]{1,0:T(8,128)} %get-tuple-element.32), channel_id=1, source_target_pairs={{0,18},{1,19},{2,16},{3,17},{4,22},{5,23},{6,20},{7,21},{8,26},{9,... | collective-permute-start | bytes 73736 | tf_op jit(solution)/shard_map/ppermute | solution.py:423
  55.9 2.4 %collective-permute-start.7 = (f32[48,128]{1,0:T(8,128)}, f32[48,128]{1,0:T(8,128)S(1)}, u32[]{:S(2)}, u32[]{:S(2)}) collective-permute-start(f32[48,128]{1,0:T(8,128)} %get-tuple-element.32), channel_id=1, source_target_pairs={{0,2},{1,3},{2,0},{3,1},{4,6},{5,7},{6,4},{7,5},{8,10},{9,11},{10,... | collective-permute-start | bytes 73736 | tf_op jit(solution)/shard_map/ppermute | solution.py:423
  58.3 0.1 collective-permute-start.6
  58.4 2.5 %collective-permute-start.5 = (f32[48,128]{1,0:T(8,128)}, f32[48,128]{1,0:T(8,128)S(1)}, u32[]{:S(2)}, u32[]{:S(2)}) collective-permute-start(f32[48,128]{1,0:T(8,128)} %get-tuple-element.32), channel_id=1, source_target_pairs={{0,16},{1,17},{2,18},{3,19},{4,20},{5,21},{6,22},{7,23},{8,24},{9,... | collective-permute-start | bytes 73736 | tf_op jit(solution)/shard_map/ppermute | solution.py:423
  60.9 0.6 collective-permute-done.7
  61.5 0.3 collective-permute-done.6
  61.8 1.4 %collective-permute-done.5 = f32[48,128]{1,0:T(8,128)S(1)} collective-permute-done((f32[48,128]{1,0:T(8,128)}, f32[48,128]{1,0:T(8,128)S(1)}, u32[]{:S(2)}, u32[]{:S(2)}) %collective-permute-start.5) | collective-permute-done | bytes 24608 | tf_op jit(solution)/shard_map/ppermute | solution.py:423
  63.2 0.8 add_add_fusion.1
  63.9 1.9 %collective-permute-start.13 = (f32[48,128]{1,0:T(8,128)S(1)}, f32[48,128]{1,0:T(8,128)S(1)}, u32[]{:S(2)}, u32[]{:S(2)}) collective-permute-start(f32[48,128]{1,0:T(8,128)S(1)} %add_add_fusion.1), channel_id=1, source_target_pairs={{0,96},{1,97},{2,98},{3,99},{4,100},{5,101},{6,102},{7,103},{8,104... | collective-permute-start | bytes 73736 | tf_op jit(solution)/shard_map/ppermute | solution.py:423
  65.8 0.6 collective-permute-start.12
  66.5 1.7 %collective-permute-start.11 = (f32[48,128]{1,0:T(8,128)S(1)}, f32[48,128]{1,0:T(8,128)S(1)}, u32[]{:S(2)}, u32[]{:S(2)}) collective-permute-start(f32[48,128]{1,0:T(8,128)S(1)} %add_add_fusion.1), channel_id=1, source_target_pairs={{0,32},{1,33},{2,34},{3,35},{4,36},{5,37},{6,38},{7,39},{8,40},{9,... | collective-permute-start | bytes 73736 | tf_op jit(solution)/shard_map/ppermute | solution.py:423
  68.1 0.9 %collective-permute-done.13 = f32[48,128]{1,0:T(8,128)S(1)} collective-permute-done((f32[48,128]{1,0:T(8,128)S(1)}, f32[48,128]{1,0:T(8,128)S(1)}, u32[]{:S(2)}, u32[]{:S(2)}) %collective-permute-start.13) | collective-permute-done | bytes 24608 | tf_op jit(solution)/shard_map/ppermute | solution.py:423
  69.1 2.1 %collective-permute-done.12 = f32[48,128]{1,0:T(8,128)S(1)} collective-permute-done((f32[48,128]{1,0:T(8,128)S(1)}, f32[48,128]{1,0:T(8,128)S(1)}, u32[]{:S(2)}, u32[]{:S(2)}) %collective-permute-start.12) | collective-permute-done | bytes 24608 | tf_op jit(solution)/shard_map/ppermute | solution.py:423
  71.2 4.1 %collective-permute-start.16 = (f32[48,128]{1,0:T(8,128)S(1)}, f32[48,128]{1,0:T(8,128)S(1)}, u32[]{:S(2)}, u32[]{:S(2)}) collective-permute-start(f32[48,128]{1,0:T(8,128)S(1)} %add_add_fusion), channel_id=1, source_target_pairs={{0,12},{1,13},{2,14},{3,15},{4,8},{5,9},{6,10},{7,11},{8,4},{9,5},... | collective-permute-start | bytes 73736 | tf_op jit(solution)/shard_map/ppermute | solution.py:423
  75.3 0.9 %collective-permute-start.14 = (f32[48,128]{1,0:T(8,128)S(1)}, f32[48,128]{1,0:T(8,128)S(1)}, u32[]{:S(2)}, u32[]{:S(2)}) collective-permute-start(f32[48,128]{1,0:T(8,128)S(1)} %add_add_fusion), channel_id=1, source_target_pairs={{0,4},{1,5},{2,6},{3,7},{4,0},{5,1},{6,2},{7,3},{8,12},{9,13},{10,... | collective-permute-start | bytes 73736 | tf_op jit(solution)/shard_map/ppermute | solution.py:423
  76.2 0.9 %collective-permute-done.16 = f32[48,128]{1,0:T(8,128)S(1)} collective-permute-done((f32[48,128]{1,0:T(8,128)S(1)}, f32[48,128]{1,0:T(8,128)S(1)}, u32[]{:S(2)}, u32[]{:S(2)}) %collective-permute-start.16) | collective-permute-done | bytes 24608 | tf_op jit(solution)/shard_map/ppermute | solution.py:423
  77.1 3.5 %collective-permute-done.15 = f32[48,128]{1,0:T(8,128)S(1)} collective-permute-done((f32[48,128]{1,0:T(8,128)S(1)}, f32[48,128]{1,0:T(8,128)S(1)}, u32[]{:S(2)}, u32[]{:S(2)}) %collective-permute-start.15) | collective-permute-done | bytes 24608 | tf_op jit(solution)/shard_map/ppermute | solution.py:423
  80.6 0.5 slice_bitcast_fusion.2
  81.2 0.5 slice_bitcast_fusion.1
  81.7 0.6 slice_bitcast_fusion
  (21 shorter events, 0.2 us)
Async XLA Ops:
  2.5 8.2 %collective-permute-start = (bf16[160,128]{1,0:T(8,128)(2,1)}, bf16[160,128]{1,0:T(8,128)(2,1)S(1)}, u32[]{:S(2)}, u32[]{:S(2)}) collective-permute-start(bf16[160,128]{1,0:T(8,128)(2,1)} %get-tuple-element.19), channel_id=1, source_target_pairs={{0,16},{16,32},{32,48},{48,64},{64,80},{80,96},{96,112},{112,0},{1... | collective-permute-start | bytes 122888 | tf_op jit(solution)/shard_map/ppermute | solution.py:433
  4.1 6.6 %collective-permute-start.1 = (bf16[160,128]{1,0:T(8,128)(2,1)}, bf16[160,128]{1,0:T(8,128)(2,1)S(1)}, u32[]{:S(2)}, u32[]{:S(2)}) collective-permute-start(bf16[160,128]{1,0:T(8,128)(2,1)} %get-tuple-element.20), channel_id=1, source_target_pairs={{16,0},{32,16},{48,32},{64,48},{80,64},{96,80},{112,96},{0,112},{1... | collective-permute-start | bytes 122888 | tf_op jit(solution)/shard_map/ppermute | solution.py:434
  10.7 0.6 copy-start.2
  11.3 0.6 copy-start.3
  13.9 7.8 %collective-permute-start.2 = (bf16[160,256]{1,0:T(8,128)(2,1)}, bf16[160,256]{1,0:T(8,128)(2,1)S(1)}, u32[]{:S(2)}, u32[]{:S(2)}) collective-permute-start(bf16[160,256]{1,0:T(8,128)(2,1)} %get-tuple-element.22), channel_id=1, source_target_pairs={{0,1},{1,2},{2,3},{3,4},{4,5},{5,6},{6,7},{7,8},{8,9},{9,10},{10,1... | collective-permute-start | bytes 245768 | tf_op jit(solution)/shard_map/ppermute | solution.py:438
  13.9 7.8 %collective-permute-start.3 = (bf16[160,256]{1,0:T(8,128)(2,1)}, bf16[160,256]{1,0:T(8,128)(2,1)S(1)}, u32[]{:S(2)}, u32[]{:S(2)}) collective-permute-start(bf16[160,256]{1,0:T(8,128)(2,1)} %get-tuple-element.23), channel_id=1, source_target_pairs={{1,0},{2,1},{3,2},{4,3},{5,4},{6,5},{7,6},{8,7},{9,8},{10,9},{11,1... | collective-permute-start | bytes 245768 | tf_op jit(solution)/shard_map/ppermute | solution.py:439
  21.7 0.6 copy-start
  21.8 0.6 copy-start.1
  52.1 6.3 %collective-permute-start.10 = (f32[48,128]{1,0:T(8,128)}, f32[48,128]{1,0:T(8,128)S(1)}, u32[]{:S(2)}, u32[]{:S(2)}) collective-permute-start(f32[48,128]{1,0:T(8,128)} %get-tuple-element.32), channel_id=1, source_target_pairs={{0,19},{1,18},{2,17},{3,16},{4,23},{5,22},{6,21},{7,20},{8,27},{9,... | collective-permute-start | bytes 73736 | tf_op jit(solution)/shard_map/ppermute | solution.py:423
  54.0 7.0 %collective-permute-start.9 = (f32[48,128]{1,0:T(8,128)}, f32[48,128]{1,0:T(8,128)S(1)}, u32[]{:S(2)}, u32[]{:S(2)}) collective-permute-start(f32[48,128]{1,0:T(8,128)} %get-tuple-element.32), channel_id=1, source_target_pairs={{0,18},{1,19},{2,16},{3,17},{4,22},{5,23},{6,20},{7,21},{8,26},{9,... | collective-permute-start | bytes 73736 | tf_op jit(solution)/shard_map/ppermute | solution.py:423
  55.9 5.0 %collective-permute-start.8 = (f32[48,128]{1,0:T(8,128)}, f32[48,128]{1,0:T(8,128)S(1)}, u32[]{:S(2)}, u32[]{:S(2)}) collective-permute-start(f32[48,128]{1,0:T(8,128)} %get-tuple-element.32), channel_id=1, source_target_pairs={{0,3},{1,2},{2,1},{3,0},{4,7},{5,6},{6,5},{7,4},{8,11},{9,10},{10,... | collective-permute-start | bytes 73736 | tf_op jit(solution)/shard_map/ppermute | solution.py:423
  55.9 5.6 %collective-permute-start.7 = (f32[48,128]{1,0:T(8,128)}, f32[48,128]{1,0:T(8,128)S(1)}, u32[]{:S(2)}, u32[]{:S(2)}) collective-permute-start(f32[48,128]{1,0:T(8,128)} %get-tuple-element.32), channel_id=1, source_target_pairs={{0,2},{1,3},{2,0},{3,1},{4,6},{5,7},{6,4},{7,5},{8,10},{9,11},{10,... | collective-permute-start | bytes 73736 | tf_op jit(solution)/shard_map/ppermute | solution.py:423
  58.3 3.5 %collective-permute-start.6 = (f32[48,128]{1,0:T(8,128)}, f32[48,128]{1,0:T(8,128)S(1)}, u32[]{:S(2)}, u32[]{:S(2)}) collective-permute-start(f32[48,128]{1,0:T(8,128)} %get-tuple-element.32), channel_id=1, source_target_pairs={{0,17},{1,16},{2,19},{3,18},{4,21},{5,20},{6,23},{7,22},{8,25},{9,... | collective-permute-start | bytes 73736 | tf_op jit(solution)/shard_map/ppermute | solution.py:423
  58.4 4.8 %collective-permute-start.5 = (f32[48,128]{1,0:T(8,128)}, f32[48,128]{1,0:T(8,128)S(1)}, u32[]{:S(2)}, u32[]{:S(2)}) collective-permute-start(f32[48,128]{1,0:T(8,128)} %get-tuple-element.32), channel_id=1, source_target_pairs={{0,16},{1,17},{2,18},{3,19},{4,20},{5,21},{6,22},{7,23},{8,24},{9,... | collective-permute-start | bytes 73736 | tf_op jit(solution)/shard_map/ppermute | solution.py:423
  60.9 2.3 %collective-permute-start.4 = (f32[48,128]{1,0:T(8,128)}, f32[48,128]{1,0:T(8,128)S(1)}, u32[]{:S(2)}, u32[]{:S(2)}) collective-permute-start(f32[48,128]{1,0:T(8,128)} %get-tuple-element.32), channel_id=1, source_target_pairs={{0,1},{1,0},{2,3},{3,2},{4,5},{5,4},{6,7},{7,6},{8,9},{9,8},{10,11... | collective-permute-start | bytes 73736 | tf_op jit(solution)/shard_map/ppermute | solution.py:423
  63.9 5.1 %collective-permute-start.13 = (f32[48,128]{1,0:T(8,128)S(1)}, f32[48,128]{1,0:T(8,128)S(1)}, u32[]{:S(2)}, u32[]{:S(2)}) collective-permute-start(f32[48,128]{1,0:T(8,128)S(1)} %add_add_fusion.1), channel_id=1, source_target_pairs={{0,96},{1,97},{2,98},{3,99},{4,100},{5,101},{6,102},{7,103},{8,104... | collective-permute-start | bytes 73736 | tf_op jit(solution)/shard_map/ppermute | solution.py:423
  65.8 5.3 %collective-permute-start.12 = (f32[48,128]{1,0:T(8,128)S(1)}, f32[48,128]{1,0:T(8,128)S(1)}, u32[]{:S(2)}, u32[]{:S(2)}) collective-permute-start(f32[48,128]{1,0:T(8,128)S(1)} %add_add_fusion.1), channel_id=1, source_target_pairs={{0,64},{1,65},{2,66},{3,67},{4,68},{5,69},{6,70},{7,71},{8,72},{9,... | collective-permute-start | bytes 73736 | tf_op jit(solution)/shard_map/ppermute | solution.py:423
  66.5 4.7 %collective-permute-start.11 = (f32[48,128]{1,0:T(8,128)S(1)}, f32[48,128]{1,0:T(8,128)S(1)}, u32[]{:S(2)}, u32[]{:S(2)}) collective-permute-start(f32[48,128]{1,0:T(8,128)S(1)} %add_add_fusion.1), channel_id=1, source_target_pairs={{0,32},{1,33},{2,34},{3,35},{4,36},{5,37},{6,38},{7,39},{8,40},{9,... | collective-permute-start | bytes 73736 | tf_op jit(solution)/shard_map/ppermute | solution.py:423
  71.2 5.9 %collective-permute-start.16 = (f32[48,128]{1,0:T(8,128)S(1)}, f32[48,128]{1,0:T(8,128)S(1)}, u32[]{:S(2)}, u32[]{:S(2)}) collective-permute-start(f32[48,128]{1,0:T(8,128)S(1)} %add_add_fusion), channel_id=1, source_target_pairs={{0,12},{1,13},{2,14},{3,15},{4,8},{5,9},{6,10},{7,11},{8,4},{9,5},... | collective-permute-start | bytes 73736 | tf_op jit(solution)/shard_map/ppermute | solution.py:423
  75.3 5.3 %collective-permute-start.15 = (f32[48,128]{1,0:T(8,128)S(1)}, f32[48,128]{1,0:T(8,128)S(1)}, u32[]{:S(2)}, u32[]{:S(2)}) collective-permute-start(f32[48,128]{1,0:T(8,128)S(1)} %add_add_fusion), channel_id=1, source_target_pairs={{0,8},{1,9},{2,10},{3,11},{4,12},{5,13},{6,14},{7,15},{8,0},{9,1},... | collective-permute-start | bytes 73736 | tf_op jit(solution)/shard_map/ppermute | solution.py:423
  75.3 5.3 %collective-permute-start.14 = (f32[48,128]{1,0:T(8,128)S(1)}, f32[48,128]{1,0:T(8,128)S(1)}, u32[]{:S(2)}, u32[]{:S(2)}) collective-permute-start(f32[48,128]{1,0:T(8,128)S(1)} %add_add_fusion), channel_id=1, source_target_pairs={{0,4},{1,5},{2,6},{3,7},{4,0},{5,1},{6,2},{7,3},{8,12},{9,13},{10,... | collective-permute-start | bytes 73736 | tf_op jit(solution)/shard_map/ppermute | solution.py:423

commit v7 on v6

--- a/solution.py
+++ b/solution.py
@@ -133,17 +133,17 @@
     )(dist.reshape(38 * 128, 128), cot.reshape(38 * 128, 128), mask.reshape(256, 128))
 
 
-def corner_kernel(from_up, from_down, cols, send_up, send_down, edge, lines):
-    sides = ((from_down, 0, 0), (from_down, 1, 1), (from_up, 0, 126), (from_up, 1, 127))
+def corner_kernel(received, cols, send_up, send_down, edge, lines):
+    sides = ((2, 0), (3, 1), (0, 126), (1, 127))
     lane = iota((80, 128), 1)
-    got = [ref[pl.ds(i * 80, 80), :].astype(f32) for ref, i, _ in sides]
-    for (_, _, place), values in zip(sides, got):
+    got = [received[pl.ds(i * 80, 80), :].astype(f32) for i, _ in sides]
+    for (_, place), values in zip(sides, got):
         lines[pl.ds(place % 8, 80, stride=8), :] = values
     for r in range(2, 6):
         lines[pl.ds(r, 80, stride=8), :] = jnp.zeros((80, 128), f32)
     for j, y in enumerate(COLS):
         out = jnp.zeros((80, 128), f32)
-        for (_, _, place), values in zip(sides, got):
+        for (_, place), values in zip(sides, got):
             out = jnp.where(lane == place, values[:, y : y + 1], out)
         edge[pl.ds(j * 80, 80), :] = out
     for out, first in ((send_up, 0), (send_down, 6)):
@@ -151,14 +151,14 @@
         out[:, 128:] = edge[pl.ds(first * 80, 160), :].astype(bf16)
 
 
-def corners(from_up, from_down, cols):
+def corners(received, cols):
     return pl.pallas_call(
         corner_kernel,
         out_shape=[jax.ShapeDtypeStruct((160, 256), bf16)] * 2
         + [jax.ShapeDtypeStruct((640, 128), f32)] * 2,
-        in_specs=vmem(3),
+        in_specs=vmem(2),
         out_specs=vmem(4),
-    )(from_up, from_down, cols)
+    )(received, cols)
 
 
 def main_kernel(
@@ -433,7 +433,7 @@
     from_up = lax.ppermute(send_up, "gx", up)
     from_down = lax.ppermute(send_down, "gx", down)
     cols = pack(dist, cot, mask)
-    side_up, side_down, edge, lines = corners(from_up, from_down, cols)
+    side_up, side_down, edge, lines = corners(jnp.concatenate([from_up, from_down]), cols)
     up, down = neighbours("gy")
     from_left = lax.ppermute(side_up, "gy", up)
     from_right = lax.ppermute(side_down, "gy", down)

time: 82.7 us -> 82.2 us (level)
  local copies, waits for them, and re-layouts: 3.48 us -> 2.26 us
    unnamed x8 -> x4, local copies, waits for them, and re-layouts: 1.85 us -> 0.63 us
where the time goes in v7:
time: 82.2 us; the launch traced here: 81.7 us
  Pallas kernels  40 us (49%)
  starting transfers between devices  27.3 us (33%)
  waiting for transfers between devices  10.1 us (12%)
  local copies, waits for them, and re-layouts  2.26 us (3%)
  other arithmetic  1.42 us (2%)
    pallas_call x1, Pallas kernels, main_call(): pl.pallas_call(main_kernel, out_shape=[jax.ShapeDtypeStruct((Q, 2, 128, 1...  29.7 us
    ppermute x13, starting transfers between devices, summed(): got.append(lax.ppermute(values, ('gx', 'gy'), pairs))  17.7 us
    ppermute x13, waiting for transfers between devices, summed(): got.append(lax.ppermute(values, ('gx', 'gy'), pairs))  10 us
    ppermute x1, starting transfers between devices, shards(): from_right = lax.ppermute(side_down, 'gy', down)  5.46 us
    pallas_call x1, Pallas kernels, pack(): pl.pallas_call(pack_kernel, out_shape=jax.ShapeDtypeStruct((640, 128), f3...  4.01 us
    ppermute x1, starting transfers between devices, shards(): from_down = lax.ppermute(send_down, 'gx', down)  2.56 us
    pallas_call x1, Pallas kernels, make_weights(): pl.pallas_call(weights_kernel, out_shape=[jax.ShapeDtypeStruct((1024, 160...  2.3 us
    pallas_call x1, Pallas kernels, corners(): pl.pallas_call(corner_kernel, out_shape=[jax.ShapeDtypeStruct((160, 256),...  2.1 us
  transfers between devices with their start and end apart: 17, of which 7 were waited for; matrix products, arithmetic and copies ran while one was open for 0% of the time, Pallas kernels for 8%

profile of v7, /device:TPU:0, one launch (start us, length us, event | category | flops | bytes accessed | tf_op | source)
XLA Modules:
  0.0 81.7 jit_solution(10310888747197157371)
XLA Ops:
  0.6 1.9 %shard_map.111 = (bf16[160,128]{1,0:T(8,128)(2,1)}, bf16[160,128]{1,0:T(8,128)(2,1)}) custom-call(f32[38,128,128]{2,1,0:T(8,128)} %bitcast.14, f32[38,128,128]{2,1,0:T(8,128)} %bitcast.15, f32[38,128,128]{2,1,0:T(8,128)} %bitcast.17, f32[38,128,128]{2,1,0:T(8,128)} %bitcast.18, s32[2,128,128]{2,1,0:T(8,128)} %mask.1, s32[2,128,128]{2,1,0:T(8,128)} %mask.1), custom_call_target="tpu_custom_call" | custom-call | tf_op jit(solution)/shard_map/pallas_call | solution.py:95
  2.5 1.6 %collective-permute-start = (bf16[160,128]{1,0:T(8,128)(2,1)}, bf16[160,128]{1,0:T(8,128)(2,1)S(1)}, u32[]{:S(2)}, u32[]{:S(2)}) collective-permute-start(bf16[160,128]{1,0:T(8,128)(2,1)} %get-tuple-element.19), channel_id=1, source_target_pairs={{0,16},{16,32},{32,48},{48,64},{64,80},{80,96},{96,112},{112,0},{1... | collective-permute-start | bytes 122888 | tf_op jit(solution)/shard_map/ppermute | solution.py:433
  4.1 2.6 %collective-permute-start.1 = (bf16[160,128]{1,0:T(8,128)(2,1)}, bf16[160,128]{1,0:T(8,128)(2,1)S(1)}, u32[]{:S(2)}, u32[]{:S(2)}) collective-permute-start(bf16[160,128]{1,0:T(8,128)(2,1)} %get-tuple-element.20), channel_id=1, source_target_pairs={{16,0},{32,16},{48,32},{64,48},{80,64},{96,80},{112,96},{0,112},{1... | collective-permute-start | bytes 122888 | tf_op jit(solution)/shard_map/ppermute | solution.py:434
  6.6 4.0 %shard_map.110.cols = f32[640,128]{1,0:T(8,128)} custom-call(f32[4864,128]{1,0:T(8,128)} %bitcast.16, f32[4864,128]{1,0:T(8,128)} %bitcast.19, s32[256,128]{1,0:T(8,128)} %bitcast.20), custom_call_target="tpu_custom_call" | custom-call | flops 100000000 | bytes 6000000 | tf_op jit(solution)/shard_map/pallas_call | solution.py:127
  10.7 0.6 pad_maximum_fusion.received
  11.3 2.1 %shard_map.112 = (bf16[160,256]{1,0:T(8,128)(2,1)}, bf16[160,256]{1,0:T(8,128)(2,1)}, f32[640,128]{1,0:T(8,128)}, f32[640,128]{1,0:T(8,128)}) custom-call(bf16[320,128]{1,0:T(8,128)(2,1)} %pad_maximum_fusion.received, f32[640,128]{1,0:T(8,128)} %shard_map.110.cols), custom_call_target="tpu_custom_call" | custom-call | tf_op jit(solution)/shard_map/pallas_call | solution.py:155
  13.4 5.5 %collective-permute-start.3 = (bf16[160,256]{1,0:T(8,128)(2,1)}, bf16[160,256]{1,0:T(8,128)(2,1)S(1)}, u32[]{:S(2)}, u32[]{:S(2)}) collective-permute-start(bf16[160,256]{1,0:T(8,128)(2,1)} %get-tuple-element.23), channel_id=1, source_target_pairs={{1,0},{2,1},{3,2},{4,3},{5,4},{6,5},{7,6},{8,7},{9,8},{10,9},{11,1... | collective-permute-start | bytes 245768 | tf_op jit(solution)/shard_map/ppermute | solution.py:439
  18.9 2.3 %shard_map.113 = (bf16[1024,160]{1,0:T(8,128)(2,1)}, bf16[1024,160]{1,0:T(8,128)(2,1)}, bf16[160,1024]{1,0:T(8,128)(2,1)}, bf16[160,1024]{1,0:T(8,128)(2,1)}, f32[152,128]{1,0:T(8,128)}) custom-call(bf16[19,128]{1,0:T(8,128)(2,1)} %win, bf16[19,128]{1,0:T(8,128)(2,1)} %bitcast.21, f32[1,128]{1,0:T(1,128)} %bitcast.22, f32[1,19]{1,0:T(1,128)} %bitcast.23), custom_call_target="tpu_custom_call" | custom-call | flops 100000000 | bytes 2000000 | tf_op jit(solution)/shard_map/pallas_call | solution.py:65
  21.2 0.6 copy-done
  21.9 29.7 %shard_map.114 = (f32[19,2,128,128]{3,2,1,0:T(8,128)}, f32[48,128]{1,0:T(8,128)}) custom-call(f32[19,2,128,128]{3,2,1,0:T(8,128)} %dist.1, f32[19,2,128,128]{3,2,1,0:T(8,128)} %cot.1, s32[2,128,128]{2,1,0:T(8,128)} %mask.1, f32[640,128]{1,0:T(8,128)} %shard_map.110.cols, f32[640,128]{1,0:T(8,128)} %get-tuple-element.21.edge, bf16[160,256]{1,0:T(8,128)(2,1)} %copy-done, ...), custom_call_target="tpu_custom_call" | custom-call | tf_op jit(solution)/shard_map/pallas_call | solution.py:382
  51.6 2.5 %collective-permute-start.10 = (f32[48,128]{1,0:T(8,128)}, f32[48,128]{1,0:T(8,128)S(1)}, u32[]{:S(2)}, u32[]{:S(2)}) collective-permute-start(f32[48,128]{1,0:T(8,128)} %get-tuple-element.32), channel_id=1, source_target_pairs={{0,19},{1,18},{2,17},{3,16},{4,23},{5,22},{6,21},{7,20},{8,27},{9,... | collective-permute-start | bytes 73736 | tf_op jit(solution)/shard_map/ppermute | solution.py:423
  54.0 1.3 %collective-permute-start.9 = (f32[48,128]{1,0:T(8,128)}, f32[48,128]{1,0:T(8,128)S(1)}, u32[]{:S(2)}, u32[]{:S(2)}) collective-permute-start(f32[48,128]{1,0:T(8,128)} %get-tuple-element.32), channel_id=1, source_target_pairs={{0,18},{1,19},{2,16},{3,17},{4,22},{5,23},{6,20},{7,21},{8,26},{9,... | collective-permute-start | bytes 73736 | tf_op jit(solution)/shard_map/ppermute | solution.py:423
  55.4 2.4 %collective-permute-start.7 = (f32[48,128]{1,0:T(8,128)}, f32[48,128]{1,0:T(8,128)S(1)}, u32[]{:S(2)}, u32[]{:S(2)}) collective-permute-start(f32[48,128]{1,0:T(8,128)} %get-tuple-element.32), channel_id=1, source_target_pairs={{0,2},{1,3},{2,0},{3,1},{4,6},{5,7},{6,4},{7,5},{8,10},{9,11},{10,... | collective-permute-start | bytes 73736 | tf_op jit(solution)/shard_map/ppermute | solution.py:423
  57.8 0.1 collective-permute-start.6
  57.9 2.5 %collective-permute-start.5 = (f32[48,128]{1,0:T(8,128)}, f32[48,128]{1,0:T(8,128)S(1)}, u32[]{:S(2)}, u32[]{:S(2)}) collective-permute-start(f32[48,128]{1,0:T(8,128)} %get-tuple-element.32), channel_id=1, source_target_pairs={{0,16},{1,17},{2,18},{3,19},{4,20},{5,21},{6,22},{7,23},{8,24},{9,... | collective-permute-start | bytes 73736 | tf_op jit(solution)/shard_map/ppermute | solution.py:423
  60.4 0.6 collective-permute-done.7
  60.9 0.3 collective-permute-done.6
  61.2 1.4 %collective-permute-done.5 = f32[48,128]{1,0:T(8,128)S(1)} collective-permute-done((f32[48,128]{1,0:T(8,128)}, f32[48,128]{1,0:T(8,128)S(1)}, u32[]{:S(2)}, u32[]{:S(2)}) %collective-permute-start.5) | collective-permute-done | bytes 24608 | tf_op jit(solution)/shard_map/ppermute | solution.py:423
  62.6 0.8 add_add_fusion.1
  63.4 2.2 %collective-permute-start.13 = (f32[48,128]{1,0:T(8,128)S(1)}, f32[48,128]{1,0:T(8,128)S(1)}, u32[]{:S(2)}, u32[]{:S(2)}) collective-permute-start(f32[48,128]{1,0:T(8,128)S(1)} %add_add_fusion.1), channel_id=1, source_target_pairs={{0,96},{1,97},{2,98},{3,99},{4,100},{5,101},{6,102},{7,103},{8,104... | collective-permute-start | bytes 73736 | tf_op jit(solution)/shard_map/ppermute | solution.py:423
  65.6 0.8 collective-permute-start.12
  66.4 1.2 %collective-permute-start.11 = (f32[48,128]{1,0:T(8,128)S(1)}, f32[48,128]{1,0:T(8,128)S(1)}, u32[]{:S(2)}, u32[]{:S(2)}) collective-permute-start(f32[48,128]{1,0:T(8,128)S(1)} %add_add_fusion.1), channel_id=1, source_target_pairs={{0,32},{1,33},{2,34},{3,35},{4,36},{5,37},{6,38},{7,39},{8,40},{9,... | collective-permute-start | bytes 73736 | tf_op jit(solution)/shard_map/ppermute | solution.py:423
  67.6 0.9 %collective-permute-done.13 = f32[48,128]{1,0:T(8,128)S(1)} collective-permute-done((f32[48,128]{1,0:T(8,128)S(1)}, f32[48,128]{1,0:T(8,128)S(1)}, u32[]{:S(2)}, u32[]{:S(2)}) %collective-permute-start.13) | collective-permute-done | bytes 24608 | tf_op jit(solution)/shard_map/ppermute | solution.py:423
  68.5 2.4 %collective-permute-done.12 = f32[48,128]{1,0:T(8,128)S(1)} collective-permute-done((f32[48,128]{1,0:T(8,128)S(1)}, f32[48,128]{1,0:T(8,128)S(1)}, u32[]{:S(2)}, u32[]{:S(2)}) %collective-permute-start.12) | collective-permute-done | bytes 24608 | tf_op jit(solution)/shard_map/ppermute | solution.py:423
  70.9 3.8 %collective-permute-start.16 = (f32[48,128]{1,0:T(8,128)S(1)}, f32[48,128]{1,0:T(8,128)S(1)}, u32[]{:S(2)}, u32[]{:S(2)}) collective-permute-start(f32[48,128]{1,0:T(8,128)S(1)} %add_add_fusion), channel_id=1, source_target_pairs={{0,12},{1,13},{2,14},{3,15},{4,8},{5,9},{6,10},{7,11},{8,4},{9,5},... | collective-permute-start | bytes 73736 | tf_op jit(solution)/shard_map/ppermute | solution.py:423
  74.8 0.3 collective-permute-start.15
  75.0 0.7 collective-permute-start.14
  75.7 0.9 %collective-permute-done.16 = f32[48,128]{1,0:T(8,128)S(1)} collective-permute-done((f32[48,128]{1,0:T(8,128)S(1)}, f32[48,128]{1,0:T(8,128)S(1)}, u32[]{:S(2)}, u32[]{:S(2)}) %collective-permute-start.16) | collective-permute-done | bytes 24608 | tf_op jit(solution)/shard_map/ppermute | solution.py:423
  76.6 3.5 %collective-permute-done.15 = f32[48,128]{1,0:T(8,128)S(1)} collective-permute-done((f32[48,128]{1,0:T(8,128)S(1)}, f32[48,128]{1,0:T(8,128)S(1)}, u32[]{:S(2)}, u32[]{:S(2)}) %collective-permute-start.15) | collective-permute-done | bytes 24608 | tf_op jit(solution)/shard_map/ppermute | solution.py:423
  80.1 0.5 slice_bitcast_fusion.2
  80.6 0.5 slice_bitcast_fusion.1
  81.1 0.6 slice_bitcast_fusion
  (18 shorter events, 0.2 us)
Async XLA Ops:
  2.5 8.2 %collective-permute-start = (bf16[160,128]{1,0:T(8,128)(2,1)}, bf16[160,128]{1,0:T(8,128)(2,1)S(1)}, u32[]{:S(2)}, u32[]{:S(2)}) collective-permute-start(bf16[160,128]{1,0:T(8,128)(2,1)} %get-tuple-element.19), channel_id=1, source_target_pairs={{0,16},{16,32},{32,48},{48,64},{64,80},{80,96},{96,112},{112,0},{1... | collective-permute-start | bytes 122888 | tf_op jit(solution)/shard_map/ppermute | solution.py:433
  4.1 6.6 %collective-permute-start.1 = (bf16[160,128]{1,0:T(8,128)(2,1)}, bf16[160,128]{1,0:T(8,128)(2,1)S(1)}, u32[]{:S(2)}, u32[]{:S(2)}) collective-permute-start(bf16[160,128]{1,0:T(8,128)(2,1)} %get-tuple-element.20), channel_id=1, source_target_pairs={{16,0},{32,16},{48,32},{64,48},{80,64},{96,80},{112,96},{0,112},{1... | collective-permute-start | bytes 122888 | tf_op jit(solution)/shard_map/ppermute | solution.py:434
  13.4 7.8 %collective-permute-start.2 = (bf16[160,256]{1,0:T(8,128)(2,1)}, bf16[160,256]{1,0:T(8,128)(2,1)S(1)}, u32[]{:S(2)}, u32[]{:S(2)}) collective-permute-start(bf16[160,256]{1,0:T(8,128)(2,1)} %get-tuple-element.22), channel_id=1, source_target_pairs={{0,1},{1,2},{2,3},{3,4},{4,5},{5,6},{6,7},{7,8},{8,9},{9,10},{10,1... | collective-permute-start | bytes 245768 | tf_op jit(solution)/shard_map/ppermute | solution.py:438
  13.4 7.8 %collective-permute-start.3 = (bf16[160,256]{1,0:T(8,128)(2,1)}, bf16[160,256]{1,0:T(8,128)(2,1)S(1)}, u32[]{:S(2)}, u32[]{:S(2)}) collective-permute-start(bf16[160,256]{1,0:T(8,128)(2,1)} %get-tuple-element.23), channel_id=1, source_target_pairs={{1,0},{2,1},{3,2},{4,3},{5,4},{6,5},{7,6},{8,7},{9,8},{10,9},{11,1... | collective-permute-start | bytes 245768 | tf_op jit(solution)/shard_map/ppermute | solution.py:439
  21.2 0.6 copy-start
  21.2 0.6 copy-start.1
  51.6 6.3 %collective-permute-start.10 = (f32[48,128]{1,0:T(8,128)}, f32[48,128]{1,0:T(8,128)S(1)}, u32[]{:S(2)}, u32[]{:S(2)}) collective-permute-start(f32[48,128]{1,0:T(8,128)} %get-tuple-element.32), channel_id=1, source_target_pairs={{0,19},{1,18},{2,17},{3,16},{4,23},{5,22},{6,21},{7,20},{8,27},{9,... | collective-permute-start | bytes 73736 | tf_op jit(solution)/shard_map/ppermute | solution.py:423
  54.0 6.3 %collective-permute-start.9 = (f32[48,128]{1,0:T(8,128)}, f32[48,128]{1,0:T(8,128)S(1)}, u32[]{:S(2)}, u32[]{:S(2)}) collective-permute-start(f32[48,128]{1,0:T(8,128)} %get-tuple-element.32), channel_id=1, source_target_pairs={{0,18},{1,19},{2,16},{3,17},{4,22},{5,23},{6,20},{7,21},{8,26},{9,... | collective-permute-start | bytes 73736 | tf_op jit(solution)/shard_map/ppermute | solution.py:423
  55.4 5.0 %collective-permute-start.8 = (f32[48,128]{1,0:T(8,128)}, f32[48,128]{1,0:T(8,128)S(1)}, u32[]{:S(2)}, u32[]{:S(2)}) collective-permute-start(f32[48,128]{1,0:T(8,128)} %get-tuple-element.32), channel_id=1, source_target_pairs={{0,3},{1,2},{2,1},{3,0},{4,7},{5,6},{6,5},{7,4},{8,11},{9,10},{10,... | collective-permute-start | bytes 73736 | tf_op jit(solution)/shard_map/ppermute | solution.py:423
  55.4 5.6 %collective-permute-start.7 = (f32[48,128]{1,0:T(8,128)}, f32[48,128]{1,0:T(8,128)S(1)}, u32[]{:S(2)}, u32[]{:S(2)}) collective-permute-start(f32[48,128]{1,0:T(8,128)} %get-tuple-element.32), channel_id=1, source_target_pairs={{0,2},{1,3},{2,0},{3,1},{4,6},{5,7},{6,4},{7,5},{8,10},{9,11},{10,... | collective-permute-start | bytes 73736 | tf_op jit(solution)/shard_map/ppermute | solution.py:423
  57.8 3.5 %collective-permute-start.6 = (f32[48,128]{1,0:T(8,128)}, f32[48,128]{1,0:T(8,128)S(1)}, u32[]{:S(2)}, u32[]{:S(2)}) collective-permute-start(f32[48,128]{1,0:T(8,128)} %get-tuple-element.32), channel_id=1, source_target_pairs={{0,17},{1,16},{2,19},{3,18},{4,21},{5,20},{6,23},{7,22},{8,25},{9,... | collective-permute-start | bytes 73736 | tf_op jit(solution)/shard_map/ppermute | solution.py:423
  57.9 4.8 %collective-permute-start.5 = (f32[48,128]{1,0:T(8,128)}, f32[48,128]{1,0:T(8,128)S(1)}, u32[]{:S(2)}, u32[]{:S(2)}) collective-permute-start(f32[48,128]{1,0:T(8,128)} %get-tuple-element.32), channel_id=1, source_target_pairs={{0,16},{1,17},{2,18},{3,19},{4,20},{5,21},{6,22},{7,23},{8,24},{9,... | collective-permute-start | bytes 73736 | tf_op jit(solution)/shard_map/ppermute | solution.py:423
  60.4 2.3 %collective-permute-start.4 = (f32[48,128]{1,0:T(8,128)}, f32[48,128]{1,0:T(8,128)S(1)}, u32[]{:S(2)}, u32[]{:S(2)}) collective-permute-start(f32[48,128]{1,0:T(8,128)} %get-tuple-element.32), channel_id=1, source_target_pairs={{0,1},{1,0},{2,3},{3,2},{4,5},{5,4},{6,7},{7,6},{8,9},{9,8},{10,11... | collective-permute-start | bytes 73736 | tf_op jit(solution)/shard_map/ppermute | solution.py:423
  63.4 5.1 %collective-permute-start.13 = (f32[48,128]{1,0:T(8,128)S(1)}, f32[48,128]{1,0:T(8,128)S(1)}, u32[]{:S(2)}, u32[]{:S(2)}) collective-permute-start(f32[48,128]{1,0:T(8,128)S(1)} %add_add_fusion.1), channel_id=1, source_target_pairs={{0,96},{1,97},{2,98},{3,99},{4,100},{5,101},{6,102},{7,103},{8,104... | collective-permute-start | bytes 73736 | tf_op jit(solution)/shard_map/ppermute | solution.py:423
  65.6 5.3 %collective-permute-start.12 = (f32[48,128]{1,0:T(8,128)S(1)}, f32[48,128]{1,0:T(8,128)S(1)}, u32[]{:S(2)}, u32[]{:S(2)}) collective-permute-start(f32[48,128]{1,0:T(8,128)S(1)} %add_add_fusion.1), channel_id=1, source_target_pairs={{0,64},{1,65},{2,66},{3,67},{4,68},{5,69},{6,70},{7,71},{8,72},{9,... | collective-permute-start | bytes 73736 | tf_op jit(solution)/shard_map/ppermute | solution.py:423
  66.4 4.6 %collective-permute-start.11 = (f32[48,128]{1,0:T(8,128)S(1)}, f32[48,128]{1,0:T(8,128)S(1)}, u32[]{:S(2)}, u32[]{:S(2)}) collective-permute-start(f32[48,128]{1,0:T(8,128)S(1)} %add_add_fusion.1), channel_id=1, source_target_pairs={{0,32},{1,33},{2,34},{3,35},{4,36},{5,37},{6,38},{7,39},{8,40},{9,... | collective-permute-start | bytes 73736 | tf_op jit(solution)/shard_map/ppermute | solution.py:423
  70.9 5.6 %collective-permute-start.16 = (f32[48,128]{1,0:T(8,128)S(1)}, f32[48,128]{1,0:T(8,128)S(1)}, u32[]{:S(2)}, u32[]{:S(2)}) collective-permute-start(f32[48,128]{1,0:T(8,128)S(1)} %add_add_fusion), channel_id=1, source_target_pairs={{0,12},{1,13},{2,14},{3,15},{4,8},{5,9},{6,10},{7,11},{8,4},{9,5},... | collective-permute-start | bytes 73736 | tf_op jit(solution)/shard_map/ppermute | solution.py:423
  74.8 5.3 %collective-permute-start.15 = (f32[48,128]{1,0:T(8,128)S(1)}, f32[48,128]{1,0:T(8,128)S(1)}, u32[]{:S(2)}, u32[]{:S(2)}) collective-permute-start(f32[48,128]{1,0:T(8,128)S(1)} %add_add_fusion), channel_id=1, source_target_pairs={{0,8},{1,9},{2,10},{3,11},{4,12},{5,13},{6,14},{7,15},{8,0},{9,1},... | collective-permute-start | bytes 73736 | tf_op jit(solution)/shard_map/ppermute | solution.py:423
  75.0 5.1 %collective-permute-start.14 = (f32[48,128]{1,0:T(8,128)S(1)}, f32[48,128]{1,0:T(8,128)S(1)}, u32[]{:S(2)}, u32[]{:S(2)}) collective-permute-start(f32[48,128]{1,0:T(8,128)S(1)} %add_add_fusion), channel_id=1, source_target_pairs={{0,4},{1,5},{2,6},{3,7},{4,0},{5,1},{6,2},{7,3},{8,12},{9,13},{10,... | collective-permute-start | bytes 73736 | tf_op jit(solution)/shard_map/ppermute | solution.py:423

commit v8 on v7

--- a/solution.py
+++ b/solution.py
@@ -162,7 +162,7 @@
 
 
 def main_kernel(
-    dist, cot, mask, cols, edge, from_left, from_right, lines,
+    dist, cot, mask, cols, edge, beside, lines,
     a_in, a_out, b_out, b_in, bias_out,
     out, parts,
     post, gmid, gpad, hid, hpost, hcot, hmid, strip, spost, smid, flip, uo, acc_in, acc_out, accb,
@@ -175,10 +175,10 @@
 
     strip[0] = cols[...]
     strip[1] = edge[...]
-    strip[0, pl.ds(0, 160), :] = from_left[:, :128].astype(f32)
-    strip[1, pl.ds(0, 160), :] = from_left[:, 128:].astype(f32)
-    strip[0, pl.ds(480, 160), :] = from_right[:, :128].astype(f32)
-    strip[1, pl.ds(480, 160), :] = from_right[:, 128:].astype(f32)
+    strip[0, pl.ds(0, 160), :] = beside[:160, :128].astype(f32)
+    strip[1, pl.ds(0, 160), :] = beside[:160, 128:].astype(f32)
+    strip[0, pl.ds(480, 160), :] = beside[160:, :128].astype(f32)
+    strip[1, pl.ds(480, 160), :] = beside[160:, 128:].astype(f32)
 
     def strip_of(i):
         return join(strip[0, pl.ds(i, 8, stride=IDX), :], strip[1, pl.ds(i, 8, stride=IDX), :])
@@ -439,7 +439,9 @@
     from_right = lax.ppermute(side_down, "gy", down)
     weight_in, _ = lax.optimization_barrier((weight_in, edge))
     nets = make_weights(weight_in, weight_out, bias_in, bias_out)
-    grad, parts = main_call(dist, cot, mask, cols, edge, from_left, from_right, lines, *nets)
+    grad, parts = main_call(
+        dist, cot, mask, cols, edge, jnp.concatenate([from_left, from_right]), lines, *nets
+    )
     total = summed(parts)
     cells = mask.size * lax.axis_size("gx") * lax.axis_size("gy")
     total = total * (1.0 / math.sqrt(cells))

time: 82.2 us -> 82.2 us (level)
  no operation moved by 1% of the time
where the time goes in v8:
time: 82.2 us; the launch traced here: 81.7 us
  Pallas kernels  39.9 us (49%)
  starting transfers between devices  27.3 us (33%)
  waiting for transfers between devices  10.1 us (12%)
  other arithmetic  2.1 us (3%)
  local copies, waits for them, and re-layouts  1.63 us (2%)
    pallas_call x1, Pallas kernels, main_call(): pl.pallas_call(main_kernel, out_shape=[jax.ShapeDtypeStruct((Q, 2, 128, 1...  29.7 us
    ppermute x13, starting transfers between devices, summed(): got.append(lax.ppermute(values, ('gx', 'gy'), pairs))  17.7 us
    ppermute x13, waiting for transfers between devices, summed(): got.append(lax.ppermute(values, ('gx', 'gy'), pairs))  10 us
    ppermute x1, starting transfers between devices, shards(): from_right = lax.ppermute(side_down, 'gy', down)  5.46 us
    pallas_call x1, Pallas kernels, pack(): pl.pallas_call(pack_kernel, out_shape=jax.ShapeDtypeStruct((640, 128), f3...  4.01 us
    ppermute x1, starting transfers between devices, shards(): from_down = lax.ppermute(send_down, 'gx', down)  2.56 us
    pallas_call x1, Pallas kernels, make_weights(): pl.pallas_call(weights_kernel, out_shape=[jax.ShapeDtypeStruct((1024, 160...  2.3 us
    pallas_call x1, Pallas kernels, corners(): pl.pallas_call(corner_kernel, out_shape=[jax.ShapeDtypeStruct((160, 256),...  2.08 us
  transfers between devices with their start and end apart: 17, of which 7 were waited for; matrix products, arithmetic and copies ran while one was open for 0% of the time, Pallas kernels for 8%

profile of v8, /device:TPU:0, one launch (start us, length us, event | category | flops | bytes accessed | tf_op | source)
XLA Modules:
  0.0 81.7 jit_solution(16954016197223682498)
XLA Ops:
  0.6 1.9 %shard_map.111 = (bf16[160,128]{1,0:T(8,128)(2,1)}, bf16[160,128]{1,0:T(8,128)(2,1)}) custom-call(f32[38,128,128]{2,1,0:T(8,128)} %bitcast.14, f32[38,128,128]{2,1,0:T(8,128)} %bitcast.15, f32[38,128,128]{2,1,0:T(8,128)} %bitcast.17, f32[38,128,128]{2,1,0:T(8,128)} %bitcast.18, s32[2,128,128]{2,1,0:T(8,128)} %mask.1, s32[2,128,128]{2,1,0:T(8,128)} %mask.1), custom_call_target="tpu_custom_call" | custom-call | tf_op jit(solution)/shard_map/pallas_call | solution.py:95
  2.5 1.6 %collective-permute-start = (bf16[160,128]{1,0:T(8,128)(2,1)}, bf16[160,128]{1,0:T(8,128)(2,1)S(1)}, u32[]{:S(2)}, u32[]{:S(2)}) collective-permute-start(bf16[160,128]{1,0:T(8,128)(2,1)} %get-tuple-element.19), channel_id=1, source_target_pairs={{0,16},{16,32},{32,48},{48,64},{64,80},{80,96},{96,112},{112,0},{1... | collective-permute-start | bytes 122888 | tf_op jit(solution)/shard_map/ppermute | solution.py:433
  4.1 2.6 %collective-permute-start.1 = (bf16[160,128]{1,0:T(8,128)(2,1)}, bf16[160,128]{1,0:T(8,128)(2,1)S(1)}, u32[]{:S(2)}, u32[]{:S(2)}) collective-permute-start(bf16[160,128]{1,0:T(8,128)(2,1)} %get-tuple-element.20), channel_id=1, source_target_pairs={{16,0},{32,16},{48,32},{64,48},{80,64},{96,80},{112,96},{0,112},{1... | collective-permute-start | bytes 122888 | tf_op jit(solution)/shard_map/ppermute | solution.py:434
  6.6 4.0 %shard_map.110.cols = f32[640,128]{1,0:T(8,128)} custom-call(f32[4864,128]{1,0:T(8,128)} %bitcast.16, f32[4864,128]{1,0:T(8,128)} %bitcast.19, s32[256,128]{1,0:T(8,128)} %bitcast.20), custom_call_target="tpu_custom_call" | custom-call | flops 100000000 | bytes 6000000 | tf_op jit(solution)/shard_map/pallas_call | solution.py:127
  10.7 0.6 pad_maximum_fusion.1.received
  11.3 2.1 %shard_map.112 = (bf16[160,256]{1,0:T(8,128)(2,1)}, bf16[160,256]{1,0:T(8,128)(2,1)}, f32[640,128]{1,0:T(8,128)}, f32[640,128]{1,0:T(8,128)}) custom-call(bf16[320,128]{1,0:T(8,128)(2,1)} %pad_maximum_fusion.1.received, f32[640,128]{1,0:T(8,128)} %shard_map.110.cols), custom_call_target="tpu_custom_call" | custom-call | tf_op jit(solution)/shard_map/pallas_call | solution.py:155
  13.4 5.5 %collective-permute-start.3 = (bf16[160,256]{1,0:T(8,128)(2,1)}, bf16[160,256]{1,0:T(8,128)(2,1)S(1)}, u32[]{:S(2)}, u32[]{:S(2)}) collective-permute-start(bf16[160,256]{1,0:T(8,128)(2,1)} %get-tuple-element.23), channel_id=1, source_target_pairs={{1,0},{2,1},{3,2},{4,3},{5,4},{6,5},{7,6},{8,7},{9,8},{10,9},{11,1... | collective-permute-start | bytes 245768 | tf_op jit(solution)/shard_map/ppermute | solution.py:439
  18.8 2.3 %shard_map.113 = (bf16[1024,160]{1,0:T(8,128)(2,1)}, bf16[1024,160]{1,0:T(8,128)(2,1)}, bf16[160,1024]{1,0:T(8,128)(2,1)}, bf16[160,1024]{1,0:T(8,128)(2,1)}, f32[152,128]{1,0:T(8,128)}) custom-call(bf16[19,128]{1,0:T(8,128)(2,1)} %win, bf16[19,128]{1,0:T(8,128)(2,1)} %bitcast.21, f32[1,128]{1,0:T(1,128)} %bitcast.22, f32[1,19]{1,0:T(1,128)} %bitcast.23), custom_call_target="tpu_custom_call" | custom-call | flops 100000000 | bytes 2000000 | tf_op jit(solution)/shard_map/pallas_call | solution.py:65
  21.2 0.7 pad_maximum_fusion.beside
  21.9 29.7 %shard_map.114 = (f32[19,2,128,128]{3,2,1,0:T(8,128)}, f32[48,128]{1,0:T(8,128)}) custom-call(f32[19,2,128,128]{3,2,1,0:T(8,128)} %dist.1, f32[19,2,128,128]{3,2,1,0:T(8,128)} %cot.1, s32[2,128,128]{2,1,0:T(8,128)} %mask.1, f32[640,128]{1,0:T(8,128)} %shard_map.110.cols, f32[640,128]{1,0:T(8,128)} %get-tuple-element.21.edge, ...), custom_call_target="tpu_custom_call" | custom-call | tf_op jit(solution)/shard_map/pallas_call | solution.py:382
  51.6 2.5 %collective-permute-start.10 = (f32[48,128]{1,0:T(8,128)}, f32[48,128]{1,0:T(8,128)S(1)}, u32[]{:S(2)}, u32[]{:S(2)}) collective-permute-start(f32[48,128]{1,0:T(8,128)} %get-tuple-element.32), channel_id=1, source_target_pairs={{0,19},{1,18},{2,17},{3,16},{4,23},{5,22},{6,21},{7,20},{8,27},{9,... | collective-permute-start | bytes 73736 | tf_op jit(solution)/shard_map/ppermute | solution.py:423
  54.0 1.3 %collective-permute-start.9 = (f32[48,128]{1,0:T(8,128)}, f32[48,128]{1,0:T(8,128)S(1)}, u32[]{:S(2)}, u32[]{:S(2)}) collective-permute-start(f32[48,128]{1,0:T(8,128)} %get-tuple-element.32), channel_id=1, source_target_pairs={{0,18},{1,19},{2,16},{3,17},{4,22},{5,23},{6,20},{7,21},{8,26},{9,... | collective-permute-start | bytes 73736 | tf_op jit(solution)/shard_map/ppermute | solution.py:423
  55.4 2.4 %collective-permute-start.7 = (f32[48,128]{1,0:T(8,128)}, f32[48,128]{1,0:T(8,128)S(1)}, u32[]{:S(2)}, u32[]{:S(2)}) collective-permute-start(f32[48,128]{1,0:T(8,128)} %get-tuple-element.32), channel_id=1, source_target_pairs={{0,2},{1,3},{2,0},{3,1},{4,6},{5,7},{6,4},{7,5},{8,10},{9,11},{10,... | collective-permute-start | bytes 73736 | tf_op jit(solution)/shard_map/ppermute | solution.py:423
  57.8 0.1 collective-permute-start.6
  57.9 2.5 %collective-permute-start.5 = (f32[48,128]{1,0:T(8,128)}, f32[48,128]{1,0:T(8,128)S(1)}, u32[]{:S(2)}, u32[]{:S(2)}) collective-permute-start(f32[48,128]{1,0:T(8,128)} %get-tuple-element.32), channel_id=1, source_target_pairs={{0,16},{1,17},{2,18},{3,19},{4,20},{5,21},{6,22},{7,23},{8,24},{9,... | collective-permute-start | bytes 73736 | tf_op jit(solution)/shard_map/ppermute | solution.py:423
  60.4 0.6 collective-permute-done.7
  61.0 0.3 collective-permute-done.6
  61.2 1.4 %collective-permute-done.5 = f32[48,128]{1,0:T(8,128)S(1)} collective-permute-done((f32[48,128]{1,0:T(8,128)}, f32[48,128]{1,0:T(8,128)S(1)}, u32[]{:S(2)}, u32[]{:S(2)}) %collective-permute-start.5) | collective-permute-done | bytes 24608 | tf_op jit(solution)/shard_map/ppermute | solution.py:423
  62.7 0.8 add_add_fusion.1
  63.4 2.2 %collective-permute-start.13 = (f32[48,128]{1,0:T(8,128)S(1)}, f32[48,128]{1,0:T(8,128)S(1)}, u32[]{:S(2)}, u32[]{:S(2)}) collective-permute-start(f32[48,128]{1,0:T(8,128)S(1)} %add_add_fusion.1), channel_id=1, source_target_pairs={{0,96},{1,97},{2,98},{3,99},{4,100},{5,101},{6,102},{7,103},{8,104... | collective-permute-start | bytes 73736 | tf_op jit(solution)/shard_map/ppermute | solution.py:423
  65.6 0.8 collective-permute-start.12
  66.4 1.2 %collective-permute-start.11 = (f32[48,128]{1,0:T(8,128)S(1)}, f32[48,128]{1,0:T(8,128)S(1)}, u32[]{:S(2)}, u32[]{:S(2)}) collective-permute-start(f32[48,128]{1,0:T(8,128)S(1)} %add_add_fusion.1), channel_id=1, source_target_pairs={{0,32},{1,33},{2,34},{3,35},{4,36},{5,37},{6,38},{7,39},{8,40},{9,... | collective-permute-start | bytes 73736 | tf_op jit(solution)/shard_map/ppermute | solution.py:423
  67.6 0.9 %collective-permute-done.13 = f32[48,128]{1,0:T(8,128)S(1)} collective-permute-done((f32[48,128]{1,0:T(8,128)S(1)}, f32[48,128]{1,0:T(8,128)S(1)}, u32[]{:S(2)}, u32[]{:S(2)}) %collective-permute-start.13) | collective-permute-done | bytes 24608 | tf_op jit(solution)/shard_map/ppermute | solution.py:423
  68.5 2.4 %collective-permute-done.12 = f32[48,128]{1,0:T(8,128)S(1)} collective-permute-done((f32[48,128]{1,0:T(8,128)S(1)}, f32[48,128]{1,0:T(8,128)S(1)}, u32[]{:S(2)}, u32[]{:S(2)}) %collective-permute-start.12) | collective-permute-done | bytes 24608 | tf_op jit(solution)/shard_map/ppermute | solution.py:423
  70.9 3.8 %collective-permute-start.16 = (f32[48,128]{1,0:T(8,128)S(1)}, f32[48,128]{1,0:T(8,128)S(1)}, u32[]{:S(2)}, u32[]{:S(2)}) collective-permute-start(f32[48,128]{1,0:T(8,128)S(1)} %add_add_fusion), channel_id=1, source_target_pairs={{0,12},{1,13},{2,14},{3,15},{4,8},{5,9},{6,10},{7,11},{8,4},{9,5},... | collective-permute-start | bytes 73736 | tf_op jit(solution)/shard_map/ppermute | solution.py:423
  74.8 0.3 collective-permute-start.15
  75.0 0.7 collective-permute-start.14
  75.7 0.9 %collective-permute-done.16 = f32[48,128]{1,0:T(8,128)S(1)} collective-permute-done((f32[48,128]{1,0:T(8,128)S(1)}, f32[48,128]{1,0:T(8,128)S(1)}, u32[]{:S(2)}, u32[]{:S(2)}) %collective-permute-start.16) | collective-permute-done | bytes 24608 | tf_op jit(solution)/shard_map/ppermute | solution.py:423
  76.6 3.5 %collective-permute-done.15 = f32[48,128]{1,0:T(8,128)S(1)} collective-permute-done((f32[48,128]{1,0:T(8,128)S(1)}, f32[48,128]{1,0:T(8,128)S(1)}, u32[]{:S(2)}, u32[]{:S(2)}) %collective-permute-start.15) | collective-permute-done | bytes 24608 | tf_op jit(solution)/shard_map/ppermute | solution.py:423
  80.1 0.5 slice_bitcast_fusion.2
  80.6 0.5 slice_bitcast_fusion.1
  81.1 0.6 slice_bitcast_fusion
  (15 shorter events, 0.1 us)
Async XLA Ops:
  2.5 8.1 %collective-permute-start = (bf16[160,128]{1,0:T(8,128)(2,1)}, bf16[160,128]{1,0:T(8,128)(2,1)S(1)}, u32[]{:S(2)}, u32[]{:S(2)}) collective-permute-start(bf16[160,128]{1,0:T(8,128)(2,1)} %get-tuple-element.19), channel_id=1, source_target_pairs={{0,16},{16,32},{32,48},{48,64},{64,80},{80,96},{96,112},{112,0},{1... | collective-permute-start | bytes 122888 | tf_op jit(solution)/shard_map/ppermute | solution.py:433
  4.1 6.6 %collective-permute-start.1 = (bf16[160,128]{1,0:T(8,128)(2,1)}, bf16[160,128]{1,0:T(8,128)(2,1)S(1)}, u32[]{:S(2)}, u32[]{:S(2)}) collective-permute-start(bf16[160,128]{1,0:T(8,128)(2,1)} %get-tuple-element.20), channel_id=1, source_target_pairs={{16,0},{32,16},{48,32},{64,48},{80,64},{96,80},{112,96},{0,112},{1... | collective-permute-start | bytes 122888 | tf_op jit(solution)/shard_map/ppermute | solution.py:434
  13.4 7.8 %collective-permute-start.2 = (bf16[160,256]{1,0:T(8,128)(2,1)}, bf16[160,256]{1,0:T(8,128)(2,1)S(1)}, u32[]{:S(2)}, u32[]{:S(2)}) collective-permute-start(bf16[160,256]{1,0:T(8,128)(2,1)} %get-tuple-element.22), channel_id=1, source_target_pairs={{0,1},{1,2},{2,3},{3,4},{4,5},{5,6},{6,7},{7,8},{8,9},{9,10},{10,1... | collective-permute-start | bytes 245768 | tf_op jit(solution)/shard_map/ppermute | solution.py:438
  13.4 7.8 %collective-permute-start.3 = (bf16[160,256]{1,0:T(8,128)(2,1)}, bf16[160,256]{1,0:T(8,128)(2,1)S(1)}, u32[]{:S(2)}, u32[]{:S(2)}) collective-permute-start(bf16[160,256]{1,0:T(8,128)(2,1)} %get-tuple-element.23), channel_id=1, source_target_pairs={{1,0},{2,1},{3,2},{4,3},{5,4},{6,5},{7,6},{8,7},{9,8},{10,9},{11,1... | collective-permute-start | bytes 245768 | tf_op jit(solution)/shard_map/ppermute | solution.py:439
  51.6 6.3 %collective-permute-start.10 = (f32[48,128]{1,0:T(8,128)}, f32[48,128]{1,0:T(8,128)S(1)}, u32[]{:S(2)}, u32[]{:S(2)}) collective-permute-start(f32[48,128]{1,0:T(8,128)} %get-tuple-element.32), channel_id=1, source_target_pairs={{0,19},{1,18},{2,17},{3,16},{4,23},{5,22},{6,21},{7,20},{8,27},{9,... | collective-permute-start | bytes 73736 | tf_op jit(solution)/shard_map/ppermute | solution.py:423
  54.0 6.3 %collective-permute-start.9 = (f32[48,128]{1,0:T(8,128)}, f32[48,128]{1,0:T(8,128)S(1)}, u32[]{:S(2)}, u32[]{:S(2)}) collective-permute-start(f32[48,128]{1,0:T(8,128)} %get-tuple-element.32), channel_id=1, source_target_pairs={{0,18},{1,19},{2,16},{3,17},{4,22},{5,23},{6,20},{7,21},{8,26},{9,... | collective-permute-start | bytes 73736 | tf_op jit(solution)/shard_map/ppermute | solution.py:423
  55.4 5.0 %collective-permute-start.8 = (f32[48,128]{1,0:T(8,128)}, f32[48,128]{1,0:T(8,128)S(1)}, u32[]{:S(2)}, u32[]{:S(2)}) collective-permute-start(f32[48,128]{1,0:T(8,128)} %get-tuple-element.32), channel_id=1, source_target_pairs={{0,3},{1,2},{2,1},{3,0},{4,7},{5,6},{6,5},{7,4},{8,11},{9,10},{10,... | collective-permute-start | bytes 73736 | tf_op jit(solution)/shard_map/ppermute | solution.py:423
  55.4 5.6 %collective-permute-start.7 = (f32[48,128]{1,0:T(8,128)}, f32[48,128]{1,0:T(8,128)S(1)}, u32[]{:S(2)}, u32[]{:S(2)}) collective-permute-start(f32[48,128]{1,0:T(8,128)} %get-tuple-element.32), channel_id=1, source_target_pairs={{0,2},{1,3},{2,0},{3,1},{4,6},{5,7},{6,4},{7,5},{8,10},{9,11},{10,... | collective-permute-start | bytes 73736 | tf_op jit(solution)/shard_map/ppermute | solution.py:423
  57.8 3.5 %collective-permute-start.6 = (f32[48,128]{1,0:T(8,128)}, f32[48,128]{1,0:T(8,128)S(1)}, u32[]{:S(2)}, u32[]{:S(2)}) collective-permute-start(f32[48,128]{1,0:T(8,128)} %get-tuple-element.32), channel_id=1, source_target_pairs={{0,17},{1,16},{2,19},{3,18},{4,21},{5,20},{6,23},{7,22},{8,25},{9,... | collective-permute-start | bytes 73736 | tf_op jit(solution)/shard_map/ppermute | solution.py:423
  57.9 4.8 %collective-permute-start.5 = (f32[48,128]{1,0:T(8,128)}, f32[48,128]{1,0:T(8,128)S(1)}, u32[]{:S(2)}, u32[]{:S(2)}) collective-permute-start(f32[48,128]{1,0:T(8,128)} %get-tuple-element.32), channel_id=1, source_target_pairs={{0,16},{1,17},{2,18},{3,19},{4,20},{5,21},{6,22},{7,23},{8,24},{9,... | collective-permute-start | bytes 73736 | tf_op jit(solution)/shard_map/ppermute | solution.py:423
  60.4 2.3 %collective-permute-start.4 = (f32[48,128]{1,0:T(8,128)}, f32[48,128]{1,0:T(8,128)S(1)}, u32[]{:S(2)}, u32[]{:S(2)}) collective-permute-start(f32[48,128]{1,0:T(8,128)} %get-tuple-element.32), channel_id=1, source_target_pairs={{0,1},{1,0},{2,3},{3,2},{4,5},{5,4},{6,7},{7,6},{8,9},{9,8},{10,11... | collective-permute-start | bytes 73736 | tf_op jit(solution)/shard_map/ppermute | solution.py:423
  63.4 5.1 %collective-permute-start.13 = (f32[48,128]{1,0:T(8,128)S(1)}, f32[48,128]{1,0:T(8,128)S(1)}, u32[]{:S(2)}, u32[]{:S(2)}) collective-permute-start(f32[48,128]{1,0:T(8,128)S(1)} %add_add_fusion.1), channel_id=1, source_target_pairs={{0,96},{1,97},{2,98},{3,99},{4,100},{5,101},{6,102},{7,103},{8,104... | collective-permute-start | bytes 73736 | tf_op jit(solution)/shard_map/ppermute | solution.py:423
  65.6 5.3 %collective-permute-start.12 = (f32[48,128]{1,0:T(8,128)S(1)}, f32[48,128]{1,0:T(8,128)S(1)}, u32[]{:S(2)}, u32[]{:S(2)}) collective-permute-start(f32[48,128]{1,0:T(8,128)S(1)} %add_add_fusion.1), channel_id=1, source_target_pairs={{0,64},{1,65},{2,66},{3,67},{4,68},{5,69},{6,70},{7,71},{8,72},{9,... | collective-permute-start | bytes 73736 | tf_op jit(solution)/shard_map/ppermute | solution.py:423
  66.4 4.6 %collective-permute-start.11 = (f32[48,128]{1,0:T(8,128)S(1)}, f32[48,128]{1,0:T(8,128)S(1)}, u32[]{:S(2)}, u32[]{:S(2)}) collective-permute-start(f32[48,128]{1,0:T(8,128)S(1)} %add_add_fusion.1), channel_id=1, source_target_pairs={{0,32},{1,33},{2,34},{3,35},{4,36},{5,37},{6,38},{7,39},{8,40},{9,... | collective-permute-start | bytes 73736 | tf_op jit(solution)/shard_map/ppermute | solution.py:423
  70.9 5.6 %collective-permute-start.16 = (f32[48,128]{1,0:T(8,128)S(1)}, f32[48,128]{1,0:T(8,128)S(1)}, u32[]{:S(2)}, u32[]{:S(2)}) collective-permute-start(f32[48,128]{1,0:T(8,128)S(1)} %add_add_fusion), channel_id=1, source_target_pairs={{0,12},{1,13},{2,14},{3,15},{4,8},{5,9},{6,10},{7,11},{8,4},{9,5},... | collective-permute-start | bytes 73736 | tf_op jit(solution)/shard_map/ppermute | solution.py:423
  74.8 5.3 %collective-permute-start.15 = (f32[48,128]{1,0:T(8,128)S(1)}, f32[48,128]{1,0:T(8,128)S(1)}, u32[]{:S(2)}, u32[]{:S(2)}) collective-permute-start(f32[48,128]{1,0:T(8,128)S(1)} %add_add_fusion), channel_id=1, source_target_pairs={{0,8},{1,9},{2,10},{3,11},{4,12},{5,13},{6,14},{7,15},{8,0},{9,1},... | collective-permute-start | bytes 73736 | tf_op jit(solution)/shard_map/ppermute | solution.py:423
  75.0 5.1 %collective-permute-start.14 = (f32[48,128]{1,0:T(8,128)S(1)}, f32[48,128]{1,0:T(8,128)S(1)}, u32[]{:S(2)}, u32[]{:S(2)}) collective-permute-start(f32[48,128]{1,0:T(8,128)S(1)} %add_add_fusion), channel_id=1, source_target_pairs={{0,4},{1,5},{2,6},{3,7},{4,0},{5,1},{6,2},{7,3},{8,12},{9,13},{10,... | collective-permute-start | bytes 73736 | tf_op jit(solution)/shard_map/ppermute | solution.py:423
